TPU v7x, 256 devices: a whole 4x4x8 slice. The times are simulated.
256 devices in a mesh: grp: 8 (over z_lo, y), seq: 32 (over x, z_hi, core).
Axes of the slice: x: 4, y: 4, z: 8 (z_hi: 4, z_lo: 2; z = z_hi * 2 + z_lo), core: 2. Of those that a mesh axis runs over, the one named last changes fastest.
Arguments:
- queries: bfloat16 [32768, 1024], P(('grp', 'seq'))
- keys: bfloat16 [32768, 1024], P(('grp', 'seq'))
- values: bfloat16 [32768, 1024], P(('grp', 'seq')), may hold values from -6 to 6
- cotangent: bfloat16 [32768, 1024], P(('grp', 'seq')), may hold values from -6 to 6
- head_offsets: int32 [4, 8], replicated, may hold values from 0 to 7, as said below
- level_bias: float32 [4, 8], replicated, may hold values from -1.5 to 1.5
Outputs:
- attended: bfloat16 [32768, 1024], P(('grp', 'seq'))
- query_grad: bfloat16 [32768, 1024], P(('grp', 'seq'))
- key_grad: bfloat16 [32768, 1024], P(('grp', 'seq'))
- value_grad: bfloat16 [32768, 1024], P(('grp', 'seq'))
- bias_grad: float32 [4, 8], replicated
Inputs may be any that keep to these rules, and one draw needn't show every extreme that they name: head_offsets[l, h] lies in 0 to 2**l - 1.
All inputs are finite; a program needn't handle non-finite values.
Results may differ from a plain program's by a relative error of at most 0.025.
Values may be sent and summed in bfloat16 or wider, within the bound.
No kernel may reach another device: no remote copies, remote signals or barrier semaphores. Data moves between devices by JAX's collectives and lax.ppermute only.
A program may use at most 128 MiB of HBM per device.

v0:
```python
import jax
import jax.numpy as jnp
from jax import lax
from jax.sharding import PartitionSpec as P

H = 8
HD = 128
KEEP = 256
LEVELS = 4


def partner(x, axis, stride):
    return lax.ppermute(x, axis, [(i, i ^ 1 << stride) for i in range(lax.axis_size(axis))])


def pick(x, r, offsets):
    onehot = (jnp.arange(r)[:, None] == offsets[None, :]).astype(x.dtype)
    shaped = x.reshape((x.shape[0] // r, r) + x.shape[1:])
    weight = onehot.reshape((1, r, onehot.shape[1]) + (1,) * (x.ndim - 2))
    return jnp.sum(shaped * weight, axis=1)


def spread(x, r, offsets):
    onehot = (jnp.arange(r)[:, None] == offsets[None, :]).astype(x.dtype)
    weight = onehot.reshape((1, r, onehot.shape[1]) + (1,) * (x.ndim - 2))
    placed = x[:, None] * weight
    return placed.reshape((x.shape[0] * r,) + x.shape[1:])


def join(mine, theirs, upper):
    lower_part = jnp.where(upper, theirs, mine)
    upper_part = jnp.where(upper, mine, theirs)
    return jnp.concatenate([lower_part, upper_part], axis=1)


def gather_pairs(block, count, index):
    for bit in range(count):
        other = partner(block, "seq", bit)
        block = join(block, other, index >> bit & 1 == 1)
    return block


def return_pairs(block, count, index):
    for bit in reversed(range(count)):
        half = block.shape[1] // 2
        lower_part = block[:, :half]
        upper_part = block[:, half:]
        upper = index >> bit & 1 == 1
        outgoing = jnp.where(upper, lower_part, upper_part)
        staying = jnp.where(upper, upper_part, lower_part)
        block = staying + partner(outgoing.astype(jnp.bfloat16), "seq", bit).astype(outgoing.dtype)
    return block


def local(queries, keys, values, cotangent, head_offsets, level_bias):
    rows_all = queries.shape[0]
    scale = HD ** (-0.5)
    q3 = queries.reshape(rows_all, H, HD)
    k3 = keys.reshape(rows_all, H, HD)
    v3 = values.reshape(rows_all, H, HD)
    d3 = cotangent.reshape(rows_all, H, HD).astype(jnp.float32)
    index = lax.axis_index("seq")
    blocks = []
    counts = []
    picked = []
    for level in range(LEVELS):
        r = 2**level
        offs = head_offsets[level]
        picked.append((pick(q3, r, offs), pick(k3, r, offs), pick(v3, r, offs)))
        blocks.append(jnp.stack([picked[level][1], picked[level][2]]))
        counts.append((KEEP * r // rows_all).bit_length() - 1)
    gathered = [gather_pairs(blocks[level], counts[level], index) for level in range(LEVELS)]
    saved = []
    placed_out = []
    logits = []
    for level in range(LEVELS):
        r = 2**level
        offs = head_offsets[level]
        qs = picked[level][0]
        s = (
            jnp.einsum("qhd,khd->hqk", qs, gathered[level][0], preferred_element_type=jnp.float32)
            * scale
        )
        lse = jax.nn.logsumexp(s, axis=-1)
        p = jnp.exp(s - lse[..., None])
        pb = p.astype(jnp.bfloat16)
        o = jnp.einsum("hqk,khd->qhd", pb, gathered[level][1], preferred_element_type=jnp.float32)
        saved.append((lse, p, pb, o))
        placed_out.append(spread(o, r, offs))
        kept = spread(jnp.ones((rows_all // r, H), jnp.float32), r, offs)
        logits.append(
            jnp.where(kept > 0, spread(lse.T, r, offs) + level_bias[level][None, :], -jnp.inf)
        )
    mix = jax.nn.softmax(jnp.stack(logits), axis=0)
    out = jnp.zeros((rows_all, H, HD), jnp.float32)
    for level in range(LEVELS):
        out = out + mix[level][..., None] * placed_out[level]
    attended = out.astype(jnp.bfloat16)
    dq_sum = jnp.zeros((rows_all, H, HD), jnp.float32)
    dk_sum = jnp.zeros((rows_all, H, HD), jnp.float32)
    dv_sum = jnp.zeros((rows_all, H, HD), jnp.float32)
    bias_rows = []
    for level in range(LEVELS):
        r = 2**level
        offs = head_offsets[level]
        qs, ks, vs = picked[level]
        lse, p, pb, o = saved[level]
        g_rows = mix[level] * jnp.sum(d3 * (placed_out[level] - out), axis=-1)
        bias_rows.append(jnp.sum(g_rows, axis=0))
        dob = pick(mix[level][..., None] * d3, r, offs).astype(jnp.bfloat16)
        c_rows = jnp.sum(dob.astype(jnp.float32) * o, axis=-1) - pick(g_rows, r, offs)
        dp = jnp.einsum("qhd,khd->hqk", dob, gathered[level][1], preferred_element_type=jnp.float32)
        dsb = (p * (dp - c_rows.T[..., None])).astype(jnp.bfloat16)
        dq = (
            jnp.einsum("hqk,khd->qhd", dsb, gathered[level][0], preferred_element_type=jnp.float32)
            * scale
        )
        dk_part = jnp.einsum("hqk,qhd->khd", dsb, qs, preferred_element_type=jnp.float32) * scale
        dv_part = jnp.einsum("hqk,qhd->khd", pb, dob, preferred_element_type=jnp.float32)
        returned = return_pairs(jnp.stack([dk_part, dv_part]), counts[level], index)
        dk = returned[0]
        dv = returned[1]
        dq_sum = dq_sum + spread(dq, r, offs)
        dk_sum = dk_sum + spread(dk, r, offs)
        dv_sum = dv_sum + spread(dv, r, offs)
    bias_grad = lax.psum(jnp.stack(bias_rows), ("grp", "seq"))
    shape2 = (rows_all, H * HD)
    return (
        attended.reshape(shape2),
        dq_sum.astype(jnp.bfloat16).reshape(shape2),
        dk_sum.astype(jnp.bfloat16).reshape(shape2),
        dv_sum.astype(jnp.bfloat16).reshape(shape2),
        bias_grad,
    )


def solution(mesh):
    return jax.shard_map(
        local,
        mesh=mesh,
        in_specs=(
            P(("grp", "seq"), None),
            P(("grp", "seq"), None),
            P(("grp", "seq"), None),
            P(("grp", "seq"), None),
            P(),
            P(),
        ),
        out_specs=(
            P(("grp", "seq"), None),
            P(("grp", "seq"), None),
            P(("grp", "seq"), None),
            P(("grp", "seq"), None),
            P(),
        ),
        check_vma=False,
    )
```

profile of v0, /device:TPU:1, one launch (start us, length us, event | category | flops | bytes accessed | tf_op | source)
XLA Modules:
  0.0 358.8 jit_solution(3274667638761875966)
XLA Ops:
  5.2 3.3 collective-permute-start.3
  24.7 12.0 %collective-permute-done.7 = bf16[2,32,8,128]{3,1,2,0:T(8,128)(2,1)S(1)} collective-permute-done((bf16[2,32,8,128]{3,1,2,0:T(8,128)(2,1)S(1)}, bf16[2,32,8,128]{3,1,2,0:T(8,128)(2,1)S(1)}, u32[]{:S(2)}, u32[]{:S(2)}) %collective-permute-start.7) | collective-permute-done | bytes 131104 | tf_op jit(solution)/shard_map/ppermute | solution.py:13
  36.8 5.1 %collective-permute-start.8 = (bf16[2,64,8,128]{3,1,2,0:T(8,128)(2,1)S(1)}, bf16[2,64,8,128]{3,1,2,0:T(8,128)(2,1)S(1)}, u32[]{:S(2)}, u32[]{:S(2)}) collective-permute-start(bf16[2,64,8,128]{3,1,2,0:T(8,128)(2,1)S(1)} %pad_maximum_fusion.14), channel_id=1, source_target_pairs={{0,4},{1,5},{2,6},{3,7},{4,0},{5,1},{6,2},{7,3},{8,12},{9,13},{10,... | collective-permute-start | bytes 786440 | tf_op jit(solution)/shard_map/ppermute | solution.py:13
  44.0 26.8 %collective-permute-start.5 = (bf16[2,128,8,128]{3,1,2,0:T(8,128)(2,1)}, bf16[2,128,8,128]{3,1,2,0:T(8,128)(2,1)}, u32[]{:S(2)}, u32[]{:S(2)}) collective-permute-start(bf16[2,128,8,128]{3,1,2,0:T(8,128)(2,1)} %pad_maximum_fusion.10), channel_id=1, source_target_pairs={{0,4},{1,5},{2,6},{3,7},{4,0},{5,1},{6,2},{7,3},{8,12},{9,13},{10,... | collective-permute-start | bytes 1572872 | tf_op jit(solution)/shard_map/ppermute | solution.py:13
  75.6 14.2 %collective-permute-done.2 = bf16[2,128,8,128]{3,1,2,0:T(8,128)(2,1)S(1)} collective-permute-done((bf16[2,128,8,128]{3,1,2,0:T(8,128)(2,1)S(1)}, bf16[2,128,8,128]{3,1,2,0:T(8,128)(2,1)S(1)}, u32[]{:S(2)}, u32[]{:S(2)}) %collective-permute-start.2) | collective-permute-done | bytes 524320 | tf_op jit(solution)/shard_map/ppermute | solution.py:13
  93.2 1.5 copy.331
  96.0 1.5 copy.327
  98.8 2.4 broadcast_select_fusion.3
  101.2 1.4 fusion.124
  104.8 1.4 broadcast_select_fusion.1
  108.9 1.6 copy.421
  111.2 1.5 fusion.72
  113.6 1.5 copy.329
  115.1 1.4 mul.844
  116.5 1.5 mul.852
  120.9 1.4 copy.361
  123.6 2.0 multiply_reduce_fusion.18
  126.5 2.0 copy.349
  128.6 1.4 mul.940
  132.0 2.0 multiply_reduce_fusion.20
  135.5 2.0 copy.350
  137.5 1.4 copy.354
  140.3 1.7 multiply_reduce_fusion.8
  142.9 2.0 copy.348
  145.0 2.8 multiply_add_fusion
  147.9 1.9 multiply_reduce_fusion.4
  149.8 1.4 reduce_sum.370
  156.4 1.4 copy.363
  157.8 1.5 multiply_reduce_fusion.21
  162.7 1.9 fusion.11
  166.0 1.5 convolution_bitcast_fusion.2
  173.8 1.5 convolution_bitcast_fusion
  177.0 1.5 convolution_bitcast_fusion.1
  178.5 80.4 %psum.7 = f32[4,8]{1,0:T(4,128)} all-reduce(f32[4,8]{1,0:T(4,128)S(1)} %pad_maximum_fusion.18), channel_id=1, replica_groups=mesh['grp'=8,'seq'=32] {'grp','seq'}, use_global_device_ids=true, to_apply=%region_36.37 | all-reduce | flops 32 | bytes 256 | tf_op jit(solution)/shard_map/psum | solution.py:126
  261.3 1.4 fusion.3
  268.7 2.1 collective-permute-start.13
  272.6 2.0 copy.343
  274.6 1.9 copy.500
  276.5 2.0 copy.345
  278.6 1.9 copy.502
  280.5 2.1 copy.340
  284.0 2.3 fusion.44
  291.4 2.1 copy.375
  294.5 3.3 collective-permute-start.17
  299.3 2.4 collective-permute-start.14
  301.7 34.0 %collective-permute-done.11 = bf16[2,128,8,128]{3,1,2,0:T(8,128)(2,1)} collective-permute-done((bf16[2,128,8,128]{3,1,2,0:T(8,128)(2,1)}, bf16[2,128,8,128]{3,1,2,0:T(8,128)(2,1)}, u32[]{:S(2)}, u32[]{:S(2)}) %collective-permute-start.11) | collective-permute-done | bytes 524320 | tf_op jit(solution)/shard_map/ppermute | solution.py:13
  338.0 6.0 %collective-permute-done.14 = bf16[2,64,8,128]{3,1,2,0:T(8,128)(2,1)S(1)} collective-permute-done((bf16[2,64,8,128]{3,1,2,0:T(8,128)(2,1)S(1)}, bf16[2,64,8,128]{3,1,2,0:T(8,128)(2,1)S(1)}, u32[]{:S(2)}, u32[]{:S(2)}) %collective-permute-start.14) | collective-permute-done | bytes 262176 | tf_op jit(solution)/shard_map/ppermute | solution.py:13
  353.7 2.5 fusion.32
  (427 shorter events, 101.5 us)
Async XLA Ops:
  0.6 3.4 copy-start.28
  2.0 15.2 %copy-start.79 = (f32[4,8]{1,0:T(4,128)}, f32[4,8]{1,0:T(4,128)S(1)}, u32[]{:S(2)}) copy-start(f32[4,8]{1,0:T(4,128)S(1)} %get-tuple-element.101) | copy-start | bytes 388
  4.0 4.5 %copy-start.27 = (bf16[128,1024]{1,0:T(8,128)(2,1)S(1)}, bf16[128,1024]{1,0:T(8,128)(2,1)}, u32[]{:S(2)}) copy-start(bf16[128,1024]{1,0:T(8,128)(2,1)} %param.7) | copy-start | bytes 786436
  4.0 4.5 %copy-start.29 = (bf16[128,1024]{1,0:T(8,128)(2,1)S(1)}, bf16[128,1024]{1,0:T(8,128)(2,1)}, u32[]{:S(2)}) copy-start(bf16[128,1024]{1,0:T(8,128)(2,1)} %param.6) | copy-start | bytes 786436
  5.2 18.3 %collective-permute-start.3 = (bf16[2,32,8,128]{3,1,2,0:T(8,128)(2,1)S(1)}, bf16[2,32,8,128]{3,1,2,0:T(8,128)(2,1)S(1)}, u32[]{:S(2)}, u32[]{:S(2)}) collective-permute-start(bf16[2,32,8,128]{3,1,2,0:T(8,128)(2,1)S(1)} %pad_maximum_fusion.15), channel_id=1, source_target_pairs={{0,1},{1,0},{2,3},{3,2},{4,5},{5,4},{6,7},{7,6},{8,9},{9,8},{10,11... | collective-permute-start | bytes 393224 | tf_op jit(solution)/shard_map/ppermute | solution.py:13
  8.6 99.7 %copy-start.71 = (f32[8,8]{0,1:T(8,128)}, f32[8,8]{0,1:T(8,128)S(1)}, u32[]{:S(2)}) copy-start(f32[8,8]{0,1:T(8,128)S(1)} %get-tuple-element.104) | copy-start | bytes 772
  9.9 12.2 %collective-permute-start.6 = (bf16[2,16,8,128]{3,1,2,0:T(8,128)(2,1)S(1)}, bf16[2,16,8,128]{3,1,2,0:T(8,128)(2,1)S(1)}, u32[]{:S(2)}, u32[]{:S(2)}) collective-permute-start(bf16[2,16,8,128]{3,1,2,0:T(8,128)(2,1)S(1)} %pad_maximum_fusion.17), channel_id=1, source_target_pairs={{0,1},{1,0},{2,3},{3,2},{4,5},{5,4},{6,7},{7,6},{8,9},{9,8},{10,11... | collective-permute-start | bytes 196616 | tf_op jit(solution)/shard_map/ppermute | solution.py:13
  10.0 7.2 %copy-start.91 = (f32[2,8]{1,0:T(2,128)}, f32[2,8]{1,0:T(2,128)S(1)}, u32[]{:S(2)}) copy-start(f32[2,8]{1,0:T(2,128)S(1)} %get-tuple-element.98) | copy-start | bytes 196
  10.5 79.6 %copy-start.48 = (bf16[64,8,128]{2,1,0:T(8,128)(2,1)}, bf16[64,8,128]{2,1,0:T(8,128)(2,1)S(1)}, u32[]{:S(2)}) copy-start(bf16[64,8,128]{2,1,0:T(8,128)(2,1)S(1)} %get-tuple-element.40) | copy-start | bytes 393220
  10.6 31.3 %collective-permute-start.1 = (bf16[2,64,8,128]{3,1,2,0:T(8,128)(2,1)S(1)}, bf16[2,64,8,128]{3,1,2,0:T(8,128)(2,1)}, u32[]{:S(2)}, u32[]{:S(2)}) collective-permute-start(bf16[2,64,8,128]{3,1,2,0:T(8,128)(2,1)S(1)} %pad_maximum_fusion.12), channel_id=1, source_target_pairs={{0,1},{1,0},{2,3},{3,2},{4,5},{5,4},{6,7},{7,6},{8,9},{9,8},{10,11... | collective-permute-start | bytes 786440 | tf_op jit(solution)/shard_map/ppermute | solution.py:13
  12.9 60.3 %collective-permute-start = (bf16[2,128,8,128]{3,1,2,0:T(8,128)(2,1)}, bf16[2,128,8,128]{3,1,2,0:T(8,128)(2,1)}, u32[]{:S(2)}, u32[]{:S(2)}) collective-permute-start(bf16[2,128,8,128]{3,1,2,0:T(8,128)(2,1)} %pad_maximum_fusion.8), channel_id=1, source_target_pairs={{0,1},{1,0},{2,3},{3,2},{4,5},{5,4},{6,7},{7,6},{8,9},{9,8},{10,11... | collective-permute-start | bytes 1572872 | tf_op jit(solution)/shard_map/ppermute | solution.py:13
  15.5 58.9 %copy-start.34 = (bf16[128,1024]{0,1:T(8,128)(2,1)}, bf16[128,1024]{0,1:T(8,128)(2,1)S(1)}, u32[]{:S(2)}) copy-start(bf16[128,1024]{0,1:T(8,128)(2,1)S(1)} %copy.419) | copy-start | bytes 786436
  17.2 100.9 %copy-start.59 = (f32[128,8]{0,1:T(8,128)}, f32[128,8]{0,1:T(8,128)S(1)}, u32[]{:S(2)}) copy-start(f32[128,8]{0,1:T(8,128)S(1)} %reshape.787) | copy-start | bytes 12292
  17.2 100.8 %copy-start.62 = (f32[128,8]{0,1:T(8,128)}, f32[128,8]{0,1:T(8,128)S(1)}, u32[]{:S(2)}) copy-start(f32[128,8]{0,1:T(8,128)S(1)} %copy.333) | copy-start | bytes 12292
  17.3 100.7 %copy-start.65 = (f32[128,8]{0,1:T(8,128)}, f32[128,8]{0,1:T(8,128)S(1)}, u32[]{:S(2)}) copy-start(f32[128,8]{0,1:T(8,128)S(1)} %copy.330) | copy-start | bytes 12292
  22.1 14.6 %collective-permute-start.7 = (bf16[2,32,8,128]{3,1,2,0:T(8,128)(2,1)S(1)}, bf16[2,32,8,128]{3,1,2,0:T(8,128)(2,1)S(1)}, u32[]{:S(2)}, u32[]{:S(2)}) collective-permute-start(bf16[2,32,8,128]{3,1,2,0:T(8,128)(2,1)S(1)} %pad_maximum_fusion.16), channel_id=1, source_target_pairs={{0,2},{1,3},{2,0},{3,1},{4,6},{5,7},{6,4},{7,5},{8,10},{9,11},{10,... | collective-permute-start | bytes 393224 | tf_op jit(solution)/shard_map/ppermute | solution.py:13
  23.5 19.5 %collective-permute-start.4 = (bf16[2,64,8,128]{3,1,2,0:T(8,128)(2,1)S(1)}, bf16[2,64,8,128]{3,1,2,0:T(8,128)(2,1)S(1)}, u32[]{:S(2)}, u32[]{:S(2)}) collective-permute-start(bf16[2,64,8,128]{3,1,2,0:T(8,128)(2,1)S(1)} %pad_maximum_fusion.13), channel_id=1, source_target_pairs={{0,2},{1,3},{2,0},{3,1},{4,6},{5,7},{6,4},{7,5},{8,10},{9,11},{10,... | collective-permute-start | bytes 786440 | tf_op jit(solution)/shard_map/ppermute | solution.py:13
  36.8 34.1 %collective-permute-start.8 = (bf16[2,64,8,128]{3,1,2,0:T(8,128)(2,1)S(1)}, bf16[2,64,8,128]{3,1,2,0:T(8,128)(2,1)S(1)}, u32[]{:S(2)}, u32[]{:S(2)}) collective-permute-start(bf16[2,64,8,128]{3,1,2,0:T(8,128)(2,1)S(1)} %pad_maximum_fusion.14), channel_id=1, source_target_pairs={{0,4},{1,5},{2,6},{3,7},{4,0},{5,1},{6,2},{7,3},{8,12},{9,13},{10,... | collective-permute-start | bytes 786440 | tf_op jit(solution)/shard_map/ppermute | solution.py:13
  42.9 46.8 %collective-permute-start.2 = (bf16[2,128,8,128]{3,1,2,0:T(8,128)(2,1)S(1)}, bf16[2,128,8,128]{3,1,2,0:T(8,128)(2,1)S(1)}, u32[]{:S(2)}, u32[]{:S(2)}) collective-permute-start(bf16[2,128,8,128]{3,1,2,0:T(8,128)(2,1)S(1)} %pad_maximum_fusion.9), channel_id=1, source_target_pairs={{0,2},{1,3},{2,0},{3,1},{4,6},{5,7},{6,4},{7,5},{8,10},{9,11},{10,... | collective-permute-start | bytes 1572872 | tf_op jit(solution)/shard_map/ppermute | solution.py:13
  43.2 27.7 %copy-start.33 = (bf16[2,64,8,128]{3,1,2,0:T(8,128)(2,1)}, bf16[2,64,8,128]{3,1,2,0:T(8,128)(2,1)S(1)}, u32[]{:S(2)}) copy-start(bf16[2,64,8,128]{3,1,2,0:T(8,128)(2,1)S(1)} %get-tuple-element.61) | copy-start | bytes 786436
  44.0 54.8 %collective-permute-start.5 = (bf16[2,128,8,128]{3,1,2,0:T(8,128)(2,1)}, bf16[2,128,8,128]{3,1,2,0:T(8,128)(2,1)}, u32[]{:S(2)}, u32[]{:S(2)}) collective-permute-start(bf16[2,128,8,128]{3,1,2,0:T(8,128)(2,1)} %pad_maximum_fusion.10), channel_id=1, source_target_pairs={{0,4},{1,5},{2,6},{3,7},{4,0},{5,1},{6,2},{7,3},{8,12},{9,13},{10,... | collective-permute-start | bytes 1572872 | tf_op jit(solution)/shard_map/ppermute | solution.py:13
  71.1 3.3 copy-start.31
  72.0 32.8 %collective-permute-start.9 = (bf16[2,128,8,128]{3,1,2,0:T(8,128)(2,1)}, bf16[2,128,8,128]{3,1,2,0:T(8,128)(2,1)}, u32[]{:S(2)}, u32[]{:S(2)}) collective-permute-start(bf16[2,128,8,128]{3,1,2,0:T(8,128)(2,1)} %pad_maximum_fusion.11), channel_id=1, source_target_pairs={{0,8},{1,9},{2,10},{3,11},{4,12},{5,13},{6,14},{7,15},{8,0},{9,1},... | collective-permute-start | bytes 1572872 | tf_op jit(solution)/shard_map/ppermute | solution.py:13
  113.6 5.3 %copy-start.86 = (f32[1,128,8]{1,2,0:T(8,128)}, f32[1,128,8]{1,2,0:T(8,128)S(1)}, u32[]{:S(2)}) copy-start(f32[1,128,8]{1,2,0:T(8,128)S(1)} %copy.328) | copy-start | bytes 12292
  132.0 3.4 copy-start.54
  151.2 3.1 copy-start.20
  151.2 3.1 copy-start.22
  162.7 3.3 copy-start.51
  162.7 3.3 copy-start.74
  173.7 3.2 copy-start.55
  173.7 3.2 copy-start.73
  175.3 83.7 %copy-start.70 = (f32[32,8,128]{2,0,1:T(8,128)S(1)}, f32[32,8,128]{2,0,1:T(8,128)}, u32[]{:S(2)}) copy-start(f32[32,8,128]{2,0,1:T(8,128)} %fusion.11) | copy-start | bytes 393220
  175.3 83.8 %copy-start.30 = (bf16[128,8,128]{0,2,1:T(8,128)(2,1)S(1)}, bf16[128,8,128]{0,2,1:T(8,128)(2,1)}, u32[]{:S(2)}) copy-start(bf16[128,8,128]{0,2,1:T(8,128)(2,1)} %get-tuple-element.43) | copy-start | bytes 786436
  260.1 4.8 %copy-start.9 = (f32[1,256,8,128]{3,1,2,0:T(8,128)}, f32[1,256,8,128]{3,1,2,0:T(8,128)S(1)}, u32[]{:S(2)}) copy-start(f32[1,256,8,128]{3,1,2,0:T(8,128)S(1)} %convolution_bitcast_fusion.3) | copy-start | bytes 3145732
  265.9 20.4 %collective-permute-start.10 = (bf16[2,128,8,128]{3,1,2,0:T(8,128)(2,1)}, bf16[2,128,8,128]{3,1,2,0:T(8,128)(2,1)}, u32[]{:S(2)}, u32[]{:S(2)}) collective-permute-start(bf16[2,128,8,128]{3,1,2,0:T(8,128)(2,1)} %select_convert_fusion.3), channel_id=1, source_target_pairs={{0,1},{1,0},{2,3},{3,2},{4,5},{5,4},{6,7},{7,6},{8,9},{9,8},{10,11... | collective-permute-start | bytes 1572872 | tf_op jit(solution)/shard_map/ppermute | solution.py:13
  267.7 3.0 copy-start.3
  267.7 3.0 copy-start.5
  267.7 20.9 %collective-permute-start.16 = (bf16[2,128,8,128]{3,1,2,0:T(8,128)(2,1)}, bf16[2,128,8,128]{3,1,2,0:T(8,128)(2,1)}, u32[]{:S(2)}, u32[]{:S(2)}) collective-permute-start(bf16[2,128,8,128]{3,1,2,0:T(8,128)(2,1)} %select_convert_fusion), channel_id=1, source_target_pairs={{0,8},{1,9},{2,10},{3,11},{4,12},{5,13},{6,14},{7,15},{8,0},{9,1},... | collective-permute-start | bytes 1572872 | tf_op jit(solution)/shard_map/ppermute | solution.py:13
  268.7 29.1 %collective-permute-start.13 = (bf16[2,128,8,128]{3,1,2,0:T(8,128)(2,1)}, bf16[2,128,8,128]{3,1,2,0:T(8,128)(2,1)}, u32[]{:S(2)}, u32[]{:S(2)}) collective-permute-start(bf16[2,128,8,128]{3,1,2,0:T(8,128)(2,1)} %select_convert_fusion.1), channel_id=1, source_target_pairs={{0,4},{1,5},{2,6},{3,7},{4,0},{5,1},{6,2},{7,3},{8,12},{9,13},{10,... | collective-permute-start | bytes 1572872 | tf_op jit(solution)/shard_map/ppermute | solution.py:13
  271.7 64.0 %collective-permute-start.11 = (bf16[2,128,8,128]{3,1,2,0:T(8,128)(2,1)}, bf16[2,128,8,128]{3,1,2,0:T(8,128)(2,1)}, u32[]{:S(2)}, u32[]{:S(2)}) collective-permute-start(bf16[2,128,8,128]{3,1,2,0:T(8,128)(2,1)} %select_convert_fusion.2), channel_id=1, source_target_pairs={{0,2},{1,3},{2,0},{3,1},{4,6},{5,7},{6,4},{7,5},{8,10},{9,11},{10,... | collective-permute-start | bytes 1572872 | tf_op jit(solution)/shard_map/ppermute | solution.py:13
  294.5 43.2 %collective-permute-start.17 = (bf16[2,64,8,128]{3,1,2,0:T(8,128)(2,1)S(1)}, bf16[2,64,8,128]{3,1,2,0:T(8,128)(2,1)S(1)}, u32[]{:S(2)}, u32[]{:S(2)}) collective-permute-start(bf16[2,64,8,128]{3,1,2,0:T(8,128)(2,1)S(1)} %select_convert_fusion.4), channel_id=1, source_target_pairs={{0,4},{1,5},{2,6},{3,7},{4,0},{5,1},{6,2},{7,3},{8,12},{9,13},{10,... | collective-permute-start | bytes 786440 | tf_op jit(solution)/shard_map/ppermute | solution.py:13
  297.8 37.8 %copy-start.4 = (f32[1,256,8,128]{3,1,2,0:T(8,128)S(1)}, f32[1,256,8,128]{3,1,2,0:T(8,128)}, u32[]{:S(2)}) copy-start(f32[1,256,8,128]{3,1,2,0:T(8,128)} %fusion.4) | copy-start | bytes 3145732
  297.8 37.8 %copy-start.6 = (f32[1,256,8,128]{3,1,2,0:T(8,128)S(1)}, f32[1,256,8,128]{3,1,2,0:T(8,128)}, u32[]{:S(2)}) copy-start(f32[1,256,8,128]{3,1,2,0:T(8,128)} %convolution_bitcast_fusion) | copy-start | bytes 3145732
  299.3 44.7 %collective-permute-start.14 = (bf16[2,64,8,128]{3,1,2,0:T(8,128)(2,1)S(1)}, bf16[2,64,8,128]{3,1,2,0:T(8,128)(2,1)S(1)}, u32[]{:S(2)}, u32[]{:S(2)}) collective-permute-start(bf16[2,64,8,128]{3,1,2,0:T(8,128)(2,1)S(1)} %select_convert_fusion.5), channel_id=1, source_target_pairs={{0,2},{1,3},{2,0},{3,1},{4,6},{5,7},{6,4},{7,5},{8,10},{9,11},{10,... | collective-permute-start | bytes 786440 | tf_op jit(solution)/shard_map/ppermute | solution.py:13
  337.1 7.7 %collective-permute-start.12 = (bf16[2,64,8,128]{3,1,2,0:T(8,128)(2,1)S(1)}, bf16[2,64,8,128]{3,1,2,0:T(8,128)(2,1)S(1)}, u32[]{:S(2)}, u32[]{:S(2)}) collective-permute-start(bf16[2,64,8,128]{3,1,2,0:T(8,128)(2,1)S(1)} %select_convert_fusion.6), channel_id=1, source_target_pairs={{0,1},{1,0},{2,3},{3,2},{4,5},{5,4},{6,7},{7,6},{8,9},{9,8},{10,11... | collective-permute-start | bytes 786440 | tf_op jit(solution)/shard_map/ppermute | solution.py:13
  337.9 9.6 %collective-permute-start.18 = (bf16[2,32,8,128]{3,1,2,0:T(8,128)(2,1)S(1)}, bf16[2,32,8,128]{3,1,2,0:T(8,128)(2,1)S(1)}, u32[]{:S(2)}, u32[]{:S(2)}) collective-permute-start(bf16[2,32,8,128]{3,1,2,0:T(8,128)(2,1)S(1)} %select_convert_fusion.7), channel_id=1, source_target_pairs={{0,2},{1,3},{2,0},{3,1},{4,6},{5,7},{6,4},{7,5},{8,10},{9,11},{10,... | collective-permute-start | bytes 393224 | tf_op jit(solution)/shard_map/ppermute | solution.py:13
  344.1 3.9 %collective-permute-start.15 = (bf16[2,32,8,128]{3,1,2,0:T(8,128)(2,1)S(1)}, bf16[2,32,8,128]{3,1,2,0:T(8,128)(2,1)S(1)}, u32[]{:S(2)}, u32[]{:S(2)}) collective-permute-start(bf16[2,32,8,128]{3,1,2,0:T(8,128)(2,1)S(1)} %select_convert_fusion.8), channel_id=1, source_target_pairs={{0,1},{1,0},{2,3},{3,2},{4,5},{5,4},{6,7},{7,6},{8,9},{9,8},{10,11... | collective-permute-start | bytes 393224 | tf_op jit(solution)/shard_map/ppermute | solution.py:13
  347.6 2.9 collective-permute-start.19
  (77 other events, 137.7 us)
where the time goes:
time: 361 us; the launch traced here: 359 us
  blocking collectives  80.4 us (22%)
  local copies, waits for them, and re-layouts  77.8 us (22%)
  waiting for transfers between devices  66.1 us (18%)
  other arithmetic  51.6 us (14%)
  starting transfers between devices  50.4 us (14%)
  matrix products  30.2 us (8%)
    psum x1, blocking collectives, local(): bias_grad = lax.psum(jnp.stack(bias_rows), ('grp', 'seq'))  80.4 us
    ppermute x20, waiting for transfers between devices, partner(): lax.ppermute(x, axis, [(i, i ^ 1 << stride) for i in range(lax.axis_size(...  66.1 us
    ppermute x20, starting transfers between devices, partner(): lax.ppermute(x, axis, [(i, i ^ 1 << stride) for i in range(lax.axis_size(...  50.4 us
    mul x49, local copies, waits for them, and re-layouts, spread(): placed = x[:, None] * weight  33.3 us
    unnamed x233, local copies, waits for them, and re-layouts  19.7 us
    reduce_sum x9, other arithmetic, pick(): return jnp.sum(shaped * weight, axis=1)  10 us
    dot_general x4, matrix products, local(): jnp.einsum('hqk,khd->qhd', pb, gathered[level][1], preferred_element_type...  8.43 us
  transfers between devices with their start and end apart: 20, of which 4 were waited for; matrix products, arithmetic and copies ran while one was open for 18% of the time, Pallas kernels for 0%

commit v1 on v0

v1 whole, which is shorter than its diff:
```python
import jax
import jax.numpy as jnp
from jax import lax
from jax.experimental import pallas as pl
from jax.experimental.pallas import tpu as pltpu
from jax.sharding import PartitionSpec as P

H = 8
HD = 128
LEVELS = 4
ROWS = 128
TILE = 16
BIG = 60 * 1024 * 1024
RES = 8
SCALE = HD ** (-0.5)
F32 = jnp.float32
BF16 = jnp.bfloat16
I32 = jnp.int32
VM = pl.BlockSpec(memory_space=pltpu.VMEM)
SM = pl.BlockSpec(memory_space=pltpu.SMEM)
PARAMS = pltpu.CompilerParams(vmem_limit_bytes=16 * 1024 * 1024)

SLOTS = [(dz, dc) for dz in range(4) for dc in range(2)]
CORE, FAR, FAR2 = 1, 4, 5
NEAR = [2, 6, 3, 7]
SEND = [CORE] + NEAR + [FAR, FAR2]

PER = [8, 4, 2, 1]
BASE = [0, 1024, 1536, 1792]
COMPACT = 1920


def z_perm(dz, dc):
    pairs = []
    for i in range(32):
        x, z, c = i // 8, i % 8 // 2, i % 2
        pairs.append((i, x * 8 + (z + dz) % 4 * 2 + (c ^ dc)))
    return pairs


def xor_perm(bits):
    return [(i, i ^ bits) for i in range(32)]


def dest_head(e, dz, dc):
    z = e // 2
    c = e - 2 * z
    return lax.rem(z + dz, 4) * 2 + (c if dc == 0 else 1 - c)


def dot_nn(a, b):
    return jnp.dot(a, b, preferred_element_type=F32)


def dot_nt(a, b):
    return lax.dot_general(a, b, (((1,), (1,)), ((), ())), preferred_element_type=F32)


def dot_tn(a, b):
    return lax.dot_general(a, b, (((0,), (0,)), ((), ())), preferred_element_type=F32)


def row_order(transposed):
    shape = (ROWS, ROWS)
    packed = lax.broadcasted_iota(I32, shape, 1 if transposed else 0)
    plain = lax.broadcasted_iota(I32, shape, 0 if transposed else 1)
    return (plain == (packed % TILE) * RES + packed // TILE).astype(BF16)


def tile_at(row):
    return pl.ds(pl.multiple_of(row, TILE), TILE)


def head_at(h):
    return pl.ds(pl.multiple_of(h * HD, HD), HD)


def shape(dtype, *dims):
    return jax.ShapeDtypeStruct(dims, dtype)


def call(kernel, outs, ins, out_specs, scratch=(), cost=None):
    return pl.pallas_call(
        kernel,
        out_shape=outs,
        in_specs=ins,
        out_specs=out_specs,
        scratch_shapes=list(scratch),
        compiler_params=PARAMS,
        cost_estimate=cost,
    )


def pack_kernel(offs, k, v, q, d, *rest):
    outs, info, tmp = rest[:8], rest[8], rest[9]
    e = lax.rem(lax.axis_index("seq"), 8)
    order = row_order(False)
    for level in range(LEVELS):
        info[level] = offs[level, e]
    info[4] = e
    for a, ref in enumerate((k, v, q, d)):
        tmp[...] = dot_nn(order, ref[...]).astype(BF16)
        for slot, (dz, dc) in enumerate(SLOTS):
            outs[slot][a] = tmp[:, head_at(dest_head(e, dz, dc))]


def pack(offs, k, v, q, d):
    return pl.pallas_call(
        pack_kernel,
        out_shape=[shape(BF16, 4, ROWS, HD)] * 8 + [shape(I32, 8)],
        in_specs=[SM] + [VM] * 4,
        out_specs=[VM] * 8 + [SM],
        scratch_shapes=[pltpu.VMEM((ROWS, H * HD), BF16)],
        compiler_params=pltpu.CompilerParams(vmem_limit_bytes=BIG),
    )(offs, k, v, q, d)


def by_slot(refs):
    return [refs[([0] + SEND).index(slot)] for slot in range(8)]


def in_order(got):
    return [got[slot] for slot in [0] + SEND]


def pick_kernel(info, *refs):
    got, out = by_slot(refs[:8]), refs[8]
    rows = tile_at(info[3] * TILE)
    for s in range(8):
        out[:, s * TILE : (s + 1) * TILE] = got[s][0:2, rows]


def pick3(info, got):
    return call(pick_kernel, shape(BF16, 2, ROWS, HD), [SM] + [VM] * 8, VM)(
        info, *in_order(got)
    )


def join(pieces):
    return pieces[0] if len(pieces) == 1 else jnp.concatenate(pieces, axis=0)


def load(ref, parts):
    return join([ref[pl.ds(start, size)] for start, size in parts])


def store(ref, parts, value):
    row = 0
    for start, size in parts:
        ref[pl.ds(start, size)] = value[row : row + size]
        row += size


def segments(e):
    mate = jnp.where(lax.rem(e // 2, 2) == 0, 3, 1)
    near = pl.multiple_of(BASE[1] + mate * 128, 128)
    far = pl.multiple_of(BASE[1] + (4 - mate) * 128, 128)
    segs = [(0, [(m * 256, 256)]) for m in range(4)]
    segs.append((1, [(BASE[1], 128), (near, 128)]))
    segs.append((1, [(BASE[1] + 256, 128), (far, 128)]))
    segs.append((2, [(BASE[2], 256)]))
    return segs


def kept(level, off):
    r = 1 << level
    return [s * ROWS + (off + r * t) * TILE for s in range(8) for t in range(PER[level])]


def wide(column):
    return jnp.broadcast_to(column, (column.shape[0], HD))


def twice(x):
    return jnp.concatenate([x, x], axis=1)


def row_sum(x):
    return wide(jnp.sum(x, axis=-1, keepdims=True))


def softmax_rows(q, k, v):
    s = dot_nt(q, k) * SCALE
    m = jnp.max(s, axis=-1, keepdims=True)
    p = jnp.exp(s - m)
    l = jnp.sum(p, axis=-1, keepdims=True)
    p = p * (1.0 / l)
    return p, wide(m + jnp.log(l)), dot_nn(p.astype(BF16), v)


def fwd_kernel(info, *refs):
    got = by_slot(refs[:8])
    comp, p_s, o_s, z_s = refs[8:]
    for a in range(4):
        for s in range(8):
            comp[a, s * ROWS : (s + 1) * ROWS] = got[s][a]
            for level in range(1, LEVELS):
                for t in range(PER[level]):
                    at = tile_at((info[level] + (1 << level) * t) * TILE)
                    row = BASE[level] + (s * PER[level] + t) * TILE
                    comp[a, row : row + TILE] = got[s][a, at]
    for level, parts in segments(info[4]):
        q, k, v = (load(comp.at[a], parts) for a in (2, 0, 1))
        p, lse, o = softmax_rows(q, k, v)
        store(p_s, parts, p)
        store(z_s, parts, lse)
        store(o_s, parts, o)


def forward(info, got):
    return call(
        fwd_kernel,
        [
            shape(BF16, 4, COMPACT, HD),
            shape(F32, BASE[3], 256),
            shape(F32, BASE[3], HD),
            shape(F32, BASE[3], HD),
        ],
        [SM] + [VM] * 8,
        [VM] * 4,
        cost=pl.CostEstimate(flops=250000000, bytes_accessed=6000000, transcendentals=460000),
    )(info, *in_order(got))


def mix_kernel(info, bias, comp, o_s, z_s, xkv, *refs):
    att, do_s, c_s, acc3, xout, bias_out, z_t, lz_s, d_s = refs
    e = info[4]
    offs = [info[level] for level in range(LEVELS)]
    last = slice(BASE[3], COMPACT)
    q3 = comp[2, last]
    k3 = jnp.concatenate([comp[0, last], xkv[0]], axis=0)
    v3 = jnp.concatenate([comp[1, last], xkv[1]], axis=0)
    p3, lse3, o3 = softmax_rows(q3, k3, v3)
    for level in range(LEVELS - 1):
        at = slice(BASE[level], BASE[level + 1])
        z_t[at] = z_s[at] + bias[level, e]
    z_t[last] = lse3 + bias[3, e]

    ninf = jnp.float32(-jnp.inf)
    for s in range(8):
        rows = slice(s * ROWS, (s + 1) * ROWS)
        zs = [z_t[rows]]
        os = [o_s[rows]]
        for level in range(1, LEVELS):
            r = 1 << level
            zp, op = [], []
            for rho in range(RES):
                row = BASE[level] + (s * PER[level] + rho // r) * TILE
                zp.append(jnp.where(offs[level] == rho % r, z_t[row : row + TILE], ninf))
                if level == 3:
                    op.append(o3[s * TILE : (s + 1) * TILE])
                else:
                    op.append(o_s[row : row + TILE])
            zs.append(join(zp))
            os.append(join(op))
        top = jnp.maximum(jnp.maximum(zs[0], zs[1]), jnp.maximum(zs[2], zs[3]))
        es = [jnp.exp(x - top) for x in zs]
        den = es[0] + es[1] + es[2] + es[3]
        inv = 1.0 / den
        out = (es[0] * inv) * os[0]
        for level in range(1, LEVELS):
            out = out + (es[level] * inv) * os[level]
        att[s] = out.astype(BF16)
        lz_s[rows] = top + jnp.log(den)
        d_s[rows] = row_sum(comp[3, rows].astype(F32) * out)

    lane = lax.broadcasted_iota(I32, (1, 128), 1)
    biases = jnp.zeros((1, 128), F32)
    for level in (3, 0, 1, 2):
        end = COMPACT if level == 3 else BASE[level + 1]
        span = slice(BASE[level], end)
        if level == 0:
            lz, dd = lz_s[span], d_s[span]
        else:
            places = kept(level, offs[level])
            lz = join([lz_s[tile_at(x)] for x in places])
            dd = join([d_s[tile_at(x)] for x in places])
        cot = comp[3, span].astype(F32)
        o = o3 if level == 3 else o_s[span]
        a = jnp.exp(z_t[span] - lz)
        do = (a * cot).astype(BF16)
        g = a * (row_sum(cot * o) - dd)
        c = row_sum(do.astype(F32) * o) - g
        total = jnp.sum(g, axis=0, keepdims=True)
        biases = biases + jnp.where(lane == level * H + e, total, 0.0)
        if level < 3:
            do_s[span] = do
            c_s[span] = c
            continue
        dp = dot_nt(do, v3)
        ds = (p3 * (dp - twice(c))).astype(BF16)
        acc3[0] = dot_nn(ds, k3) * SCALE
        for n, value in ((1, dot_tn(ds, q3) * SCALE), (2, dot_tn(p3.astype(BF16), do))):
            acc3[n] = value[:ROWS]
            xout[n - 1] = value[ROWS:].astype(BF16)
    bias_out[...] = biases


def mixing(info, bias, comp, o, z, xkv):
    return call(
        mix_kernel,
        [
            shape(BF16, 8, ROWS, HD),
            shape(BF16, BASE[3], HD),
            shape(F32, BASE[3], HD),
            shape(F32, 3, ROWS, HD),
            shape(BF16, 2, ROWS, HD),
            shape(F32, 1, 128),
        ],
        [SM, SM] + [VM] * 4,
        [VM] * 6,
        [
            pltpu.VMEM((COMPACT, HD), F32),
            pltpu.VMEM((1024, HD), F32),
            pltpu.VMEM((1024, HD), F32),
        ],
        cost=pl.CostEstimate(flops=50000000, bytes_accessed=6000000, transcendentals=40000),
    )(info, bias, comp, o, z, xkv)


def bwd_kernel(info, comp, p_s, do_s, c_s, acc3, att, *refs):
    msgs, own3, acc = refs[:8], refs[8], refs[9]
    offs = [info[level] for level in range(LEVELS)]
    for level, parts in segments(info[4]):
        q, k, v = (load(comp.at[a], parts) for a in (2, 0, 1))
        p, do = load(p_s, parts), load(do_s, parts)
        ds = (p * (dot_nt(do, v) - twice(load(c_s, parts)))).astype(BF16)
        dq = dot_nn(ds, k) * SCALE
        dk = dot_tn(ds, q) * SCALE
        dv = dot_tn(p.astype(BF16), do)
        for which, value in enumerate((dq, dk, dv)):
            if level == 0:
                acc[which, pl.ds(parts[0][0], 256)] = value
                continue
            row = 0
            for start, size in parts:
                for i in range(size // TILE):
                    s = (start - BASE[level]) // (TILE * PER[level]) + i // PER[level]
                    rho = offs[level] + (1 << level) * (i % PER[level])
                    at = tile_at(s * ROWS + rho * TILE)
                    acc[which, at] = acc[which, at] + value[row : row + TILE]
                    row += TILE
    for s in range(8):
        at = tile_at(s * ROWS + offs[3] * TILE)
        part = slice(s * TILE, (s + 1) * TILE)
        for which in range(3):
            total = acc[which, at] + acc3[which, part]
            acc[which, at] = total
            if which > 0:
                own3[which - 1, part] = total
    for s in range(8):
        msgs[s][0] = att[s]
        for which in range(3):
            msgs[s][1 + which] = acc[which, s * ROWS : (s + 1) * ROWS].astype(BF16)


MSG = shape(BF16, 4, ROWS, HD)


def backward(info, comp, p, do, c, acc3, att):
    return call(
        bwd_kernel,
        [MSG] * 8 + [shape(F32, 2, ROWS, HD)],
        [SM] + [VM] * 6,
        [VM] * 9,
        [pltpu.VMEM((3, 1024, HD), F32)],
        cost=pl.CostEstimate(flops=600000000, bytes_accessed=6000000, transcendentals=0),
    )(info, comp, p, do, c, acc3, att)


def merge_kernel(info, *refs):
    own3, xin, bias = refs[8:11]
    outs, spread = refs[11:19], refs[19]
    for s in range(8):
        at = slice(s * TILE, (s + 1) * TILE)
        outs[s][...] = (own3[:, at] + xin[:, at].astype(F32)).astype(BF16)
    spread[...] = jnp.broadcast_to(bias[:, : LEVELS * H], spread.shape)


def merge(info, msgs, own3, xin, bias, devices):
    tile = pl.BlockSpec((2, TILE, HD), lambda i, info: (1, info[3], 0))

    def full(*dims):
        return pl.BlockSpec(dims, lambda i, info: (0,) * len(dims))

    rows = full(2, ROWS, HD)
    return pl.pallas_call(
        merge_kernel,
        out_shape=[MSG] * 8 + [shape(F32, devices, LEVELS * H)],
        grid_spec=pltpu.PrefetchScalarGridSpec(
            num_scalar_prefetch=1,
            grid=(1,),
            in_specs=[pl.BlockSpec(memory_space=pl.ANY)] * 8 + [rows, rows, full(1, 128)],
            out_specs=[tile] * 8 + [full(devices, LEVELS * H)],
        ),
        input_output_aliases={1 + n: n for n in range(8)},
        compiler_params=PARAMS,
    )(info, *msgs, own3, xin, bias)


def unpack_kernel(info, *refs):
    got, bias = by_slot(refs[:8]), refs[8]
    outs, bias_out = refs[9:13], refs[13]
    e = info[4]
    order = row_order(True)
    for a in range(4):
        for slot, (dz, dc) in enumerate(SLOTS):
            at = head_at(dest_head(e, dz, dc))
            outs[a][:, at] = dot_nn(order, got[slot][a]).astype(BF16)
    total = jnp.sum(bias[...], axis=0, keepdims=True)
    for level in range(LEVELS):
        bias_out[level : level + 1] = total[:, level * H : (level + 1) * H]


def unpack(info, got, bias):
    return call(
        unpack_kernel,
        [shape(BF16, ROWS, H * HD)] * 4 + [shape(F32, LEVELS, H)],
        [SM] + [VM] * 9,
        [VM] * 5,
    )(info, *in_order(got), bias)


def local(queries, keys, values, cotangent, head_offsets, level_bias):
    def move(x, pairs):
        return lax.ppermute(x, "seq", pairs)

    packed = pack(head_offsets, keys, values, queries, cotangent)
    sent, info = packed[:8], packed[8]
    got = [sent[0]] + [None] * 7
    for slot in SEND:
        got[slot] = move(sent[slot], z_perm(*SLOTS[slot]))
    xkv = move(pick3(info, got), xor_perm(8))
    comp, p, o, z = forward(info, got)
    att, do, c, acc3, xout, bias = mixing(info, level_bias, comp, o, z, xkv)
    xin = move(xout, xor_perm(8))
    *msgs, own3 = backward(info, comp, p, do, c, acc3, att)
    devices = lax.axis_size("grp") * lax.axis_size("seq")
    *msgs, spread = merge(info, msgs, own3, xin, bias, devices)
    back = [msgs[0]] + [None] * 7
    for slot in SEND:
        dz, dc = SLOTS[slot]
        back[slot] = move(msgs[slot], z_perm(-dz, dc))
    bias = lax.all_to_all(spread, ("grp", "seq"), 0, 0, tiled=True)
    return tuple(unpack(info, back, bias))


def solution(mesh):
    rows = P(("grp", "seq"), None)
    return jax.shard_map(
        local,
        mesh=mesh,
        in_specs=(rows, rows, rows, rows, P(), P()),
        out_specs=(rows, rows, rows, rows, P()),
        check_vma=False,
    )
```

time: 361 us -> 91.5 us (0.25)
  local copies, waits for them, and re-layouts: 77.8 us -> 1.57 us
  waiting for transfers between devices: 66.1 us -> 6.97 us
  blocking collectives: 80.4 us -> 26.8 us
  other arithmetic: 51.6 us -> 0 us
  matrix products: 30.2 us -> 0 us
  Pallas kernels: 0 us -> 13 us
  starting transfers between devices: 50.4 us -> 42.3 us
    psum x1 -> x0, blocking collectives: 80.4 us -> none  [local(): bias_grad = lax.psum(jnp.stack(bias_rows), ('grp', 'seq'))]
    ppermute x20 -> x16, waiting for transfers between devices: 66.1 us -> 6.97 us  [move(): return lax.ppermute(x, 'seq', pairs)]
    mul x54 -> x0, local copies, waits for them, and re-layouts: 36.4 us -> none  [the longest x49 33.3 us: spread(): placed = x[:, None] * weight]
    dot_general x24 -> x0, matrix products: 30.2 us -> none  [the longest x4 8.43 us: local(): jnp.einsum('hqk,khd->qhd', pb, gathered[level][1], preferred_element_type...]
    all_to_all x0 -> x1, blocking collectives: none -> 26.8 us  [local(): bias = lax.all_to_all(spread, ('grp', 'seq'), 0, 0, tiled=True)]
    unnamed x233 -> x8, local copies, waits for them, and re-layouts: 19.7 us -> 1.57 us
    reduce_sum x16 -> x0, other arithmetic: 14.2 us -> none  [the longest x9 10 us: pick(): return jnp.sum(shaped * weight, axis=1)]
    pallas_call x0 -> x7, Pallas kernels: none -> 13 us  [the longest x1 2.9 us: backward(): call(bwd_kernel, [MSG] * 8 + [shape(F32, 2, ROWS, HD)], [SM] + [VM] * 6,...]
  transfers between devices with their start and end apart: 20 -> 16, of which waited for: 4 -> 4; matrix products, arithmetic and copies ran while one was open for 18% -> 0% of each run, Pallas kernels for 0% -> 6%
where the time goes in v1:
time: 91.5 us; the launch traced here: 91.4 us
  starting transfers between devices  42.3 us (46%)
  blocking collectives  26.8 us (29%)
  Pallas kernels  13 us (14%)
  waiting for transfers between devices  6.97 us (8%)
  local copies, waits for them, and re-layouts  1.57 us (2%)
    ppermute x16, starting transfers between devices, move(): return lax.ppermute(x, 'seq', pairs)  42.3 us
    all_to_all x1, blocking collectives, local(): bias = lax.all_to_all(spread, ('grp', 'seq'), 0, 0, tiled=True)  26.8 us
    ppermute x16, waiting for transfers between devices, move(): return lax.ppermute(x, 'seq', pairs)  6.97 us
    pallas_call x1, Pallas kernels, backward(): call(bwd_kernel, [MSG] * 8 + [shape(F32, 2, ROWS, HD)], [SM] + [VM] * 6,...  2.9 us
    pallas_call x1, Pallas kernels, pack(): pl.pallas_call(pack_kernel, out_shape=[shape(BF16, 4, ROWS, HD)] * 8 + [s...  2.74 us
    pallas_call x1, Pallas kernels, mixing(): call(mix_kernel, [shape(BF16, 8, ROWS, HD), shape(BF16, BASE[3], HD), sha...  2.29 us
    pallas_call x1, Pallas kernels, forward(): call(fwd_kernel, [shape(BF16, 4, COMPACT, HD), shape(F32, BASE[3], 256),...  2.16 us
  transfers between devices with their start and end apart: 16, of which 4 were waited for; matrix products, arithmetic and copies ran while one was open for 0% of the time, Pallas kernels for 6%

profile of v1, /device:TPU:1, one launch (start us, length us, event | category | flops | bytes accessed | tf_op | source)
XLA Modules:
  0.0 91.4 jit_solution(17811975430981581621)
XLA Ops:
  0.6 0.0 copy-start.3
  0.6 2.7 %shard_map.101 = (bf16[4,128,128]{2,1,0:T(8,128)(2,1)}, bf16[4,128,128]{2,1,0:T(8,128)(2,1)}, bf16[4,128,128]{2,1,0:T(8,128)(2,1)}, bf16[4,128,128]{2,1,0:T(8,12...) custom-call(s32[4,8]{1,0:T(4,128)} %offs.1, ...), custom_call_target="tpu_custom_call" | custom-call | tf_op jit(solution)/shard_map/pallas_call | solution.py:108
  3.4 0.0 copy-start.2
  3.4 3.3 %collective-permute-start = (bf16[4,128,128]{2,1,0:T(8,128)(2,1)}, bf16[4,128,128]{2,1,0:T(8,128)(2,1)S(1)}, u32[]{:S(2)}, u32[]{:S(2)}) collective-permute-start(bf16[4,128,128]{2,1,0:T(8,128)(2,1)} %get-tuple-element.44), channel_id=1, source_target_pairs={{0,1},{1,0},{2,3},{3,2},{4,5},{5,4},{6,7},{7,6},{8,9},{9,8},{10,11... | collective-permute-start | bytes 393224 | tf_op jit(solution)/shard_map/ppermute | solution.py:426
  6.7 1.3 %collective-permute-start.1 = (bf16[4,128,128]{2,1,0:T(8,128)(2,1)}, bf16[4,128,128]{2,1,0:T(8,128)(2,1)S(1)}, u32[]{:S(2)}, u32[]{:S(2)}) collective-permute-start(bf16[4,128,128]{2,1,0:T(8,128)(2,1)} %get-tuple-element.45), channel_id=1, source_target_pairs={{0,2},{1,3},{2,4},{3,5},{4,6},{5,7},{6,0},{7,1},{8,10},{9,11},{10,... | collective-permute-start | bytes 393224 | tf_op jit(solution)/shard_map/ppermute | solution.py:426
  8.0 3.0 %collective-permute-start.2 = (bf16[4,128,128]{2,1,0:T(8,128)(2,1)}, bf16[4,128,128]{2,1,0:T(8,128)(2,1)S(1)}, u32[]{:S(2)}, u32[]{:S(2)}) collective-permute-start(bf16[4,128,128]{2,1,0:T(8,128)(2,1)} %get-tuple-element.46), channel_id=1, source_target_pairs={{0,6},{1,7},{2,0},{3,1},{4,2},{5,3},{6,4},{7,5},{8,14},{9,15},{10,... | collective-permute-start | bytes 393224 | tf_op jit(solution)/shard_map/ppermute | solution.py:426
  11.0 1.4 %collective-permute-start.3 = (bf16[4,128,128]{2,1,0:T(8,128)(2,1)}, bf16[4,128,128]{2,1,0:T(8,128)(2,1)S(1)}, u32[]{:S(2)}, u32[]{:S(2)}) collective-permute-start(bf16[4,128,128]{2,1,0:T(8,128)(2,1)} %get-tuple-element.47), channel_id=1, source_target_pairs={{0,3},{1,2},{2,5},{3,4},{4,7},{5,6},{6,1},{7,0},{8,11},{9,10},{10,... | collective-permute-start | bytes 393224 | tf_op jit(solution)/shard_map/ppermute | solution.py:426
  12.4 2.4 %collective-permute-start.4 = (bf16[4,128,128]{2,1,0:T(8,128)(2,1)}, bf16[4,128,128]{2,1,0:T(8,128)(2,1)S(1)}, u32[]{:S(2)}, u32[]{:S(2)}) collective-permute-start(bf16[4,128,128]{2,1,0:T(8,128)(2,1)} %get-tuple-element.48), channel_id=1, source_target_pairs={{0,7},{1,6},{2,1},{3,0},{4,3},{5,2},{6,5},{7,4},{8,15},{9,14},{10,... | collective-permute-start | bytes 393224 | tf_op jit(solution)/shard_map/ppermute | solution.py:426
  14.9 0.0 collective-permute-done.refs_1_
  14.9 4.5 %collective-permute-start.5 = (bf16[4,128,128]{2,1,0:T(8,128)(2,1)}, bf16[4,128,128]{2,1,0:T(8,128)(2,1)S(1)}, u32[]{:S(2)}, u32[]{:S(2)}) collective-permute-start(bf16[4,128,128]{2,1,0:T(8,128)(2,1)} %get-tuple-element.49), channel_id=1, source_target_pairs={{0,4},{1,5},{2,6},{3,7},{4,0},{5,1},{6,2},{7,3},{8,12},{9,13},{10,... | collective-permute-start | bytes 393224 | tf_op jit(solution)/shard_map/ppermute | solution.py:426
  19.4 0.0 collective-permute-done.1.refs_2_
  19.4 6.1 %collective-permute-start.6 = (bf16[4,128,128]{2,1,0:T(8,128)(2,1)}, bf16[4,128,128]{2,1,0:T(8,128)(2,1)S(1)}, u32[]{:S(2)}, u32[]{:S(2)}) collective-permute-start(bf16[4,128,128]{2,1,0:T(8,128)(2,1)} %get-tuple-element.50), channel_id=1, source_target_pairs={{0,5},{1,4},{2,7},{3,6},{4,1},{5,0},{6,3},{7,2},{8,13},{9,12},{10,... | collective-permute-start | bytes 393224 | tf_op jit(solution)/shard_map/ppermute | solution.py:426
  25.4 0.0 collective-permute-done.2.refs_3_
  25.4 0.0 collective-permute-done.3.refs_4_
  25.4 1.7 %collective-permute-done.4.refs_5_ = bf16[4,128,128]{2,1,0:T(8,128)(2,1)S(1)} collective-permute-done((bf16[4,128,128]{2,1,0:T(8,128)(2,1)}, bf16[4,128,128]{2,1,0:T(8,128)(2,1)S(1)}, u32[]{:S(2)}, u32[]{:S(2)}) %collective-permute-start.4) | collective-permute-done | bytes 131104 | tf_op jit(solution)/shard_map/ppermute | solution.py:426
  27.1 1.0 %collective-permute-done.5.refs_6_ = bf16[4,128,128]{2,1,0:T(8,128)(2,1)S(1)} collective-permute-done((bf16[4,128,128]{2,1,0:T(8,128)(2,1)}, bf16[4,128,128]{2,1,0:T(8,128)(2,1)S(1)}, u32[]{:S(2)}, u32[]{:S(2)}) %collective-permute-start.5) | collective-permute-done | bytes 131104 | tf_op jit(solution)/shard_map/ppermute | solution.py:426
  28.2 4.1 %collective-permute-done.6.refs_7_ = bf16[4,128,128]{2,1,0:T(8,128)(2,1)S(1)} collective-permute-done((bf16[4,128,128]{2,1,0:T(8,128)(2,1)}, bf16[4,128,128]{2,1,0:T(8,128)(2,1)S(1)}, u32[]{:S(2)}, u32[]{:S(2)}) %collective-permute-start.6) | collective-permute-done | bytes 131104 | tf_op jit(solution)/shard_map/ppermute | solution.py:426
  32.3 0.0 copy-start
  32.3 0.9 copy-done
  33.2 0.0 copy-start.1
  33.2 0.7 copy-done.1
  33.9 0.6 shard_map.103
  34.4 1.3 %collective-permute-start.7 = (bf16[2,128,128]{2,1,0:T(8,128)(2,1)S(1)}, bf16[2,128,128]{2,1,0:T(8,128)(2,1)S(1)}, u32[]{:S(2)}, u32[]{:S(2)}) collective-permute-start(bf16[2,128,128]{2,1,0:T(8,128)(2,1)S(1)} %shard_map.103), channel_id=1, source_target_pairs={{0,8},{1,9},{2,10},{3,11},{4,12},{5,13},{6,14},{7,15},{8,0},{9,1},... | collective-permute-start | bytes 196616 | tf_op jit(solution)/shard_map/ppermute | solution.py:426
  35.8 2.2 %shard_map.102 = (bf16[4,1920,128]{2,1,0:T(8,128)(2,1)S(1)}, f32[1792,256]{1,0:T(8,128)S(1)}, f32[1792,128]{1,0:T(8,128)S(1)}, f32[1792,128]{1,0:T(8,128)S(1)}) custom-call(s32[8]{0:T(128)S(1)} %copy-done.1, bf16[4,128,128]{2,1,0:T(8,128)(2,1)S(1)} %copy-done, bf16[4,128,128]{2,1,0:T(8,128)(2,1)S(1)} %collective-permute-done.refs_1_, ...), custom_call_target="tpu_custom_call" | custom-call | flops 250000000 | bytes 6000000 | tf_op jit(solution)/shard_map/pallas_call | solution.py:211
  37.9 0.1 collective-permute-done.7.xkv
  38.0 0.0 copy-done.3
  38.0 0.0 copy-done.2
  38.0 2.3 %shard_map.104 = (bf16[8,128,128]{2,1,0:T(8,128)(2,1)S(1)}, bf16[1792,128]{1,0:T(8,128)(2,1)S(1)}, f32[1792,128]{1,0:T(8,128)S(1)}, f32[3,128,128]{2,1,0:T(8,128...) custom-call(s32[8]{0:T(128)S(1)} %copy-done.2, f32[4,8]{1,0:T(4,128)S(1)} %copy-done.3, ...), custom_call_target="tpu_custom_call" | custom-call | flops 50000000 | bytes 6000000 | tf_op jit(solution)/shard_map/pallas_call | solution.py:300
  40.3 1.3 %collective-permute-start.8 = (bf16[2,128,128]{2,1,0:T(8,128)(2,1)S(1)}, bf16[2,128,128]{2,1,0:T(8,128)(2,1)S(1)}, u32[]{:S(2)}, u32[]{:S(2)}) collective-permute-start(bf16[2,128,128]{2,1,0:T(8,128)(2,1)S(1)} %get-tuple-element.68), channel_id=1, source_target_pairs={{0,8},{1,9},{2,10},{3,11},{4,12},{5,13},{6,14},{7,15},{8,0},{9,1},... | collective-permute-start | bytes 196616 | tf_op jit(solution)/shard_map/ppermute | solution.py:426
  41.6 2.9 %shard_map.105 = (bf16[4,128,128]{2,1,0:T(8,128)(2,1)S(1)}, bf16[4,128,128]{2,1,0:T(8,128)(2,1)S(1)}, bf16[4,128,128]{2,1,0:T(8,128)(2,1)S(1)}, bf16[4,128,128]{...) custom-call(s32[8]{0:T(128)S(1)} %copy-done.2, ...), custom_call_target="tpu_custom_call" | custom-call | flops 600000000 | bytes 6000000 | tf_op jit(solution)/shard_map/pallas_call | solution.py:361
  44.5 0.0 collective-permute-done.8.refs_9_
  44.6 0.6 shard_map.106
  45.1 1.4 %collective-permute-start.9 = (bf16[4,128,128]{2,1,0:T(8,128)(2,1)S(1)}, bf16[4,128,128]{2,1,0:T(8,128)(2,1)S(1)}, u32[]{:S(2)}, u32[]{:S(2)}) collective-permute-start(bf16[4,128,128]{2,1,0:T(8,128)(2,1)S(1)} %get-tuple-element.71), channel_id=1, source_target_pairs={{0,1},{1,0},{2,3},{3,2},{4,5},{5,4},{6,7},{7,6},{8,9},{9,8},{10,11... | collective-permute-start | bytes 393224 | tf_op jit(solution)/shard_map/ppermute | solution.py:426
  46.5 6.7 %collective-permute-start.10 = (bf16[4,128,128]{2,1,0:T(8,128)(2,1)S(1)}, bf16[4,128,128]{2,1,0:T(8,128)(2,1)S(1)}, u32[]{:S(2)}, u32[]{:S(2)}) collective-permute-start(bf16[4,128,128]{2,1,0:T(8,128)(2,1)S(1)} %get-tuple-element.72), channel_id=1, source_target_pairs={{0,6},{1,7},{2,0},{3,1},{4,2},{5,3},{6,4},{7,5},{8,14},{9,15},{10,... | collective-permute-start | bytes 393224 | tf_op jit(solution)/shard_map/ppermute | solution.py:426
  53.3 0.0 collective-permute-start.11
  53.3 4.3 %collective-permute-start.12 = (bf16[4,128,128]{2,1,0:T(8,128)(2,1)S(1)}, bf16[4,128,128]{2,1,0:T(8,128)(2,1)S(1)}, u32[]{:S(2)}, u32[]{:S(2)}) collective-permute-start(bf16[4,128,128]{2,1,0:T(8,128)(2,1)S(1)} %get-tuple-element.74), channel_id=1, source_target_pairs={{0,7},{1,6},{2,1},{3,0},{4,3},{5,2},{6,5},{7,4},{8,15},{9,14},{10,... | collective-permute-start | bytes 393224 | tf_op jit(solution)/shard_map/ppermute | solution.py:426
  57.6 0.0 collective-permute-start.13
  57.6 0.0 collective-permute-done.9.refs_1_
  57.6 2.1 %collective-permute-start.14 = (bf16[4,128,128]{2,1,0:T(8,128)(2,1)S(1)}, bf16[4,128,128]{2,1,0:T(8,128)(2,1)S(1)}, u32[]{:S(2)}, u32[]{:S(2)}) collective-permute-start(bf16[4,128,128]{2,1,0:T(8,128)(2,1)S(1)} %get-tuple-element.76), channel_id=1, source_target_pairs={{0,4},{1,5},{2,6},{3,7},{4,0},{5,1},{6,2},{7,3},{8,12},{9,13},{10,... | collective-permute-start | bytes 393224 | tf_op jit(solution)/shard_map/ppermute | solution.py:426
  59.7 0.0 collective-permute-done.10.refs_2_
  59.7 3.1 %collective-permute-start.15 = (bf16[4,128,128]{2,1,0:T(8,128)(2,1)S(1)}, bf16[4,128,128]{2,1,0:T(8,128)(2,1)S(1)}, u32[]{:S(2)}, u32[]{:S(2)}) collective-permute-start(bf16[4,128,128]{2,1,0:T(8,128)(2,1)S(1)} %get-tuple-element.77), channel_id=1, source_target_pairs={{0,5},{1,4},{2,7},{3,6},{4,1},{5,0},{6,3},{7,2},{8,13},{9,12},{10,... | collective-permute-start | bytes 393224 | tf_op jit(solution)/shard_map/ppermute | solution.py:426
  62.8 26.8 %all_to_all.11 = f32[256,1,32]{2,1,0:T(1,128)S(1)} all-to-all(f32[256,1,32]{2,1,0:T(1,128)S(1)} %bitcast.5), channel_id=1, replica_groups=mesh['grp'=8,'seq'=32] {'grp','seq'}, dimensions={0} | all-to-all | bytes 65536 | tf_op jit(solution)/shard_map/all_to_all | solution.py:444
  89.5 0.0 collective-permute-done.11.refs_3_
  89.6 0.0 collective-permute-done.12.refs_4_
  89.6 0.0 collective-permute-done.13.refs_5_
  89.6 0.0 collective-permute-done.14.refs_6_
  89.6 0.0 collective-permute-done.15.refs_7_
  89.6 1.8 %shard_map.107 = (bf16[128,1024]{1,0:T(8,128)(2,1)}, bf16[128,1024]{1,0:T(8,128)(2,1)}, bf16[128,1024]{1,0:T(8,128)(2,1)}, bf16[128,1024]{1,0:T(8,128)(2,1)}, f32[4,8]{1,0:T(4,128)}) custom-call(s32[8]{0:T(128)S(1)} %copy-done.2, bf16[4,128,128]{2,1,0:T(8,128)(2,1)S(1)} %get-tuple-element.70.refs_0_, ...), custom_call_target="tpu_custom_call" | custom-call | tf_op jit(solution)/shard_map/pallas_call | solution.py:416
Async XLA Ops:
  0.6 37.4 %copy-start.3 = (f32[4,8]{1,0:T(4,128)S(1)}, f32[4,8]{1,0:T(4,128)}, u32[]{:S(2)}) copy-start(f32[4,8]{1,0:T(4,128)} %bias.1) | copy-start | bytes 388
  3.4 34.6 %copy-start.2 = (s32[8]{0:T(128)S(1)}, s32[8]{0:T(128)}, u32[]{:S(2)}) copy-start(s32[8]{0:T(128)} %get-tuple-element.42.info) | copy-start | bytes 100
  3.4 11.5 %collective-permute-start = (bf16[4,128,128]{2,1,0:T(8,128)(2,1)}, bf16[4,128,128]{2,1,0:T(8,128)(2,1)S(1)}, u32[]{:S(2)}, u32[]{:S(2)}) collective-permute-start(bf16[4,128,128]{2,1,0:T(8,128)(2,1)} %get-tuple-element.44), channel_id=1, source_target_pairs={{0,1},{1,0},{2,3},{3,2},{4,5},{5,4},{6,7},{7,6},{8,9},{9,8},{10,11... | collective-permute-start | bytes 393224 | tf_op jit(solution)/shard_map/ppermute | solution.py:426
  6.7 12.6 %collective-permute-start.1 = (bf16[4,128,128]{2,1,0:T(8,128)(2,1)}, bf16[4,128,128]{2,1,0:T(8,128)(2,1)S(1)}, u32[]{:S(2)}, u32[]{:S(2)}) collective-permute-start(bf16[4,128,128]{2,1,0:T(8,128)(2,1)} %get-tuple-element.45), channel_id=1, source_target_pairs={{0,2},{1,3},{2,4},{3,5},{4,6},{5,7},{6,0},{7,1},{8,10},{9,11},{10,... | collective-permute-start | bytes 393224 | tf_op jit(solution)/shard_map/ppermute | solution.py:426
  8.0 17.4 %collective-permute-start.2 = (bf16[4,128,128]{2,1,0:T(8,128)(2,1)}, bf16[4,128,128]{2,1,0:T(8,128)(2,1)S(1)}, u32[]{:S(2)}, u32[]{:S(2)}) collective-permute-start(bf16[4,128,128]{2,1,0:T(8,128)(2,1)} %get-tuple-element.46), channel_id=1, source_target_pairs={{0,6},{1,7},{2,0},{3,1},{4,2},{5,3},{6,4},{7,5},{8,14},{9,15},{10,... | collective-permute-start | bytes 393224 | tf_op jit(solution)/shard_map/ppermute | solution.py:426
  11.0 14.4 %collective-permute-start.3 = (bf16[4,128,128]{2,1,0:T(8,128)(2,1)}, bf16[4,128,128]{2,1,0:T(8,128)(2,1)S(1)}, u32[]{:S(2)}, u32[]{:S(2)}) collective-permute-start(bf16[4,128,128]{2,1,0:T(8,128)(2,1)} %get-tuple-element.47), channel_id=1, source_target_pairs={{0,3},{1,2},{2,5},{3,4},{4,7},{5,6},{6,1},{7,0},{8,11},{9,10},{10,... | collective-permute-start | bytes 393224 | tf_op jit(solution)/shard_map/ppermute | solution.py:426
  12.4 14.7 %collective-permute-start.4 = (bf16[4,128,128]{2,1,0:T(8,128)(2,1)}, bf16[4,128,128]{2,1,0:T(8,128)(2,1)S(1)}, u32[]{:S(2)}, u32[]{:S(2)}) collective-permute-start(bf16[4,128,128]{2,1,0:T(8,128)(2,1)} %get-tuple-element.48), channel_id=1, source_target_pairs={{0,7},{1,6},{2,1},{3,0},{4,3},{5,2},{6,5},{7,4},{8,15},{9,14},{10,... | collective-permute-start | bytes 393224 | tf_op jit(solution)/shard_map/ppermute | solution.py:426
  14.9 13.3 %collective-permute-start.5 = (bf16[4,128,128]{2,1,0:T(8,128)(2,1)}, bf16[4,128,128]{2,1,0:T(8,128)(2,1)S(1)}, u32[]{:S(2)}, u32[]{:S(2)}) collective-permute-start(bf16[4,128,128]{2,1,0:T(8,128)(2,1)} %get-tuple-element.49), channel_id=1, source_target_pairs={{0,4},{1,5},{2,6},{3,7},{4,0},{5,1},{6,2},{7,3},{8,12},{9,13},{10,... | collective-permute-start | bytes 393224 | tf_op jit(solution)/shard_map/ppermute | solution.py:426
  19.4 12.9 %collective-permute-start.6 = (bf16[4,128,128]{2,1,0:T(8,128)(2,1)}, bf16[4,128,128]{2,1,0:T(8,128)(2,1)S(1)}, u32[]{:S(2)}, u32[]{:S(2)}) collective-permute-start(bf16[4,128,128]{2,1,0:T(8,128)(2,1)} %get-tuple-element.50), channel_id=1, source_target_pairs={{0,5},{1,4},{2,7},{3,6},{4,1},{5,0},{6,3},{7,2},{8,13},{9,12},{10,... | collective-permute-start | bytes 393224 | tf_op jit(solution)/shard_map/ppermute | solution.py:426
  32.3 0.9 copy-start
  33.2 0.7 copy-start.1
  34.4 3.6 %collective-permute-start.7 = (bf16[2,128,128]{2,1,0:T(8,128)(2,1)S(1)}, bf16[2,128,128]{2,1,0:T(8,128)(2,1)S(1)}, u32[]{:S(2)}, u32[]{:S(2)}) collective-permute-start(bf16[2,128,128]{2,1,0:T(8,128)(2,1)S(1)} %shard_map.103), channel_id=1, source_target_pairs={{0,8},{1,9},{2,10},{3,11},{4,12},{5,13},{6,14},{7,15},{8,0},{9,1},... | collective-permute-start | bytes 196616 | tf_op jit(solution)/shard_map/ppermute | solution.py:426
  40.3 4.3 %collective-permute-start.8 = (bf16[2,128,128]{2,1,0:T(8,128)(2,1)S(1)}, bf16[2,128,128]{2,1,0:T(8,128)(2,1)S(1)}, u32[]{:S(2)}, u32[]{:S(2)}) collective-permute-start(bf16[2,128,128]{2,1,0:T(8,128)(2,1)S(1)} %get-tuple-element.68), channel_id=1, source_target_pairs={{0,8},{1,9},{2,10},{3,11},{4,12},{5,13},{6,14},{7,15},{8,0},{9,1},... | collective-permute-start | bytes 196616 | tf_op jit(solution)/shard_map/ppermute | solution.py:426
  45.1 12.4 %collective-permute-start.9 = (bf16[4,128,128]{2,1,0:T(8,128)(2,1)S(1)}, bf16[4,128,128]{2,1,0:T(8,128)(2,1)S(1)}, u32[]{:S(2)}, u32[]{:S(2)}) collective-permute-start(bf16[4,128,128]{2,1,0:T(8,128)(2,1)S(1)} %get-tuple-element.71), channel_id=1, source_target_pairs={{0,1},{1,0},{2,3},{3,2},{4,5},{5,4},{6,7},{7,6},{8,9},{9,8},{10,11... | collective-permute-start | bytes 393224 | tf_op jit(solution)/shard_map/ppermute | solution.py:426
  46.5 13.1 %collective-permute-start.10 = (bf16[4,128,128]{2,1,0:T(8,128)(2,1)S(1)}, bf16[4,128,128]{2,1,0:T(8,128)(2,1)S(1)}, u32[]{:S(2)}, u32[]{:S(2)}) collective-permute-start(bf16[4,128,128]{2,1,0:T(8,128)(2,1)S(1)} %get-tuple-element.72), channel_id=1, source_target_pairs={{0,6},{1,7},{2,0},{3,1},{4,2},{5,3},{6,4},{7,5},{8,14},{9,15},{10,... | collective-permute-start | bytes 393224 | tf_op jit(solution)/shard_map/ppermute | solution.py:426
  53.3 36.3 %collective-permute-start.11 = (bf16[4,128,128]{2,1,0:T(8,128)(2,1)S(1)}, bf16[4,128,128]{2,1,0:T(8,128)(2,1)S(1)}, u32[]{:S(2)}, u32[]{:S(2)}) collective-permute-start(bf16[4,128,128]{2,1,0:T(8,128)(2,1)S(1)} %get-tuple-element.73), channel_id=1, source_target_pairs={{0,2},{1,3},{2,4},{3,5},{4,6},{5,7},{6,0},{7,1},{8,10},{9,11},{10,... | collective-permute-start | bytes 393224 | tf_op jit(solution)/shard_map/ppermute | solution.py:426
  53.3 36.3 %collective-permute-start.12 = (bf16[4,128,128]{2,1,0:T(8,128)(2,1)S(1)}, bf16[4,128,128]{2,1,0:T(8,128)(2,1)S(1)}, u32[]{:S(2)}, u32[]{:S(2)}) collective-permute-start(bf16[4,128,128]{2,1,0:T(8,128)(2,1)S(1)} %get-tuple-element.74), channel_id=1, source_target_pairs={{0,7},{1,6},{2,1},{3,0},{4,3},{5,2},{6,5},{7,4},{8,15},{9,14},{10,... | collective-permute-start | bytes 393224 | tf_op jit(solution)/shard_map/ppermute | solution.py:426
  57.6 32.0 %collective-permute-start.13 = (bf16[4,128,128]{2,1,0:T(8,128)(2,1)S(1)}, bf16[4,128,128]{2,1,0:T(8,128)(2,1)S(1)}, u32[]{:S(2)}, u32[]{:S(2)}) collective-permute-start(bf16[4,128,128]{2,1,0:T(8,128)(2,1)S(1)} %get-tuple-element.75), channel_id=1, source_target_pairs={{0,3},{1,2},{2,5},{3,4},{4,7},{5,6},{6,1},{7,0},{8,11},{9,10},{10,... | collective-permute-start | bytes 393224 | tf_op jit(solution)/shard_map/ppermute | solution.py:426
  57.6 32.0 %collective-permute-start.14 = (bf16[4,128,128]{2,1,0:T(8,128)(2,1)S(1)}, bf16[4,128,128]{2,1,0:T(8,128)(2,1)S(1)}, u32[]{:S(2)}, u32[]{:S(2)}) collective-permute-start(bf16[4,128,128]{2,1,0:T(8,128)(2,1)S(1)} %get-tuple-element.76), channel_id=1, source_target_pairs={{0,4},{1,5},{2,6},{3,7},{4,0},{5,1},{6,2},{7,3},{8,12},{9,13},{10,... | collective-permute-start | bytes 393224 | tf_op jit(solution)/shard_map/ppermute | solution.py:426
  59.7 29.9 %collective-permute-start.15 = (bf16[4,128,128]{2,1,0:T(8,128)(2,1)S(1)}, bf16[4,128,128]{2,1,0:T(8,128)(2,1)S(1)}, u32[]{:S(2)}, u32[]{:S(2)}) collective-permute-start(bf16[4,128,128]{2,1,0:T(8,128)(2,1)S(1)} %get-tuple-element.77), channel_id=1, source_target_pairs={{0,5},{1,4},{2,7},{3,6},{4,1},{5,0},{6,3},{7,2},{8,13},{9,12},{10,... | collective-permute-start | bytes 393224 | tf_op jit(solution)/shard_map/ppermute | solution.py:426

commit v2 on v1

--- a/solution.py
+++ b/solution.py
@@ -10,7 +10,8 @@
 LEVELS = 4
 ROWS = 128
 TILE = 16
-BIG = 60 * 1024 * 1024
+SHADOW = pl.CostEstimate(flops=0, bytes_accessed=200000000, transcendentals=0)
+BIG = 53 * 1024 * 1024
 RES = 8
 SCALE = HD ** (-0.5)
 F32 = jnp.float32
@@ -30,12 +31,20 @@
 COMPACT = 1920
 
 
+GROUPS = [[g * 32 + i for g in range(8) for i in range(32) if i // 8 % 2 == n] for n in range(2)]
+
+
 def z_perm(dz, dc):
     pairs = []
     for i in range(32):
         x, z, c = i // 8, i % 8 // 2, i % 2
-        pairs.append((i, x * 8 + (z + dz) % 4 * 2 + (c ^ dc)))
+        step = -dz if c ^ dc else dz
+        pairs.append((i, x * 8 + (z + step) % 4 * 2 + (c ^ dc)))
     return pairs
+
+
+def back_perm(dz, dc):
+    return [(b, a) for a, b in z_perm(dz, dc)]
 
 
 def xor_perm(bits):
@@ -45,7 +54,8 @@
 def dest_head(e, dz, dc):
     z = e // 2
     c = e - 2 * z
-    return lax.rem(z + dz, 4) * 2 + (c if dc == 0 else 1 - c)
+    cd = c if dc == 0 else 1 - c
+    return lax.rem(z + dz + cd * (4 - 2 * dz), 4) * 2 + cd
 
 
 def dot_nn(a, b):
@@ -91,28 +101,25 @@
     )
 
 
-def pack_kernel(offs, k, v, q, d, *rest):
-    outs, info, tmp = rest[:8], rest[8], rest[9]
+def pack_kernel(k, v, q, d, *rest):
+    outs, tmp = rest[:8], rest[8]
     e = lax.rem(lax.axis_index("seq"), 8)
     order = row_order(False)
-    for level in range(LEVELS):
-        info[level] = offs[level, e]
-    info[4] = e
     for a, ref in enumerate((k, v, q, d)):
         tmp[...] = dot_nn(order, ref[...]).astype(BF16)
         for slot, (dz, dc) in enumerate(SLOTS):
             outs[slot][a] = tmp[:, head_at(dest_head(e, dz, dc))]
 
 
-def pack(offs, k, v, q, d):
+def pack(k, v, q, d):
     return pl.pallas_call(
         pack_kernel,
-        out_shape=[shape(BF16, 4, ROWS, HD)] * 8 + [shape(I32, 8)],
-        in_specs=[SM] + [VM] * 4,
-        out_specs=[VM] * 8 + [SM],
+        out_shape=[shape(BF16, 4, ROWS, HD)] * 8,
+        in_specs=[VM] * 4,
+        out_specs=[VM] * 8,
         scratch_shapes=[pltpu.VMEM((ROWS, H * HD), BF16)],
         compiler_params=pltpu.CompilerParams(vmem_limit_bytes=BIG),
-    )(offs, k, v, q, d)
+    )(k, v, q, d)
 
 
 def by_slot(refs):
@@ -123,17 +130,24 @@
     return [got[slot] for slot in [0] + SEND]
 
 
-def pick_kernel(info, *refs):
-    got, out = by_slot(refs[:8]), refs[8]
-    rows = tile_at(info[3] * TILE)
+def pick_kernel(offs, *refs):
+    got, out, info = by_slot(refs[:8]), refs[8], refs[9]
+    e = lax.rem(lax.axis_index("seq"), 8)
+    for level in range(LEVELS):
+        info[level] = offs[level, e]
+    info[4] = e
+    rows = tile_at(offs[3, e] * TILE)
     for s in range(8):
         out[:, s * TILE : (s + 1) * TILE] = got[s][0:2, rows]
 
 
-def pick3(info, got):
-    return call(pick_kernel, shape(BF16, 2, ROWS, HD), [SM] + [VM] * 8, VM)(
-        info, *in_order(got)
-    )
+def pick3(offs, got):
+    return call(
+        pick_kernel,
+        [shape(BF16, 2, ROWS, HD), shape(I32, 8)],
+        [SM] + [VM] * 8,
+        [VM, SM],
+    )(offs, *in_order(got))
 
 
 def join(pieces):
@@ -152,7 +166,7 @@
 
 
 def segments(e):
-    mate = jnp.where(lax.rem(e // 2, 2) == 0, 3, 1)
+    mate = jnp.where(lax.rem(e // 2 + e, 2) == 0, 3, 1)
     near = pl.multiple_of(BASE[1] + mate * 128, 128)
     far = pl.multiple_of(BASE[1] + (4 - mate) * 128, 128)
     segs = [(0, [(m * 256, 256)]) for m in range(4)]
@@ -292,8 +306,13 @@
         acc3[0] = dot_nn(ds, k3) * SCALE
         for n, value in ((1, dot_tn(ds, q3) * SCALE), (2, dot_tn(p3.astype(BF16), do))):
             acc3[n] = value[:ROWS]
-            xout[n - 1] = value[ROWS:].astype(BF16)
+            xout[(n - 1) * ROWS : n * ROWS] = value[ROWS:].astype(BF16)
     bias_out[...] = biases
+    high = biases.astype(BF16).astype(F32)
+    middle = (biases - high).astype(BF16).astype(F32)
+    row = lax.broadcasted_iota(I32, (TILE, 128), 0)
+    terms = jnp.where(row == 0, high, jnp.where(row == 1, middle, biases - high - middle))
+    xout[2 * ROWS :] = jnp.where(row < 3, terms, 0.0).astype(BF16)
 
 
 def mixing(info, bias, comp, o, z, xkv):
@@ -304,7 +323,7 @@
             shape(BF16, BASE[3], HD),
             shape(F32, BASE[3], HD),
             shape(F32, 3, ROWS, HD),
-            shape(BF16, 2, ROWS, HD),
+            shape(BF16, 2 * ROWS + TILE, HD),
             shape(F32, 1, 128),
         ],
         [SM, SM] + [VM] * 4,
@@ -319,7 +338,7 @@
 
 
 def bwd_kernel(info, comp, p_s, do_s, c_s, acc3, att, *refs):
-    msgs, own3, acc = refs[:8], refs[8], refs[9]
+    own, zs, core, own3, acc = refs[0], refs[1:4], refs[4], refs[5], refs[6]
     offs = [info[level] for level in range(LEVELS)]
     for level, parts in segments(info[4]):
         q, k, v = (load(comp.at[a], parts) for a in (2, 0, 1))
@@ -348,101 +367,157 @@
             acc[which, at] = total
             if which > 0:
                 own3[which - 1, part] = total
-    for s in range(8):
-        msgs[s][0] = att[s]
+    for s, (dz, dc) in enumerate(SLOTS):
+        home = core.at[dz] if dc else (zs[dz - 1].at[0] if dz else own)
+        home[0] = att[s]
         for which in range(3):
-            msgs[s][1 + which] = acc[which, s * ROWS : (s + 1) * ROWS].astype(BF16)
-
-
-MSG = shape(BF16, 4, ROWS, HD)
+            home[1 + which] = acc[which, s * ROWS : (s + 1) * ROWS].astype(BF16)
+
+
+MSGS = [shape(BF16, 4, ROWS, HD)] + [shape(BF16, 2, 4, ROWS, HD)] * 3
+CORES = shape(BF16, 4, 4, ROWS, HD)
 
 
 def backward(info, comp, p, do, c, acc3, att):
     return call(
         bwd_kernel,
-        [MSG] * 8 + [shape(F32, 2, ROWS, HD)],
+        MSGS + [CORES, shape(F32, 2, ROWS, HD)],
         [SM] + [VM] * 6,
-        [VM] * 9,
+        [VM] * 6,
         [pltpu.VMEM((3, 1024, HD), F32)],
         cost=pl.CostEstimate(flops=600000000, bytes_accessed=6000000, transcendentals=0),
     )(info, comp, p, do, c, acc3, att)
 
 
-def merge_kernel(info, *refs):
-    own3, xin, bias = refs[8:11]
-    outs, spread = refs[11:19], refs[19]
-    for s in range(8):
-        at = slice(s * TILE, (s + 1) * TILE)
-        outs[s][...] = (own3[:, at] + xin[:, at].astype(F32)).astype(BF16)
-    spread[...] = jnp.broadcast_to(bias[:, : LEVELS * H], spread.shape)
-
-
-def merge(info, msgs, own3, xin, bias, devices):
-    tile = pl.BlockSpec((2, TILE, HD), lambda i, info: (1, info[3], 0))
-
-    def full(*dims):
-        return pl.BlockSpec(dims, lambda i, info: (0,) * len(dims))
-
-    rows = full(2, ROWS, HD)
+def full(*dims):
+    return pl.BlockSpec(dims, lambda i, info: (0,) * len(dims))
+
+
+def patch(kernel, outs, blocks, ins, in_blocks, info):
+    count = len(blocks)
     return pl.pallas_call(
-        merge_kernel,
-        out_shape=[MSG] * 8 + [shape(F32, devices, LEVELS * H)],
+        kernel,
+        out_shape=outs,
         grid_spec=pltpu.PrefetchScalarGridSpec(
             num_scalar_prefetch=1,
             grid=(1,),
-            in_specs=[pl.BlockSpec(memory_space=pl.ANY)] * 8 + [rows, rows, full(1, 128)],
-            out_specs=[tile] * 8 + [full(devices, LEVELS * H)],
+            in_specs=[pl.BlockSpec(memory_space=pl.ANY)] * count + in_blocks,
+            out_specs=blocks + [full(*x.shape) for x in outs[count:]],
         ),
-        input_output_aliases={1 + n: n for n in range(8)},
+        input_output_aliases={1 + n: n for n in range(count)},
         compiler_params=PARAMS,
-    )(info, *msgs, own3, xin, bias)
+    )(info, *ins)
+
+
+def merge_kernel(info, *refs):
+    own3, xin, bias = refs[5:8]
+    own, zs, core, bias_out = refs[8], refs[9:12], refs[12], refs[13]
+    terms = jnp.sum(xin[2 * ROWS :].astype(F32), axis=0, keepdims=True)
+    bias_out[...] = bias[...] + terms
+    for s, (dz, dc) in enumerate(SLOTS):
+        at = slice(s * TILE, (s + 1) * TILE)
+        for a in range(2):
+            theirs = xin[a * ROWS + s * TILE : a * ROWS + (s + 1) * TILE]
+            total = (own3[a, at] + theirs.astype(F32)).astype(BF16)
+            if dc:
+                core[dz, a] = total
+            elif dz:
+                zs[dz - 1][0, a] = total
+            else:
+                own[a] = total
+
+
+def merge(info, msgs, own3, xin, bias):
+    one = pl.BlockSpec((2, TILE, HD), lambda i, info: (1, info[3], 0))
+    two = pl.BlockSpec((1, 2, TILE, HD), lambda i, info: (0, 1, info[3], 0))
+    four = pl.BlockSpec((4, 2, TILE, HD), lambda i, info: (0, 1, info[3], 0))
+    return patch(
+        merge_kernel,
+        MSGS + [CORES, shape(F32, 1, 128)],
+        [one, two, two, two, four],
+        [*msgs, own3, xin, bias],
+        [full(2, ROWS, HD), full(2 * ROWS + TILE, HD), full(1, 128)],
+        info,
+    )
+
+
+def relay_kernel(info, *refs):
+    core, bias = refs[3], refs[4]
+    zs, spread = refs[5:8], refs[8]
+    for dz in range(1, 4):
+        zs[dz - 1][0] = core[4 - dz]
+    spread[...] = jnp.broadcast_to(bias[:, : LEVELS * H], spread.shape)
+
+
+def relay(info, msgs, core, bias, devices):
+    half = pl.BlockSpec((1, 4, ROWS, HD), lambda i, info: (1, 0, 0, 0))
+    return patch(
+        relay_kernel,
+        MSGS[1:] + [shape(F32, devices, LEVELS * H)],
+        [half] * 3,
+        [*msgs, core, bias],
+        [full(*CORES.shape), full(1, 128)],
+        info,
+    )
 
 
 def unpack_kernel(info, *refs):
-    got, bias = by_slot(refs[:8]), refs[8]
-    outs, bias_out = refs[9:13], refs[13]
+    own, core = refs[0], refs[4]
+    zs = [refs[1], refs[3], refs[2]]
+    outs = refs[5:9]
     e = info[4]
     order = row_order(True)
     for a in range(4):
-        for slot, (dz, dc) in enumerate(SLOTS):
+        for dz, dc in SLOTS:
+            home = zs[3 - dz if dc else dz - 1].at[dc] if dz else (core.at[0] if dc else own)
             at = head_at(dest_head(e, dz, dc))
-            outs[a][:, at] = dot_nn(order, got[slot][a]).astype(BF16)
+            outs[a][:, at] = dot_nn(order, home[a]).astype(BF16)
+
+
+def total_kernel(bias, out):
     total = jnp.sum(bias[...], axis=0, keepdims=True)
     for level in range(LEVELS):
-        bias_out[level : level + 1] = total[:, level * H : (level + 1) * H]
-
-
-def unpack(info, got, bias):
+        out[level : level + 1] = total[:, level * H : (level + 1) * H]
+
+
+def bias_total(bias):
+    return call(total_kernel, shape(F32, LEVELS, H), [VM], VM)(bias)
+
+
+def unpack(info, own, zs, core):
     return call(
         unpack_kernel,
-        [shape(BF16, ROWS, H * HD)] * 4 + [shape(F32, LEVELS, H)],
-        [SM] + [VM] * 9,
-        [VM] * 5,
-    )(info, *in_order(got), bias)
+        [shape(BF16, ROWS, H * HD)] * 4,
+        [SM] + [VM] * 5,
+        [VM] * 4,
+        cost=SHADOW,
+    )(info, own, zs[0], zs[2], zs[1], core)
 
 
 def local(queries, keys, values, cotangent, head_offsets, level_bias):
     def move(x, pairs):
         return lax.ppermute(x, "seq", pairs)
 
-    packed = pack(head_offsets, keys, values, queries, cotangent)
-    sent, info = packed[:8], packed[8]
+    sent = pack(keys, values, queries, cotangent)
     got = [sent[0]] + [None] * 7
     for slot in SEND:
         got[slot] = move(sent[slot], z_perm(*SLOTS[slot]))
-    xkv = move(pick3(info, got), xor_perm(8))
+    picked, info = pick3(head_offsets, got)
+    xkv = move(picked, xor_perm(8))
     comp, p, o, z = forward(info, got)
     att, do, c, acc3, xout, bias = mixing(info, level_bias, comp, o, z, xkv)
     xin = move(xout, xor_perm(8))
     *msgs, own3 = backward(info, comp, p, do, c, acc3, att)
-    devices = lax.axis_size("grp") * lax.axis_size("seq")
-    *msgs, spread = merge(info, msgs, own3, xin, bias, devices)
-    back = [msgs[0]] + [None] * 7
-    for slot in SEND:
-        dz, dc = SLOTS[slot]
-        back[slot] = move(msgs[slot], z_perm(-dz, dc))
-    bias = lax.all_to_all(spread, ("grp", "seq"), 0, 0, tiled=True)
-    return tuple(unpack(info, back, bias))
+    own, *zs, core, bias = merge(info, msgs, own3, xin, bias)
+    core = move(core, xor_perm(1))
+    *zs, spread = relay(info, zs, core, bias, 128)
+    zs = [move(x, back_perm(dz, 0)) for dz, x in zip((1, 2, 3), zs)]
+    bias = lax.all_to_all(
+        spread, ("grp", "seq"), 0, 0, axis_index_groups=GROUPS, tiled=True
+    )
+    outs = unpack(info, own, zs, core)
+    outs, bias = lax.optimization_barrier((outs, bias))
+    return (*outs, bias_total(bias))
 
 
 def solution(mesh):

time: 91.5 us -> 87.9 us (0.961)
  blocking collectives: 26.8 us -> 0 us
  waiting for transfers between devices: 6.97 us -> 25.6 us
  starting transfers between devices: 42.3 us -> 45.4 us
  Pallas kernels: 13 us -> 15.2 us
    all_to_all x1 -> x0, blocking collectives: 26.8 us -> none  [local(): bias = lax.all_to_all(spread, ('grp', 'seq'), 0, 0, tiled=True)]
    ppermute x16 -> x13, waiting for transfers between devices: 6.97 us -> 21 us  [move(): return lax.ppermute(x, 'seq', pairs)]
    all_to_all x0 -> x1, starting transfers between devices: none -> 12.7 us  [local(): lax.all_to_all(spread, ('grp', 'seq'), 0, 0, axis_index_groups=GROUPS, ti...]
    ppermute x16 -> x13, starting transfers between devices: 42.3 us -> 32.8 us  [move(): return lax.ppermute(x, 'seq', pairs)]
    all_to_all x0 -> x1, waiting for transfers between devices: none -> 4.63 us  [local(): lax.all_to_all(spread, ('grp', 'seq'), 0, 0, axis_index_groups=GROUPS, ti...]
    pallas_call x5 -> x7, Pallas kernels: 8.58 us -> 10.8 us  [the longest x1 2.9 us: backward(): call(bwd_kernel, MSGS + [CORES, shape(F32, 2, ROWS, HD)], [SM] + [VM] * 6...]
  transfers between devices with their start and end apart: 16 -> 14, of which waited for: 4 -> 6; matrix products, arithmetic and copies ran while one was open for 0% -> 0% of each run, Pallas kernels for 6% -> 8%
where the time goes in v2:
time: 87.9 us; the launch traced here: 87.7 us
  starting transfers between devices  45.4 us (52%)
  waiting for transfers between devices  25.6 us (29%)
  Pallas kernels  15.2 us (17%)
    ppermute x13, starting transfers between devices, move(): return lax.ppermute(x, 'seq', pairs)  32.8 us
    ppermute x13, waiting for transfers between devices, move(): return lax.ppermute(x, 'seq', pairs)  21 us
    all_to_all x1, starting transfers between devices, local(): lax.all_to_all(spread, ('grp', 'seq'), 0, 0, axis_index_groups=GROUPS, ti...  12.7 us
    all_to_all x1, waiting for transfers between devices, local(): lax.all_to_all(spread, ('grp', 'seq'), 0, 0, axis_index_groups=GROUPS, ti...  4.63 us
    pallas_call x1, Pallas kernels, backward(): call(bwd_kernel, MSGS + [CORES, shape(F32, 2, ROWS, HD)], [SM] + [VM] * 6...  2.9 us
    pallas_call x1, Pallas kernels, pack(): pl.pallas_call(pack_kernel, out_shape=[shape(BF16, 4, ROWS, HD)] * 8, in_...  2.46 us
    pallas_call x1, Pallas kernels, mixing(): call(mix_kernel, [shape(BF16, 8, ROWS, HD), shape(BF16, BASE[3], HD), sha...  2.29 us
    pallas_call x1, Pallas kernels, forward(): call(fwd_kernel, [shape(BF16, 4, COMPACT, HD), shape(F32, BASE[3], 256),...  2.15 us
  transfers between devices with their start and end apart: 14, of which 6 were waited for; matrix products, arithmetic and copies ran while one was open for 0% of the time, Pallas kernels for 8%

profile of v2, /device:TPU:1, one launch (start us, length us, event | category | flops | bytes accessed | tf_op | source)
XLA Modules:
  0.0 87.7 jit_solution(17112087976962019705)
XLA Ops:
  0.6 0.0 copy-start
  0.6 2.5 %shard_map.101 = (bf16[4,128,128]{2,1,0:T(8,128)(2,1)S(1)}, bf16[4,128,128]{2,1,0:T(8,128)(2,1)S(1)}, bf16[4,128,128]{2,1,0:T(8,128)(2,1)S(1)}, bf16[4,128,128]{...) custom-call(bf16[128,1024]{1,0:T(8,128)(2,1)} %k.1, ...), custom_call_target="tpu_custom_call" | custom-call | tf_op jit(solution)/shard_map/pallas_call | solution.py:115
  3.1 3.2 %collective-permute-start = (bf16[4,128,128]{2,1,0:T(8,128)(2,1)S(1)}, bf16[4,128,128]{2,1,0:T(8,128)(2,1)S(1)}, u32[]{:S(2)}, u32[]{:S(2)}) collective-permute-start(bf16[4,128,128]{2,1,0:T(8,128)(2,1)S(1)} %get-tuple-element.51), channel_id=1, source_target_pairs={{0,1},{1,0},{2,3},{3,2},{4,5},{5,4},{6,7},{7,6},{8,9},{9,8},{10,11... | collective-permute-start | bytes 393224 | tf_op jit(solution)/shard_map/ppermute | solution.py:499
  6.3 4.3 %collective-permute-start.1 = (bf16[4,128,128]{2,1,0:T(8,128)(2,1)S(1)}, bf16[4,128,128]{2,1,0:T(8,128)(2,1)S(1)}, u32[]{:S(2)}, u32[]{:S(2)}) collective-permute-start(bf16[4,128,128]{2,1,0:T(8,128)(2,1)S(1)} %get-tuple-element.52), channel_id=1, source_target_pairs={{0,2},{1,7},{2,4},{3,1},{4,6},{5,3},{6,0},{7,5},{8,10},{9,15},{10,... | collective-permute-start | bytes 393224 | tf_op jit(solution)/shard_map/ppermute | solution.py:499
  10.6 0.0 collective-permute-start.2
  10.6 1.3 %collective-permute-start.3 = (bf16[4,128,128]{2,1,0:T(8,128)(2,1)S(1)}, bf16[4,128,128]{2,1,0:T(8,128)(2,1)S(1)}, u32[]{:S(2)}, u32[]{:S(2)}) collective-permute-start(bf16[4,128,128]{2,1,0:T(8,128)(2,1)S(1)} %get-tuple-element.54), channel_id=1, source_target_pairs={{0,7},{1,2},{2,1},{3,4},{4,3},{5,6},{6,5},{7,0},{8,15},{9,10},{10,... | collective-permute-start | bytes 393224 | tf_op jit(solution)/shard_map/ppermute | solution.py:499
  12.0 2.5 %collective-permute-start.4 = (bf16[4,128,128]{2,1,0:T(8,128)(2,1)}, bf16[4,128,128]{2,1,0:T(8,128)(2,1)S(1)}, u32[]{:S(2)}, u32[]{:S(2)}) collective-permute-start(bf16[4,128,128]{2,1,0:T(8,128)(2,1)} %get-tuple-element.55), channel_id=1, source_target_pairs={{0,3},{1,6},{2,5},{3,0},{4,7},{5,2},{6,1},{7,4},{8,11},{9,14},{10,... | collective-permute-start | bytes 393224 | tf_op jit(solution)/shard_map/ppermute | solution.py:499
  14.4 0.0 collective-permute-done.refs_1_
  14.4 2.1 %collective-permute-start.5 = (bf16[4,128,128]{2,1,0:T(8,128)(2,1)S(1)}, bf16[4,128,128]{2,1,0:T(8,128)(2,1)S(1)}, u32[]{:S(2)}, u32[]{:S(2)}) collective-permute-start(bf16[4,128,128]{2,1,0:T(8,128)(2,1)S(1)} %get-tuple-element.56), channel_id=1, source_target_pairs={{0,4},{1,5},{2,6},{3,7},{4,0},{5,1},{6,2},{7,3},{8,12},{9,13},{10,... | collective-permute-start | bytes 393224 | tf_op jit(solution)/shard_map/ppermute | solution.py:499
  16.6 0.2 collective-permute-done.1.refs_2_
  16.8 6.8 %collective-permute-start.6 = (bf16[4,128,128]{2,1,0:T(8,128)(2,1)S(1)}, bf16[4,128,128]{2,1,0:T(8,128)(2,1)S(1)}, u32[]{:S(2)}, u32[]{:S(2)}) collective-permute-start(bf16[4,128,128]{2,1,0:T(8,128)(2,1)S(1)} %get-tuple-element.57), channel_id=1, source_target_pairs={{0,5},{1,4},{2,7},{3,6},{4,1},{5,0},{6,3},{7,2},{8,13},{9,12},{10,... | collective-permute-start | bytes 393224 | tf_op jit(solution)/shard_map/ppermute | solution.py:499
  23.6 0.0 collective-permute-done.2.refs_3_
  23.6 0.0 collective-permute-done.3.refs_4_
  23.6 9.5 %collective-permute-done.4.refs_5_ = bf16[4,128,128]{2,1,0:T(8,128)(2,1)S(1)} collective-permute-done((bf16[4,128,128]{2,1,0:T(8,128)(2,1)}, bf16[4,128,128]{2,1,0:T(8,128)(2,1)S(1)}, u32[]{:S(2)}, u32[]{:S(2)}) %collective-permute-start.4) | collective-permute-done | bytes 131104 | tf_op jit(solution)/shard_map/ppermute | solution.py:499
  33.1 0.0 collective-permute-done.5.refs_6_
  33.1 0.0 collective-permute-done.6.refs_7_
  33.1 0.0 copy-start.1
  33.1 0.7 copy-done.1
  33.8 1.2 %shard_map.102 = (bf16[2,128,128]{2,1,0:T(8,128)(2,1)S(1)}, s32[8]{0:T(128)S(1)}) custom-call(s32[4,8]{1,0:T(4,128)S(1)} %copy-done.1, bf16[4,128,128]{2,1,0:T(8,128)(2,1)S(1)} %get-tuple-element.50.refs_0_, bf16[4,128,128]{2,1,0:T(8,128)(2,1)S(1)} %collective-permute-done.refs_1_, bf16[4,128,128]{2,1,0:T(8,128)(2,1)S(1)} %collective-permute-done.1.refs_2_, ...), custom_call_target="tpu_custom_call" | custom-call | tf_op jit(solution)/shard_map/pallas_call | solution.py:145
  35.0 1.3 %collective-permute-start.7 = (bf16[2,128,128]{2,1,0:T(8,128)(2,1)S(1)}, bf16[2,128,128]{2,1,0:T(8,128)(2,1)S(1)}, u32[]{:S(2)}, u32[]{:S(2)}) collective-permute-start(bf16[2,128,128]{2,1,0:T(8,128)(2,1)S(1)} %get-tuple-element.63), channel_id=1, source_target_pairs={{0,8},{1,9},{2,10},{3,11},{4,12},{5,13},{6,14},{7,15},{8,0},{9,1},... | collective-permute-start | bytes 196616 | tf_op jit(solution)/shard_map/ppermute | solution.py:499
  36.3 2.2 %shard_map.103 = (bf16[4,1920,128]{2,1,0:T(8,128)(2,1)S(1)}, f32[1792,256]{1,0:T(8,128)S(1)}, f32[1792,128]{1,0:T(8,128)S(1)}, f32[1792,128]{1,0:T(8,128)S(1)}) custom-call(s32[8]{0:T(128)S(1)} %get-tuple-element.58.info, bf16[4,128,128]{2,1,0:T(8,128)(2,1)S(1)} %get-tuple-element.50.refs_0_, bf16[4,128,128]{2,1,0:T(8,128)(2,1)S(1)} %collective-permute-done.refs_1_, ...), custom_call_target="tpu_custom_call" | custom-call | flops 250000000 | bytes 6000000 | tf_op jit(solution)/shard_map/pallas_call | solution.py:225
  38.5 0.0 collective-permute-done.7.xkv
  38.5 0.0 copy-done
  38.5 2.3 %shard_map.104 = (bf16[8,128,128]{2,1,0:T(8,128)(2,1)S(1)}, bf16[1792,128]{1,0:T(8,128)(2,1)S(1)}, f32[1792,128]{1,0:T(8,128)S(1)}, f32[3,128,128]{2,1,0:T(8,128...) custom-call(s32[8]{0:T(128)S(1)} %get-tuple-element.58.info, f32[4,8]{1,0:T(4,128)S(1)} %copy-done, ...), custom_call_target="tpu_custom_call" | custom-call | flops 50000000 | bytes 6000000 | tf_op jit(solution)/shard_map/pallas_call | solution.py:319
  40.8 1.0 %collective-permute-start.8 = (bf16[272,128]{1,0:T(8,128)(2,1)S(1)}, bf16[272,128]{1,0:T(8,128)(2,1)S(1)}, u32[]{:S(2)}, u32[]{:S(2)}) collective-permute-start(bf16[272,128]{1,0:T(8,128)(2,1)S(1)} %get-tuple-element.74), channel_id=1, source_target_pairs={{0,8},{1,9},{2,10},{3,11},{4,12},{5,13},{6,14},{7,15},{8,0},{9,1},... | collective-permute-start | bytes 208904 | tf_op jit(solution)/shard_map/ppermute | solution.py:499
  41.8 2.9 %shard_map.105 = (bf16[4,128,128]{2,1,0:T(8,128)(2,1)S(1)}, bf16[2,4,128,128]{3,2,1,0:T(8,128)(2,1)S(1)}, bf16[2,4,128,128]{3,2,1,0:T(8,128)(2,1)S(1)}, bf16[2,4...) custom-call(s32[8]{0:T(128)S(1)} %get-tuple-element.58.info, ...), custom_call_target="tpu_custom_call" | custom-call | flops 600000000 | bytes 6000000 | tf_op jit(solution)/shard_map/pallas_call | solution.py:382
  44.7 0.0 collective-permute-done.8.refs_6_
  44.7 0.6 shard_map.106
  45.3 2.4 %collective-permute-start.9 = (bf16[4,4,128,128]{3,2,1,0:T(8,128)(2,1)S(1)}, bf16[4,4,128,128]{3,2,1,0:T(8,128)(2,1)S(1)}, u32[]{:S(2)}, u32[]{:S(2)}) collective-permute-start(bf16[4,4,128,128]{3,2,1,0:T(8,128)(2,1)S(1)} %get-tuple-element.80), channel_id=1, source_target_pairs={{0,1},{1,0},{2,3},{3,2},{4,5},{5,4},{6,7},{7,6},{8,9},{9,8},{10,11... | collective-permute-start | bytes 1572872 | tf_op jit(solution)/shard_map/ppermute | solution.py:499
  47.7 1.5 %collective-permute-done.9.refs_3_.refs_4_ = bf16[4,4,128,128]{3,2,1,0:T(8,128)(2,1)S(1)} collective-permute-done((bf16[4,4,128,128]{3,2,1,0:T(8,128)(2,1)S(1)}, bf16[4,4,128,128]{3,2,1,0:T(8,128)(2,1)S(1)}, u32[]{:S(2)}, u32[]{:S(2)}) %collective-permute-start.9) | collective-permute-done | bytes 524320 | tf_op jit(solution)/shard_map/ppermute | solution.py:499
  49.3 1.2 %shard_map.107 = (bf16[2,4,128,128]{3,2,1,0:T(8,128)(2,1)S(1)}, bf16[2,4,128,128]{3,2,1,0:T(8,128)(2,1)S(1)}, bf16[2,4,128,128]{3,2,1,0:T(8,128)(2,1)S(1)}, f32[128,32]{1,0:T(8,128)}) custom-call(s32[8]{0:T(128)S(1)} %get-tuple-element.58.info, ...), custom_call_target="tpu_custom_call", output_to_operand_aliasing={{0}: (1, {}), {1}: (2, {}), {2}: (3, {})} | custom-call | tf_op jit(solution)/shard_map/pallas_call | solution.py:398
  50.4 4.4 %collective-permute-start.10 = (bf16[2,4,128,128]{3,2,1,0:T(8,128)(2,1)S(1)}, bf16[2,4,128,128]{3,2,1,0:T(8,128)(2,1)S(1)}, u32[]{:S(2)}, u32[]{:S(2)}) collective-permute-start(bf16[2,4,128,128]{3,2,1,0:T(8,128)(2,1)S(1)} %get-tuple-element.82), channel_id=1, source_target_pairs={{2,0},{7,1},{4,2},{1,3},{6,4},{3,5},{0,6},{5,7},{10,8},{15,9},{12,... | collective-permute-start | bytes 786440 | tf_op jit(solution)/shard_map/ppermute | solution.py:499
  54.9 0.4 collective-permute-start.11
  55.3 2.8 %collective-permute-start.12 = (bf16[2,4,128,128]{3,2,1,0:T(8,128)(2,1)S(1)}, bf16[2,4,128,128]{3,2,1,0:T(8,128)(2,1)S(1)}, u32[]{:S(2)}, u32[]{:S(2)}) collective-permute-start(bf16[2,4,128,128]{3,2,1,0:T(8,128)(2,1)S(1)} %get-tuple-element.84), channel_id=1, source_target_pairs={{4,0},{5,1},{6,2},{7,3},{0,4},{1,5},{2,6},{3,7},{12,8},{13,9},{14,... | collective-permute-start | bytes 786440 | tf_op jit(solution)/shard_map/ppermute | solution.py:499
  58.2 12.7 %all-to-all-start = ((f32[128,1,32]{2,1,0:T(1,128)}), f32[128,1,32]{2,1,0:T(1,128)S(1)}, u32[]{:S(2)}, u32[]{:S(2)}) async-start(f32[128,1,32]{2,1,0:T(1,128)} %bitcast.1), calls=%async_computation | async-start | bytes 131072 | tf_op jit(solution)/shard_map/all_to_all | solution.py:515
  70.9 0.0 collective-permute-done.10.refs_1_
  70.9 1.6 %collective-permute-done.11.refs_2_ = bf16[2,4,128,128]{3,2,1,0:T(8,128)(2,1)S(1)} collective-permute-done((bf16[2,4,128,128]{3,2,1,0:T(8,128)(2,1)S(1)}, bf16[2,4,128,128]{3,2,1,0:T(8,128)(2,1)S(1)}, u32[]{:S(2)}, u32[]{:S(2)}) %collective-permute-start.11) | collective-permute-done | bytes 262176 | tf_op jit(solution)/shard_map/ppermute | solution.py:499
  72.5 8.1 %collective-permute-done.12.refs_3_ = bf16[2,4,128,128]{3,2,1,0:T(8,128)(2,1)S(1)} collective-permute-done((bf16[2,4,128,128]{3,2,1,0:T(8,128)(2,1)S(1)}, bf16[2,4,128,128]{3,2,1,0:T(8,128)(2,1)S(1)}, u32[]{:S(2)}, u32[]{:S(2)}) %collective-permute-start.12) | collective-permute-done | bytes 262176 | tf_op jit(solution)/shard_map/ppermute | solution.py:499
  80.6 1.8 %shard_map.108 = (bf16[128,1024]{1,0:T(8,128)(2,1)}, bf16[128,1024]{1,0:T(8,128)(2,1)}, bf16[128,1024]{1,0:T(8,128)(2,1)}, bf16[128,1024]{1,0:T(8,128)(2,1)}) custom-call(s32[8]{0:T(128)S(1)} %get-tuple-element.58.info, bf16[4,128,128]{2,1,0:T(8,128)(2,1)S(1)} %get-tuple-element.76.refs_0_, bf16[2,4,128,128]{3,2,1,0:T(8,128)(2,1)S(1)} %collective-permute-done.10.refs_1_, ...), custom_call_target="tpu_custom_call" | custom-call | bytes 200000000 | tf_op jit(solution)/shard_map/pallas_call | solution.py:488
  82.4 4.6 %all-to-all-done = f32[128,1,32]{2,1,0:T(1,128)S(1)} async-done(((f32[128,1,32]{2,1,0:T(1,128)}), f32[128,1,32]{2,1,0:T(1,128)S(1)}, u32[]{:S(2)}, u32[]{:S(2)}) %all-to-all-start) | async-done | bytes 16416 | tf_op jit(solution)/shard_map/all_to_all | solution.py:515
  87.0 0.7 shard_map.109
Async XLA Ops:
  0.6 37.8 %copy-start = (f32[4,8]{1,0:T(4,128)S(1)}, f32[4,8]{1,0:T(4,128)}, u32[]{:S(2)}) copy-start(f32[4,8]{1,0:T(4,128)} %bias.1) | copy-start | bytes 388
  3.1 11.3 %collective-permute-start = (bf16[4,128,128]{2,1,0:T(8,128)(2,1)S(1)}, bf16[4,128,128]{2,1,0:T(8,128)(2,1)S(1)}, u32[]{:S(2)}, u32[]{:S(2)}) collective-permute-start(bf16[4,128,128]{2,1,0:T(8,128)(2,1)S(1)} %get-tuple-element.51), channel_id=1, source_target_pairs={{0,1},{1,0},{2,3},{3,2},{4,5},{5,4},{6,7},{7,6},{8,9},{9,8},{10,11... | collective-permute-start | bytes 393224 | tf_op jit(solution)/shard_map/ppermute | solution.py:499
  6.3 10.4 %collective-permute-start.1 = (bf16[4,128,128]{2,1,0:T(8,128)(2,1)S(1)}, bf16[4,128,128]{2,1,0:T(8,128)(2,1)S(1)}, u32[]{:S(2)}, u32[]{:S(2)}) collective-permute-start(bf16[4,128,128]{2,1,0:T(8,128)(2,1)S(1)} %get-tuple-element.52), channel_id=1, source_target_pairs={{0,2},{1,7},{2,4},{3,1},{4,6},{5,3},{6,0},{7,5},{8,10},{9,15},{10,... | collective-permute-start | bytes 393224 | tf_op jit(solution)/shard_map/ppermute | solution.py:499
  10.6 13.0 %collective-permute-start.2 = (bf16[4,128,128]{2,1,0:T(8,128)(2,1)S(1)}, bf16[4,128,128]{2,1,0:T(8,128)(2,1)S(1)}, u32[]{:S(2)}, u32[]{:S(2)}) collective-permute-start(bf16[4,128,128]{2,1,0:T(8,128)(2,1)S(1)} %get-tuple-element.53), channel_id=1, source_target_pairs={{0,6},{1,3},{2,0},{3,5},{4,2},{5,7},{6,4},{7,1},{8,14},{9,11},{10,... | collective-permute-start | bytes 393224 | tf_op jit(solution)/shard_map/ppermute | solution.py:499
  10.6 13.0 %collective-permute-start.3 = (bf16[4,128,128]{2,1,0:T(8,128)(2,1)S(1)}, bf16[4,128,128]{2,1,0:T(8,128)(2,1)S(1)}, u32[]{:S(2)}, u32[]{:S(2)}) collective-permute-start(bf16[4,128,128]{2,1,0:T(8,128)(2,1)S(1)} %get-tuple-element.54), channel_id=1, source_target_pairs={{0,7},{1,2},{2,1},{3,4},{4,3},{5,6},{6,5},{7,0},{8,15},{9,10},{10,... | collective-permute-start | bytes 393224 | tf_op jit(solution)/shard_map/ppermute | solution.py:499
  12.0 21.2 %collective-permute-start.4 = (bf16[4,128,128]{2,1,0:T(8,128)(2,1)}, bf16[4,128,128]{2,1,0:T(8,128)(2,1)S(1)}, u32[]{:S(2)}, u32[]{:S(2)}) collective-permute-start(bf16[4,128,128]{2,1,0:T(8,128)(2,1)} %get-tuple-element.55), channel_id=1, source_target_pairs={{0,3},{1,6},{2,5},{3,0},{4,7},{5,2},{6,1},{7,4},{8,11},{9,14},{10,... | collective-permute-start | bytes 393224 | tf_op jit(solution)/shard_map/ppermute | solution.py:499
  14.4 18.7 %collective-permute-start.5 = (bf16[4,128,128]{2,1,0:T(8,128)(2,1)S(1)}, bf16[4,128,128]{2,1,0:T(8,128)(2,1)S(1)}, u32[]{:S(2)}, u32[]{:S(2)}) collective-permute-start(bf16[4,128,128]{2,1,0:T(8,128)(2,1)S(1)} %get-tuple-element.56), channel_id=1, source_target_pairs={{0,4},{1,5},{2,6},{3,7},{4,0},{5,1},{6,2},{7,3},{8,12},{9,13},{10,... | collective-permute-start | bytes 393224 | tf_op jit(solution)/shard_map/ppermute | solution.py:499
  16.8 16.4 %collective-permute-start.6 = (bf16[4,128,128]{2,1,0:T(8,128)(2,1)S(1)}, bf16[4,128,128]{2,1,0:T(8,128)(2,1)S(1)}, u32[]{:S(2)}, u32[]{:S(2)}) collective-permute-start(bf16[4,128,128]{2,1,0:T(8,128)(2,1)S(1)} %get-tuple-element.57), channel_id=1, source_target_pairs={{0,5},{1,4},{2,7},{3,6},{4,1},{5,0},{6,3},{7,2},{8,13},{9,12},{10,... | collective-permute-start | bytes 393224 | tf_op jit(solution)/shard_map/ppermute | solution.py:499
  33.1 0.7 copy-start.1
  35.0 3.5 %collective-permute-start.7 = (bf16[2,128,128]{2,1,0:T(8,128)(2,1)S(1)}, bf16[2,128,128]{2,1,0:T(8,128)(2,1)S(1)}, u32[]{:S(2)}, u32[]{:S(2)}) collective-permute-start(bf16[2,128,128]{2,1,0:T(8,128)(2,1)S(1)} %get-tuple-element.63), channel_id=1, source_target_pairs={{0,8},{1,9},{2,10},{3,11},{4,12},{5,13},{6,14},{7,15},{8,0},{9,1},... | collective-permute-start | bytes 196616 | tf_op jit(solution)/shard_map/ppermute | solution.py:499
  40.8 3.9 %collective-permute-start.8 = (bf16[272,128]{1,0:T(8,128)(2,1)S(1)}, bf16[272,128]{1,0:T(8,128)(2,1)S(1)}, u32[]{:S(2)}, u32[]{:S(2)}) collective-permute-start(bf16[272,128]{1,0:T(8,128)(2,1)S(1)} %get-tuple-element.74), channel_id=1, source_target_pairs={{0,8},{1,9},{2,10},{3,11},{4,12},{5,13},{6,14},{7,15},{8,0},{9,1},... | collective-permute-start | bytes 208904 | tf_op jit(solution)/shard_map/ppermute | solution.py:499
  45.3 3.9 %collective-permute-start.9 = (bf16[4,4,128,128]{3,2,1,0:T(8,128)(2,1)S(1)}, bf16[4,4,128,128]{3,2,1,0:T(8,128)(2,1)S(1)}, u32[]{:S(2)}, u32[]{:S(2)}) collective-permute-start(bf16[4,4,128,128]{3,2,1,0:T(8,128)(2,1)S(1)} %get-tuple-element.80), channel_id=1, source_target_pairs={{0,1},{1,0},{2,3},{3,2},{4,5},{5,4},{6,7},{7,6},{8,9},{9,8},{10,11... | collective-permute-start | bytes 1572872 | tf_op jit(solution)/shard_map/ppermute | solution.py:499
  50.4 20.4 %collective-permute-start.10 = (bf16[2,4,128,128]{3,2,1,0:T(8,128)(2,1)S(1)}, bf16[2,4,128,128]{3,2,1,0:T(8,128)(2,1)S(1)}, u32[]{:S(2)}, u32[]{:S(2)}) collective-permute-start(bf16[2,4,128,128]{3,2,1,0:T(8,128)(2,1)S(1)} %get-tuple-element.82), channel_id=1, source_target_pairs={{2,0},{7,1},{4,2},{1,3},{6,4},{3,5},{0,6},{5,7},{10,8},{15,9},{12,... | collective-permute-start | bytes 786440 | tf_op jit(solution)/shard_map/ppermute | solution.py:499
  54.9 17.6 %collective-permute-start.11 = (bf16[2,4,128,128]{3,2,1,0:T(8,128)(2,1)S(1)}, bf16[2,4,128,128]{3,2,1,0:T(8,128)(2,1)S(1)}, u32[]{:S(2)}, u32[]{:S(2)}) collective-permute-start(bf16[2,4,128,128]{3,2,1,0:T(8,128)(2,1)S(1)} %get-tuple-element.83), channel_id=1, source_target_pairs={{6,0},{3,1},{0,2},{5,3},{2,4},{7,5},{4,6},{1,7},{14,8},{11,9},{8,1... | collective-permute-start | bytes 786440 | tf_op jit(solution)/shard_map/ppermute | solution.py:499
  55.3 25.2 %collective-permute-start.12 = (bf16[2,4,128,128]{3,2,1,0:T(8,128)(2,1)S(1)}, bf16[2,4,128,128]{3,2,1,0:T(8,128)(2,1)S(1)}, u32[]{:S(2)}, u32[]{:S(2)}) collective-permute-start(bf16[2,4,128,128]{3,2,1,0:T(8,128)(2,1)S(1)} %get-tuple-element.84), channel_id=1, source_target_pairs={{4,0},{5,1},{6,2},{7,3},{0,4},{1,5},{2,6},{3,7},{12,8},{13,9},{14,... | collective-permute-start | bytes 786440 | tf_op jit(solution)/shard_map/ppermute | solution.py:499
  58.2 28.8 %all-to-all-start = ((f32[128,1,32]{2,1,0:T(1,128)}), f32[128,1,32]{2,1,0:T(1,128)S(1)}, u32[]{:S(2)}, u32[]{:S(2)}) async-start(f32[128,1,32]{2,1,0:T(1,128)} %bitcast.1), calls=%async_computation | async-start | bytes 131072 | tf_op jit(solution)/shard_map/all_to_all | solution.py:515

commit v3 on v2

--- a/solution.py
+++ b/solution.py
@@ -101,25 +101,29 @@
     )
 
 
-def pack_kernel(k, v, q, d, *rest):
-    outs, tmp = rest[:8], rest[8]
+def pack_kernel(offs, k, v, q, d, *rest):
+    outs, info, tmp = rest[:8], rest[8], rest[9]
     e = lax.rem(lax.axis_index("seq"), 8)
     order = row_order(False)
+    for level in range(LEVELS):
+        info[level] = offs[level, e]
+    info[4] = e
+    info[5] = dest_head(e, 2, 0) // 2
     for a, ref in enumerate((k, v, q, d)):
         tmp[...] = dot_nn(order, ref[...]).astype(BF16)
         for slot, (dz, dc) in enumerate(SLOTS):
             outs[slot][a] = tmp[:, head_at(dest_head(e, dz, dc))]
 
 
-def pack(k, v, q, d):
+def pack(offs, k, v, q, d):
     return pl.pallas_call(
         pack_kernel,
-        out_shape=[shape(BF16, 4, ROWS, HD)] * 8,
-        in_specs=[VM] * 4,
-        out_specs=[VM] * 8,
+        out_shape=[shape(BF16, 4, ROWS, HD)] * 8 + [shape(I32, 8)],
+        in_specs=[SM] + [VM] * 4,
+        out_specs=[VM] * 8 + [SM],
         scratch_shapes=[pltpu.VMEM((ROWS, H * HD), BF16)],
         compiler_params=pltpu.CompilerParams(vmem_limit_bytes=BIG),
-    )(k, v, q, d)
+    )(offs, k, v, q, d)
 
 
 def by_slot(refs):
@@ -130,24 +134,17 @@
     return [got[slot] for slot in [0] + SEND]
 
 
-def pick_kernel(offs, *refs):
-    got, out, info = by_slot(refs[:8]), refs[8], refs[9]
-    e = lax.rem(lax.axis_index("seq"), 8)
-    for level in range(LEVELS):
-        info[level] = offs[level, e]
-    info[4] = e
-    rows = tile_at(offs[3, e] * TILE)
+def pick_kernel(info, *refs):
+    got, out = by_slot(refs[:8]), refs[8]
+    rows = tile_at(info[3] * TILE)
     for s in range(8):
         out[:, s * TILE : (s + 1) * TILE] = got[s][0:2, rows]
 
 
-def pick3(offs, got):
-    return call(
-        pick_kernel,
-        [shape(BF16, 2, ROWS, HD), shape(I32, 8)],
-        [SM] + [VM] * 8,
-        [VM, SM],
-    )(offs, *in_order(got))
+def pick3(info, got):
+    return call(pick_kernel, shape(BF16, 2, ROWS, HD), [SM] + [VM] * 8, VM)(
+        info, *in_order(got)
+    )
 
 
 def join(pieces):
@@ -463,7 +460,7 @@
 
 def unpack_kernel(info, *refs):
     own, core = refs[0], refs[4]
-    zs = [refs[1], refs[3], refs[2]]
+    zs = [refs[2], refs[1], refs[3]]
     outs = refs[5:9]
     e = info[4]
     order = row_order(True)
@@ -491,19 +488,19 @@
         [SM] + [VM] * 5,
         [VM] * 4,
         cost=SHADOW,
-    )(info, own, zs[0], zs[2], zs[1], core)
+    )(info, own, zs[1], zs[0], zs[2], core)
 
 
 def local(queries, keys, values, cotangent, head_offsets, level_bias):
     def move(x, pairs):
         return lax.ppermute(x, "seq", pairs)
 
-    sent = pack(keys, values, queries, cotangent)
+    packed = pack(head_offsets, keys, values, queries, cotangent)
+    sent, info = packed[:8], packed[8]
     got = [sent[0]] + [None] * 7
     for slot in SEND:
         got[slot] = move(sent[slot], z_perm(*SLOTS[slot]))
-    picked, info = pick3(head_offsets, got)
-    xkv = move(picked, xor_perm(8))
+    xkv = move(pick3(info, got), xor_perm(8))
     comp, p, o, z = forward(info, got)
     att, do, c, acc3, xout, bias = mixing(info, level_bias, comp, o, z, xkv)
     xin = move(xout, xor_perm(8))

time: 87.9 us -> 85.7 us (0.975)
  waiting for transfers between devices: 25.6 us -> 22.7 us
  starting transfers between devices: 45.4 us -> 46.8 us
    ppermute x13, waiting for transfers between devices: 21 us -> 17.9 us  [move(): return lax.ppermute(x, 'seq', pairs)]
    ppermute x13, starting transfers between devices: 32.8 us -> 34.1 us  [move(): return lax.ppermute(x, 'seq', pairs)]
where the time goes in v3:
time: 85.7 us; the launch traced here: 85.6 us
  starting transfers between devices  46.8 us (55%)
  waiting for transfers between devices  22.7 us (26%)
  Pallas kernels  14.6 us (17%)
    ppermute x13, starting transfers between devices, move(): return lax.ppermute(x, 'seq', pairs)  34.1 us
    ppermute x13, waiting for transfers between devices, move(): return lax.ppermute(x, 'seq', pairs)  17.9 us
    all_to_all x1, starting transfers between devices, local(): lax.all_to_all(spread, ('grp', 'seq'), 0, 0, axis_index_groups=GROUPS, ti...  12.7 us
    all_to_all x1, waiting for transfers between devices, local(): lax.all_to_all(spread, ('grp', 'seq'), 0, 0, axis_index_groups=GROUPS, ti...  4.82 us
    pallas_call x1, Pallas kernels, backward(): call(bwd_kernel, MSGS + [CORES, shape(F32, 2, ROWS, HD)], [SM] + [VM] * 6...  2.9 us
    pallas_call x1, Pallas kernels, pack(): pl.pallas_call(pack_kernel, out_shape=[shape(BF16, 4, ROWS, HD)] * 8 + [s...  2.48 us
    pallas_call x1, Pallas kernels, mixing(): call(mix_kernel, [shape(BF16, 8, ROWS, HD), shape(BF16, BASE[3], HD), sha...  2.27 us
    pallas_call x1, Pallas kernels, forward(): call(fwd_kernel, [shape(BF16, 4, COMPACT, HD), shape(F32, BASE[3], 256),...  2.15 us
  transfers between devices with their start and end apart: 14, of which 6 were waited for; matrix products, arithmetic and copies ran while one was open for 0% of the time, Pallas kernels for 8%

profile of v3, /device:TPU:1, one launch (start us, length us, event | category | flops | bytes accessed | tf_op | source)
XLA Modules:
  0.0 85.6 jit_solution(10612684214553470290)
XLA Ops:
  0.6 0.0 copy-start.1
  0.6 0.7 copy-done.1
  1.3 0.0 copy-start
  1.3 2.5 %shard_map.101 = (bf16[4,128,128]{2,1,0:T(8,128)(2,1)S(1)}, bf16[4,128,128]{2,1,0:T(8,128)(2,1)S(1)}, bf16[4,128,128]{2,1,0:T(8,128)(2,1)S(1)}, bf16[4,128,128]{...) custom-call(s32[4,8]{1,0:T(4,128)S(1)} %copy-done.1, ...), custom_call_target="tpu_custom_call" | custom-call | tf_op jit(solution)/shard_map/pallas_call | solution.py:119
  3.8 3.3 %collective-permute-start = (bf16[4,128,128]{2,1,0:T(8,128)(2,1)S(1)}, bf16[4,128,128]{2,1,0:T(8,128)(2,1)S(1)}, u32[]{:S(2)}, u32[]{:S(2)}) collective-permute-start(bf16[4,128,128]{2,1,0:T(8,128)(2,1)S(1)} %get-tuple-element.51), channel_id=1, source_target_pairs={{0,1},{1,0},{2,3},{3,2},{4,5},{5,4},{6,7},{7,6},{8,9},{9,8},{10,11... | collective-permute-start | bytes 393224 | tf_op jit(solution)/shard_map/ppermute | solution.py:496
  7.1 4.3 %collective-permute-start.1 = (bf16[4,128,128]{2,1,0:T(8,128)(2,1)S(1)}, bf16[4,128,128]{2,1,0:T(8,128)(2,1)S(1)}, u32[]{:S(2)}, u32[]{:S(2)}) collective-permute-start(bf16[4,128,128]{2,1,0:T(8,128)(2,1)S(1)} %get-tuple-element.52), channel_id=1, source_target_pairs={{0,2},{1,7},{2,4},{3,1},{4,6},{5,3},{6,0},{7,5},{8,10},{9,15},{10,... | collective-permute-start | bytes 393224 | tf_op jit(solution)/shard_map/ppermute | solution.py:496
  11.4 0.0 collective-permute-start.2
  11.4 1.4 %collective-permute-start.3 = (bf16[4,128,128]{2,1,0:T(8,128)(2,1)S(1)}, bf16[4,128,128]{2,1,0:T(8,128)(2,1)S(1)}, u32[]{:S(2)}, u32[]{:S(2)}) collective-permute-start(bf16[4,128,128]{2,1,0:T(8,128)(2,1)S(1)} %get-tuple-element.54), channel_id=1, source_target_pairs={{0,7},{1,2},{2,1},{3,4},{4,3},{5,6},{6,5},{7,0},{8,15},{9,10},{10,... | collective-permute-start | bytes 393224 | tf_op jit(solution)/shard_map/ppermute | solution.py:496
  12.9 2.4 %collective-permute-start.4 = (bf16[4,128,128]{2,1,0:T(8,128)(2,1)}, bf16[4,128,128]{2,1,0:T(8,128)(2,1)S(1)}, u32[]{:S(2)}, u32[]{:S(2)}) collective-permute-start(bf16[4,128,128]{2,1,0:T(8,128)(2,1)} %get-tuple-element.55), channel_id=1, source_target_pairs={{0,3},{1,6},{2,5},{3,0},{4,7},{5,2},{6,1},{7,4},{8,11},{9,14},{10,... | collective-permute-start | bytes 393224 | tf_op jit(solution)/shard_map/ppermute | solution.py:496
  15.2 0.0 collective-permute-done.refs_1_
  15.2 2.1 %collective-permute-start.5 = (bf16[4,128,128]{2,1,0:T(8,128)(2,1)S(1)}, bf16[4,128,128]{2,1,0:T(8,128)(2,1)S(1)}, u32[]{:S(2)}, u32[]{:S(2)}) collective-permute-start(bf16[4,128,128]{2,1,0:T(8,128)(2,1)S(1)} %get-tuple-element.56), channel_id=1, source_target_pairs={{0,4},{1,5},{2,6},{3,7},{4,0},{5,1},{6,2},{7,3},{8,12},{9,13},{10,... | collective-permute-start | bytes 393224 | tf_op jit(solution)/shard_map/ppermute | solution.py:496
  17.4 0.2 collective-permute-done.1.refs_2_
  17.6 7.0 %collective-permute-start.6 = (bf16[4,128,128]{2,1,0:T(8,128)(2,1)S(1)}, bf16[4,128,128]{2,1,0:T(8,128)(2,1)S(1)}, u32[]{:S(2)}, u32[]{:S(2)}) collective-permute-start(bf16[4,128,128]{2,1,0:T(8,128)(2,1)S(1)} %get-tuple-element.57), channel_id=1, source_target_pairs={{0,5},{1,4},{2,7},{3,6},{4,1},{5,0},{6,3},{7,2},{8,13},{9,12},{10,... | collective-permute-start | bytes 393224 | tf_op jit(solution)/shard_map/ppermute | solution.py:496
  24.6 0.0 collective-permute-done.2.refs_3_
  24.6 0.0 collective-permute-done.3.refs_4_
  24.6 0.0 collective-permute-done.4.refs_5_
  24.6 4.7 %collective-permute-done.5.refs_6_ = bf16[4,128,128]{2,1,0:T(8,128)(2,1)S(1)} collective-permute-done((bf16[4,128,128]{2,1,0:T(8,128)(2,1)S(1)}, bf16[4,128,128]{2,1,0:T(8,128)(2,1)S(1)}, u32[]{:S(2)}, u32[]{:S(2)}) %collective-permute-start.5) | collective-permute-done | bytes 131104 | tf_op jit(solution)/shard_map/ppermute | solution.py:496
  29.3 3.6 %collective-permute-done.6.refs_7_ = bf16[4,128,128]{2,1,0:T(8,128)(2,1)S(1)} collective-permute-done((bf16[4,128,128]{2,1,0:T(8,128)(2,1)S(1)}, bf16[4,128,128]{2,1,0:T(8,128)(2,1)S(1)}, u32[]{:S(2)}, u32[]{:S(2)}) %collective-permute-start.6) | collective-permute-done | bytes 131104 | tf_op jit(solution)/shard_map/ppermute | solution.py:496
  32.9 0.6 shard_map.103
  33.4 1.3 %collective-permute-start.7 = (bf16[2,128,128]{2,1,0:T(8,128)(2,1)S(1)}, bf16[2,128,128]{2,1,0:T(8,128)(2,1)S(1)}, u32[]{:S(2)}, u32[]{:S(2)}) collective-permute-start(bf16[2,128,128]{2,1,0:T(8,128)(2,1)S(1)} %shard_map.103), channel_id=1, source_target_pairs={{0,8},{1,9},{2,10},{3,11},{4,12},{5,13},{6,14},{7,15},{8,0},{9,1},... | collective-permute-start | bytes 196616 | tf_op jit(solution)/shard_map/ppermute | solution.py:496
  34.7 2.1 %shard_map.102 = (bf16[4,1920,128]{2,1,0:T(8,128)(2,1)S(1)}, f32[1792,256]{1,0:T(8,128)S(1)}, f32[1792,128]{1,0:T(8,128)S(1)}, f32[1792,128]{1,0:T(8,128)S(1)}) custom-call(s32[8]{0:T(128)S(1)} %get-tuple-element.49.info, bf16[4,128,128]{2,1,0:T(8,128)(2,1)S(1)} %get-tuple-element.50.refs_0_, bf16[4,128,128]{2,1,0:T(8,128)(2,1)S(1)} %collective-permute-done.refs_1_, ...), custom_call_target="tpu_custom_call" | custom-call | flops 250000000 | bytes 6000000 | tf_op jit(solution)/shard_map/pallas_call | solution.py:222
  36.9 0.0 collective-permute-done.7.xkv
  36.9 0.0 copy-done
  36.9 2.3 %shard_map.104 = (bf16[8,128,128]{2,1,0:T(8,128)(2,1)S(1)}, bf16[1792,128]{1,0:T(8,128)(2,1)S(1)}, f32[1792,128]{1,0:T(8,128)S(1)}, f32[3,128,128]{2,1,0:T(8,128...) custom-call(s32[8]{0:T(128)S(1)} %get-tuple-element.49.info, f32[4,8]{1,0:T(4,128)S(1)} %copy-done, ...), custom_call_target="tpu_custom_call" | custom-call | flops 50000000 | bytes 6000000 | tf_op jit(solution)/shard_map/pallas_call | solution.py:316
  39.2 1.0 %collective-permute-start.8 = (bf16[272,128]{1,0:T(8,128)(2,1)S(1)}, bf16[272,128]{1,0:T(8,128)(2,1)S(1)}, u32[]{:S(2)}, u32[]{:S(2)}) collective-permute-start(bf16[272,128]{1,0:T(8,128)(2,1)S(1)} %get-tuple-element.72), channel_id=1, source_target_pairs={{0,8},{1,9},{2,10},{3,11},{4,12},{5,13},{6,14},{7,15},{8,0},{9,1},... | collective-permute-start | bytes 208904 | tf_op jit(solution)/shard_map/ppermute | solution.py:496
  40.2 2.9 %shard_map.105 = (bf16[4,128,128]{2,1,0:T(8,128)(2,1)S(1)}, bf16[2,4,128,128]{3,2,1,0:T(8,128)(2,1)S(1)}, bf16[2,4,128,128]{3,2,1,0:T(8,128)(2,1)S(1)}, bf16[2,4...) custom-call(s32[8]{0:T(128)S(1)} %get-tuple-element.49.info, ...), custom_call_target="tpu_custom_call" | custom-call | flops 600000000 | bytes 6000000 | tf_op jit(solution)/shard_map/pallas_call | solution.py:379
  43.1 0.0 collective-permute-done.8.refs_6_
  43.1 0.6 shard_map.106
  43.7 3.5 %collective-permute-start.9 = (bf16[4,4,128,128]{3,2,1,0:T(8,128)(2,1)S(1)}, bf16[4,4,128,128]{3,2,1,0:T(8,128)(2,1)S(1)}, u32[]{:S(2)}, u32[]{:S(2)}) collective-permute-start(bf16[4,4,128,128]{3,2,1,0:T(8,128)(2,1)S(1)} %get-tuple-element.78), channel_id=1, source_target_pairs={{0,1},{1,0},{2,3},{3,2},{4,5},{5,4},{6,7},{7,6},{8,9},{9,8},{10,11... | collective-permute-start | bytes 1572872 | tf_op jit(solution)/shard_map/ppermute | solution.py:496
  47.2 1.5 %collective-permute-done.9.refs_3_.refs_4_ = bf16[4,4,128,128]{3,2,1,0:T(8,128)(2,1)S(1)} collective-permute-done((bf16[4,4,128,128]{3,2,1,0:T(8,128)(2,1)S(1)}, bf16[4,4,128,128]{3,2,1,0:T(8,128)(2,1)S(1)}, u32[]{:S(2)}, u32[]{:S(2)}) %collective-permute-start.9) | collective-permute-done | bytes 524320 | tf_op jit(solution)/shard_map/ppermute | solution.py:496
  48.7 1.2 %shard_map.107 = (bf16[2,4,128,128]{3,2,1,0:T(8,128)(2,1)S(1)}, bf16[2,4,128,128]{3,2,1,0:T(8,128)(2,1)S(1)}, bf16[2,4,128,128]{3,2,1,0:T(8,128)(2,1)S(1)}, f32[128,32]{1,0:T(8,128)}) custom-call(s32[8]{0:T(128)S(1)} %get-tuple-element.49.info, ...), custom_call_target="tpu_custom_call", output_to_operand_aliasing={{0}: (1, {}), {1}: (2, {}), {2}: (3, {})} | custom-call | tf_op jit(solution)/shard_map/pallas_call | solution.py:395
  49.9 0.2 collective-permute-start.10
  50.1 6.9 %collective-permute-start.11 = (bf16[2,4,128,128]{3,2,1,0:T(8,128)(2,1)S(1)}, bf16[2,4,128,128]{3,2,1,0:T(8,128)(2,1)S(1)}, u32[]{:S(2)}, u32[]{:S(2)}) collective-permute-start(bf16[2,4,128,128]{3,2,1,0:T(8,128)(2,1)S(1)} %get-tuple-element.81), channel_id=1, source_target_pairs={{2,0},{7,1},{4,2},{1,3},{6,4},{3,5},{0,6},{5,7},{10,8},{15,9},{12,... | collective-permute-start | bytes 786440 | tf_op jit(solution)/shard_map/ppermute | solution.py:496
  57.0 0.7 collective-permute-start.12
  57.7 12.7 %all-to-all-start = ((f32[128,1,32]{2,1,0:T(1,128)}), f32[128,1,32]{2,1,0:T(1,128)S(1)}, u32[]{:S(2)}, u32[]{:S(2)}) async-start(f32[128,1,32]{2,1,0:T(1,128)} %bitcast.1), calls=%async_computation | async-start | bytes 131072 | tf_op jit(solution)/shard_map/all_to_all | solution.py:512
  70.3 0.0 collective-permute-done.10.refs_1_
  70.4 7.9 %collective-permute-done.11.refs_2_ = bf16[2,4,128,128]{3,2,1,0:T(8,128)(2,1)S(1)} collective-permute-done((bf16[2,4,128,128]{3,2,1,0:T(8,128)(2,1)S(1)}, bf16[2,4,128,128]{3,2,1,0:T(8,128)(2,1)S(1)}, u32[]{:S(2)}, u32[]{:S(2)}) %collective-permute-start.11) | collective-permute-done | bytes 262176 | tf_op jit(solution)/shard_map/ppermute | solution.py:496
  78.2 0.0 collective-permute-done.12.refs_3_
  78.2 1.8 %shard_map.108 = (bf16[128,1024]{1,0:T(8,128)(2,1)}, bf16[128,1024]{1,0:T(8,128)(2,1)}, bf16[128,1024]{1,0:T(8,128)(2,1)}, bf16[128,1024]{1,0:T(8,128)(2,1)}) custom-call(s32[8]{0:T(128)S(1)} %get-tuple-element.49.info, bf16[4,128,128]{2,1,0:T(8,128)(2,1)S(1)} %get-tuple-element.74.refs_0_, bf16[2,4,128,128]{3,2,1,0:T(8,128)(2,1)S(1)} %collective-permute-done.10.refs_1_, ...), custom_call_target="tpu_custom_call" | custom-call | bytes 200000000 | tf_op jit(solution)/shard_map/pallas_call | solution.py:485
  80.1 4.8 %all-to-all-done = f32[128,1,32]{2,1,0:T(1,128)S(1)} async-done(((f32[128,1,32]{2,1,0:T(1,128)}), f32[128,1,32]{2,1,0:T(1,128)S(1)}, u32[]{:S(2)}, u32[]{:S(2)}) %all-to-all-start) | async-done | bytes 16416 | tf_op jit(solution)/shard_map/all_to_all | solution.py:512
  84.9 0.7 shard_map.109
Async XLA Ops:
  0.6 0.7 copy-start.1
  1.3 35.6 %copy-start = (f32[4,8]{1,0:T(4,128)S(1)}, f32[4,8]{1,0:T(4,128)}, u32[]{:S(2)}) copy-start(f32[4,8]{1,0:T(4,128)} %bias.1) | copy-start | bytes 388
  3.8 11.4 %collective-permute-start = (bf16[4,128,128]{2,1,0:T(8,128)(2,1)S(1)}, bf16[4,128,128]{2,1,0:T(8,128)(2,1)S(1)}, u32[]{:S(2)}, u32[]{:S(2)}) collective-permute-start(bf16[4,128,128]{2,1,0:T(8,128)(2,1)S(1)} %get-tuple-element.51), channel_id=1, source_target_pairs={{0,1},{1,0},{2,3},{3,2},{4,5},{5,4},{6,7},{7,6},{8,9},{9,8},{10,11... | collective-permute-start | bytes 393224 | tf_op jit(solution)/shard_map/ppermute | solution.py:496
  7.1 10.4 %collective-permute-start.1 = (bf16[4,128,128]{2,1,0:T(8,128)(2,1)S(1)}, bf16[4,128,128]{2,1,0:T(8,128)(2,1)S(1)}, u32[]{:S(2)}, u32[]{:S(2)}) collective-permute-start(bf16[4,128,128]{2,1,0:T(8,128)(2,1)S(1)} %get-tuple-element.52), channel_id=1, source_target_pairs={{0,2},{1,7},{2,4},{3,1},{4,6},{5,3},{6,0},{7,5},{8,10},{9,15},{10,... | collective-permute-start | bytes 393224 | tf_op jit(solution)/shard_map/ppermute | solution.py:496
  11.4 13.2 %collective-permute-start.2 = (bf16[4,128,128]{2,1,0:T(8,128)(2,1)S(1)}, bf16[4,128,128]{2,1,0:T(8,128)(2,1)S(1)}, u32[]{:S(2)}, u32[]{:S(2)}) collective-permute-start(bf16[4,128,128]{2,1,0:T(8,128)(2,1)S(1)} %get-tuple-element.53), channel_id=1, source_target_pairs={{0,6},{1,3},{2,0},{3,5},{4,2},{5,7},{6,4},{7,1},{8,14},{9,11},{10,... | collective-permute-start | bytes 393224 | tf_op jit(solution)/shard_map/ppermute | solution.py:496
  11.4 13.2 %collective-permute-start.3 = (bf16[4,128,128]{2,1,0:T(8,128)(2,1)S(1)}, bf16[4,128,128]{2,1,0:T(8,128)(2,1)S(1)}, u32[]{:S(2)}, u32[]{:S(2)}) collective-permute-start(bf16[4,128,128]{2,1,0:T(8,128)(2,1)S(1)} %get-tuple-element.54), channel_id=1, source_target_pairs={{0,7},{1,2},{2,1},{3,4},{4,3},{5,6},{6,5},{7,0},{8,15},{9,10},{10,... | collective-permute-start | bytes 393224 | tf_op jit(solution)/shard_map/ppermute | solution.py:496
  12.9 11.7 %collective-permute-start.4 = (bf16[4,128,128]{2,1,0:T(8,128)(2,1)}, bf16[4,128,128]{2,1,0:T(8,128)(2,1)S(1)}, u32[]{:S(2)}, u32[]{:S(2)}) collective-permute-start(bf16[4,128,128]{2,1,0:T(8,128)(2,1)} %get-tuple-element.55), channel_id=1, source_target_pairs={{0,3},{1,6},{2,5},{3,0},{4,7},{5,2},{6,1},{7,4},{8,11},{9,14},{10,... | collective-permute-start | bytes 393224 | tf_op jit(solution)/shard_map/ppermute | solution.py:496
  15.2 14.1 %collective-permute-start.5 = (bf16[4,128,128]{2,1,0:T(8,128)(2,1)S(1)}, bf16[4,128,128]{2,1,0:T(8,128)(2,1)S(1)}, u32[]{:S(2)}, u32[]{:S(2)}) collective-permute-start(bf16[4,128,128]{2,1,0:T(8,128)(2,1)S(1)} %get-tuple-element.56), channel_id=1, source_target_pairs={{0,4},{1,5},{2,6},{3,7},{4,0},{5,1},{6,2},{7,3},{8,12},{9,13},{10,... | collective-permute-start | bytes 393224 | tf_op jit(solution)/shard_map/ppermute | solution.py:496
  17.6 15.3 %collective-permute-start.6 = (bf16[4,128,128]{2,1,0:T(8,128)(2,1)S(1)}, bf16[4,128,128]{2,1,0:T(8,128)(2,1)S(1)}, u32[]{:S(2)}, u32[]{:S(2)}) collective-permute-start(bf16[4,128,128]{2,1,0:T(8,128)(2,1)S(1)} %get-tuple-element.57), channel_id=1, source_target_pairs={{0,5},{1,4},{2,7},{3,6},{4,1},{5,0},{6,3},{7,2},{8,13},{9,12},{10,... | collective-permute-start | bytes 393224 | tf_op jit(solution)/shard_map/ppermute | solution.py:496
  33.4 3.4 %collective-permute-start.7 = (bf16[2,128,128]{2,1,0:T(8,128)(2,1)S(1)}, bf16[2,128,128]{2,1,0:T(8,128)(2,1)S(1)}, u32[]{:S(2)}, u32[]{:S(2)}) collective-permute-start(bf16[2,128,128]{2,1,0:T(8,128)(2,1)S(1)} %shard_map.103), channel_id=1, source_target_pairs={{0,8},{1,9},{2,10},{3,11},{4,12},{5,13},{6,14},{7,15},{8,0},{9,1},... | collective-permute-start | bytes 196616 | tf_op jit(solution)/shard_map/ppermute | solution.py:496
  39.2 3.9 %collective-permute-start.8 = (bf16[272,128]{1,0:T(8,128)(2,1)S(1)}, bf16[272,128]{1,0:T(8,128)(2,1)S(1)}, u32[]{:S(2)}, u32[]{:S(2)}) collective-permute-start(bf16[272,128]{1,0:T(8,128)(2,1)S(1)} %get-tuple-element.72), channel_id=1, source_target_pairs={{0,8},{1,9},{2,10},{3,11},{4,12},{5,13},{6,14},{7,15},{8,0},{9,1},... | collective-permute-start | bytes 208904 | tf_op jit(solution)/shard_map/ppermute | solution.py:496
  43.7 5.1 %collective-permute-start.9 = (bf16[4,4,128,128]{3,2,1,0:T(8,128)(2,1)S(1)}, bf16[4,4,128,128]{3,2,1,0:T(8,128)(2,1)S(1)}, u32[]{:S(2)}, u32[]{:S(2)}) collective-permute-start(bf16[4,4,128,128]{3,2,1,0:T(8,128)(2,1)S(1)} %get-tuple-element.78), channel_id=1, source_target_pairs={{0,1},{1,0},{2,3},{3,2},{4,5},{5,4},{6,7},{7,6},{8,9},{9,8},{10,11... | collective-permute-start | bytes 1572872 | tf_op jit(solution)/shard_map/ppermute | solution.py:496
  49.9 20.4 %collective-permute-start.10 = (bf16[2,4,128,128]{3,2,1,0:T(8,128)(2,1)S(1)}, bf16[2,4,128,128]{3,2,1,0:T(8,128)(2,1)S(1)}, u32[]{:S(2)}, u32[]{:S(2)}) collective-permute-start(bf16[2,4,128,128]{3,2,1,0:T(8,128)(2,1)S(1)} %get-tuple-element.80), channel_id=1, source_target_pairs={{4,0},{5,1},{6,2},{7,3},{0,4},{1,5},{2,6},{3,7},{12,8},{13,9},{14,... | collective-permute-start | bytes 786440 | tf_op jit(solution)/shard_map/ppermute | solution.py:496
  50.1 28.1 %collective-permute-start.11 = (bf16[2,4,128,128]{3,2,1,0:T(8,128)(2,1)S(1)}, bf16[2,4,128,128]{3,2,1,0:T(8,128)(2,1)S(1)}, u32[]{:S(2)}, u32[]{:S(2)}) collective-permute-start(bf16[2,4,128,128]{3,2,1,0:T(8,128)(2,1)S(1)} %get-tuple-element.81), channel_id=1, source_target_pairs={{2,0},{7,1},{4,2},{1,3},{6,4},{3,5},{0,6},{5,7},{10,8},{15,9},{12,... | collective-permute-start | bytes 786440 | tf_op jit(solution)/shard_map/ppermute | solution.py:496
  57.0 21.2 %collective-permute-start.12 = (bf16[2,4,128,128]{3,2,1,0:T(8,128)(2,1)S(1)}, bf16[2,4,128,128]{3,2,1,0:T(8,128)(2,1)S(1)}, u32[]{:S(2)}, u32[]{:S(2)}) collective-permute-start(bf16[2,4,128,128]{3,2,1,0:T(8,128)(2,1)S(1)} %get-tuple-element.82), channel_id=1, source_target_pairs={{6,0},{3,1},{0,2},{5,3},{2,4},{7,5},{4,6},{1,7},{14,8},{11,9},{8,1... | collective-permute-start | bytes 786440 | tf_op jit(solution)/shard_map/ppermute | solution.py:496
  57.7 27.2 %all-to-all-start = ((f32[128,1,32]{2,1,0:T(1,128)}), f32[128,1,32]{2,1,0:T(1,128)S(1)}, u32[]{:S(2)}, u32[]{:S(2)}) async-start(f32[128,1,32]{2,1,0:T(1,128)} %bitcast.1), calls=%async_computation | async-start | bytes 131072 | tf_op jit(solution)/shard_map/all_to_all | solution.py:512

commit v4 on v3

--- a/solution.py
+++ b/solution.py
@@ -31,7 +31,11 @@
 COMPACT = 1920
 
 
-GROUPS = [[g * 32 + i for g in range(8) for i in range(32) if i // 8 % 2 == n] for n in range(2)]
+GROUPS = [
+    [g * 32 + i for g in range(8) for i in range(32) if (i // 8 % 2, i % 2) == (n, core)]
+    for n in range(2)
+    for core in range(2)
+]
 
 
 def z_perm(dz, dc):
@@ -301,7 +305,11 @@
         dp = dot_nt(do, v3)
         ds = (p3 * (dp - twice(c))).astype(BF16)
         acc3[0] = dot_nn(ds, k3) * SCALE
-        for n, value in ((1, dot_tn(ds, q3) * SCALE), (2, dot_tn(p3.astype(BF16), do))):
+        both = dot_tn(
+            jnp.concatenate([ds, p3.astype(BF16)], axis=1),
+            jnp.concatenate([q3, do], axis=1),
+        )
+        for n, value in ((1, both[:256, :HD] * SCALE), (2, both[256:, HD:])):
             acc3[n] = value[:ROWS]
             xout[(n - 1) * ROWS : n * ROWS] = value[ROWS:].astype(BF16)
     bias_out[...] = biases
@@ -342,8 +350,12 @@
         p, do = load(p_s, parts), load(do_s, parts)
         ds = (p * (dot_nt(do, v) - twice(load(c_s, parts)))).astype(BF16)
         dq = dot_nn(ds, k) * SCALE
-        dk = dot_tn(ds, q) * SCALE
-        dv = dot_tn(p.astype(BF16), do)
+        both = dot_tn(
+            jnp.concatenate([ds, p.astype(BF16)], axis=1),
+            jnp.concatenate([q, do], axis=1),
+        )
+        dk = both[:256, :HD] * SCALE
+        dv = both[256:, HD:]
         for which, value in enumerate((dq, dk, dv)):
             if level == 0:
                 acc[which, pl.ds(parts[0][0], 256)] = value
@@ -439,21 +451,21 @@
 
 
 def relay_kernel(info, *refs):
-    core, bias = refs[3], refs[4]
-    zs, spread = refs[5:8], refs[8]
+    core, bias, theirs = refs[3:6]
+    zs, spread = refs[6:9], refs[9]
     for dz in range(1, 4):
         zs[dz - 1][0] = core[4 - dz]
-    spread[...] = jnp.broadcast_to(bias[:, : LEVELS * H], spread.shape)
-
-
-def relay(info, msgs, core, bias, devices):
+    spread[...] = jnp.broadcast_to((bias[...] + theirs[...])[:, : LEVELS * H], spread.shape)
+
+
+def relay(info, msgs, core, biases, devices):
     half = pl.BlockSpec((1, 4, ROWS, HD), lambda i, info: (1, 0, 0, 0))
     return patch(
         relay_kernel,
         MSGS[1:] + [shape(F32, devices, LEVELS * H)],
         [half] * 3,
-        [*msgs, core, bias],
-        [full(*CORES.shape), full(1, 128)],
+        [*msgs, core, *biases],
+        [full(*CORES.shape), full(1, 128), full(1, 128)],
         info,
     )
 
@@ -507,7 +519,8 @@
     *msgs, own3 = backward(info, comp, p, do, c, acc3, att)
     own, *zs, core, bias = merge(info, msgs, own3, xin, bias)
     core = move(core, xor_perm(1))
-    *zs, spread = relay(info, zs, core, bias, 128)
+    biases = [bias, move(bias, xor_perm(1))]
+    *zs, spread = relay(info, zs, core, biases, 64)
     zs = [move(x, back_perm(dz, 0)) for dz, x in zip((1, 2, 3), zs)]
     bias = lax.all_to_all(
         spread, ("grp", "seq"), 0, 0, axis_index_groups=GROUPS, tiled=True

time: 85.7 us -> 85 us (level)
  starting transfers between devices: 46.8 us -> 45.6 us
  waiting for transfers between devices: 22.7 us -> 23.6 us
    all_to_all x1, starting transfers between devices: 12.7 us -> 11 us  [local(): lax.all_to_all(spread, ('grp', 'seq'), 0, 0, axis_index_groups=GROUPS, ti...]
    ppermute x13 -> x14, waiting for transfers between devices: 17.9 us -> 18.7 us  [move(): return lax.ppermute(x, 'seq', pairs)]
    ppermute x13 -> x14, starting transfers between devices: 34.1 us -> 34.6 us  [move(): return lax.ppermute(x, 'seq', pairs)]
  transfers between devices with their start and end apart: 14 -> 15, of which waited for: 6 -> 6; matrix products, arithmetic and copies ran while one was open for 0% -> 0% of each run, Pallas kernels for 8% -> 8%
where the time goes in v4:
time: 85 us; the launch traced here: 84.8 us
  starting transfers between devices  45.6 us (54%)
  waiting for transfers between devices  23.6 us (28%)
  Pallas kernels  14.2 us (17%)
    ppermute x14, starting transfers between devices, move(): return lax.ppermute(x, 'seq', pairs)  34.6 us
    ppermute x14, waiting for transfers between devices, move(): return lax.ppermute(x, 'seq', pairs)  18.7 us
    all_to_all x1, starting transfers between devices, local(): lax.all_to_all(spread, ('grp', 'seq'), 0, 0, axis_index_groups=GROUPS, ti...  11 us
    all_to_all x1, waiting for transfers between devices, local(): lax.all_to_all(spread, ('grp', 'seq'), 0, 0, axis_index_groups=GROUPS, ti...  4.9 us
    pallas_call x1, Pallas kernels, pack(): pl.pallas_call(pack_kernel, out_shape=[shape(BF16, 4, ROWS, HD)] * 8 + [s...  2.48 us
    pallas_call x1, Pallas kernels, backward(): call(bwd_kernel, MSGS + [CORES, shape(F32, 2, ROWS, HD)], [SM] + [VM] * 6...  2.44 us
    pallas_call x1, Pallas kernels, mixing(): call(mix_kernel, [shape(BF16, 8, ROWS, HD), shape(BF16, BASE[3], HD), sha...  2.32 us
    pallas_call x1, Pallas kernels, forward(): call(fwd_kernel, [shape(BF16, 4, COMPACT, HD), shape(F32, BASE[3], 256),...  2.15 us
  transfers between devices with their start and end apart: 15, of which 6 were waited for; matrix products, arithmetic and copies ran while one was open for 0% of the time, Pallas kernels for 8%

profile of v4, /device:TPU:1, one launch (start us, length us, event | category | flops | bytes accessed | tf_op | source)
XLA Modules:
  0.0 84.8 jit_solution(16348893094771448452)
XLA Ops:
  0.6 0.0 copy-start.1
  0.6 0.7 copy-done.1
  1.3 0.0 copy-start
  1.3 2.5 %shard_map.101 = (bf16[4,128,128]{2,1,0:T(8,128)(2,1)S(1)}, bf16[4,128,128]{2,1,0:T(8,128)(2,1)S(1)}, bf16[4,128,128]{2,1,0:T(8,128)(2,1)S(1)}, bf16[4,128,128]{...) custom-call(s32[4,8]{1,0:T(4,128)S(1)} %copy-done.1, ...), custom_call_target="tpu_custom_call" | custom-call | tf_op jit(solution)/shard_map/pallas_call | solution.py:123
  3.8 3.3 %collective-permute-start = (bf16[4,128,128]{2,1,0:T(8,128)(2,1)S(1)}, bf16[4,128,128]{2,1,0:T(8,128)(2,1)S(1)}, u32[]{:S(2)}, u32[]{:S(2)}) collective-permute-start(bf16[4,128,128]{2,1,0:T(8,128)(2,1)S(1)} %get-tuple-element.51), channel_id=1, source_target_pairs={{0,1},{1,0},{2,3},{3,2},{4,5},{5,4},{6,7},{7,6},{8,9},{9,8},{10,11... | collective-permute-start | bytes 393224 | tf_op jit(solution)/shard_map/ppermute | solution.py:508
  7.1 4.3 %collective-permute-start.1 = (bf16[4,128,128]{2,1,0:T(8,128)(2,1)S(1)}, bf16[4,128,128]{2,1,0:T(8,128)(2,1)S(1)}, u32[]{:S(2)}, u32[]{:S(2)}) collective-permute-start(bf16[4,128,128]{2,1,0:T(8,128)(2,1)S(1)} %get-tuple-element.52), channel_id=1, source_target_pairs={{0,2},{1,7},{2,4},{3,1},{4,6},{5,3},{6,0},{7,5},{8,10},{9,15},{10,... | collective-permute-start | bytes 393224 | tf_op jit(solution)/shard_map/ppermute | solution.py:508
  11.4 0.0 collective-permute-start.2
  11.4 1.4 %collective-permute-start.3 = (bf16[4,128,128]{2,1,0:T(8,128)(2,1)S(1)}, bf16[4,128,128]{2,1,0:T(8,128)(2,1)S(1)}, u32[]{:S(2)}, u32[]{:S(2)}) collective-permute-start(bf16[4,128,128]{2,1,0:T(8,128)(2,1)S(1)} %get-tuple-element.54), channel_id=1, source_target_pairs={{0,7},{1,2},{2,1},{3,4},{4,3},{5,6},{6,5},{7,0},{8,15},{9,10},{10,... | collective-permute-start | bytes 393224 | tf_op jit(solution)/shard_map/ppermute | solution.py:508
  12.9 2.4 %collective-permute-start.4 = (bf16[4,128,128]{2,1,0:T(8,128)(2,1)}, bf16[4,128,128]{2,1,0:T(8,128)(2,1)S(1)}, u32[]{:S(2)}, u32[]{:S(2)}) collective-permute-start(bf16[4,128,128]{2,1,0:T(8,128)(2,1)} %get-tuple-element.55), channel_id=1, source_target_pairs={{0,3},{1,6},{2,5},{3,0},{4,7},{5,2},{6,1},{7,4},{8,11},{9,14},{10,... | collective-permute-start | bytes 393224 | tf_op jit(solution)/shard_map/ppermute | solution.py:508
  15.2 0.0 collective-permute-done.refs_1_
  15.2 2.1 %collective-permute-start.5 = (bf16[4,128,128]{2,1,0:T(8,128)(2,1)S(1)}, bf16[4,128,128]{2,1,0:T(8,128)(2,1)S(1)}, u32[]{:S(2)}, u32[]{:S(2)}) collective-permute-start(bf16[4,128,128]{2,1,0:T(8,128)(2,1)S(1)} %get-tuple-element.56), channel_id=1, source_target_pairs={{0,4},{1,5},{2,6},{3,7},{4,0},{5,1},{6,2},{7,3},{8,12},{9,13},{10,... | collective-permute-start | bytes 393224 | tf_op jit(solution)/shard_map/ppermute | solution.py:508
  17.4 0.2 collective-permute-done.1.refs_2_
  17.6 7.0 %collective-permute-start.6 = (bf16[4,128,128]{2,1,0:T(8,128)(2,1)S(1)}, bf16[4,128,128]{2,1,0:T(8,128)(2,1)S(1)}, u32[]{:S(2)}, u32[]{:S(2)}) collective-permute-start(bf16[4,128,128]{2,1,0:T(8,128)(2,1)S(1)} %get-tuple-element.57), channel_id=1, source_target_pairs={{0,5},{1,4},{2,7},{3,6},{4,1},{5,0},{6,3},{7,2},{8,13},{9,12},{10,... | collective-permute-start | bytes 393224 | tf_op jit(solution)/shard_map/ppermute | solution.py:508
  24.6 0.0 collective-permute-done.2.refs_3_
  24.6 0.0 collective-permute-done.3.refs_4_
  24.6 0.0 collective-permute-done.4.refs_5_
  24.6 4.7 %collective-permute-done.5.refs_6_ = bf16[4,128,128]{2,1,0:T(8,128)(2,1)S(1)} collective-permute-done((bf16[4,128,128]{2,1,0:T(8,128)(2,1)S(1)}, bf16[4,128,128]{2,1,0:T(8,128)(2,1)S(1)}, u32[]{:S(2)}, u32[]{:S(2)}) %collective-permute-start.5) | collective-permute-done | bytes 131104 | tf_op jit(solution)/shard_map/ppermute | solution.py:508
  29.3 3.6 %collective-permute-done.6.refs_7_ = bf16[4,128,128]{2,1,0:T(8,128)(2,1)S(1)} collective-permute-done((bf16[4,128,128]{2,1,0:T(8,128)(2,1)S(1)}, bf16[4,128,128]{2,1,0:T(8,128)(2,1)S(1)}, u32[]{:S(2)}, u32[]{:S(2)}) %collective-permute-start.6) | collective-permute-done | bytes 131104 | tf_op jit(solution)/shard_map/ppermute | solution.py:508
  32.9 0.6 shard_map.103
  33.4 1.3 %collective-permute-start.7 = (bf16[2,128,128]{2,1,0:T(8,128)(2,1)S(1)}, bf16[2,128,128]{2,1,0:T(8,128)(2,1)S(1)}, u32[]{:S(2)}, u32[]{:S(2)}) collective-permute-start(bf16[2,128,128]{2,1,0:T(8,128)(2,1)S(1)} %shard_map.103), channel_id=1, source_target_pairs={{0,8},{1,9},{2,10},{3,11},{4,12},{5,13},{6,14},{7,15},{8,0},{9,1},... | collective-permute-start | bytes 196616 | tf_op jit(solution)/shard_map/ppermute | solution.py:508
  34.7 2.2 %shard_map.102 = (bf16[4,1920,128]{2,1,0:T(8,128)(2,1)S(1)}, f32[1792,256]{1,0:T(8,128)S(1)}, f32[1792,128]{1,0:T(8,128)S(1)}, f32[1792,128]{1,0:T(8,128)S(1)}) custom-call(s32[8]{0:T(128)S(1)} %get-tuple-element.49.info, bf16[4,128,128]{2,1,0:T(8,128)(2,1)S(1)} %get-tuple-element.50.refs_0_, bf16[4,128,128]{2,1,0:T(8,128)(2,1)S(1)} %collective-permute-done.refs_1_, ...), custom_call_target="tpu_custom_call" | custom-call | flops 250000000 | bytes 6000000 | tf_op jit(solution)/shard_map/pallas_call | solution.py:226
  36.9 0.0 collective-permute-done.7.xkv
  36.9 0.0 copy-done
  36.9 2.3 %shard_map.104 = (bf16[8,128,128]{2,1,0:T(8,128)(2,1)S(1)}, bf16[1792,128]{1,0:T(8,128)(2,1)S(1)}, f32[1792,128]{1,0:T(8,128)S(1)}, f32[3,128,128]{2,1,0:T(8,128...) custom-call(s32[8]{0:T(128)S(1)} %get-tuple-element.49.info, f32[4,8]{1,0:T(4,128)S(1)} %copy-done, ...), custom_call_target="tpu_custom_call" | custom-call | flops 50000000 | bytes 6000000 | tf_op jit(solution)/shard_map/pallas_call | solution.py:324
  39.2 1.0 %collective-permute-start.8 = (bf16[272,128]{1,0:T(8,128)(2,1)S(1)}, bf16[272,128]{1,0:T(8,128)(2,1)S(1)}, u32[]{:S(2)}, u32[]{:S(2)}) collective-permute-start(bf16[272,128]{1,0:T(8,128)(2,1)S(1)} %get-tuple-element.72), channel_id=1, source_target_pairs={{0,8},{1,9},{2,10},{3,11},{4,12},{5,13},{6,14},{7,15},{8,0},{9,1},... | collective-permute-start | bytes 208904 | tf_op jit(solution)/shard_map/ppermute | solution.py:508
  40.2 2.4 %shard_map.105 = (bf16[4,128,128]{2,1,0:T(8,128)(2,1)S(1)}, bf16[2,4,128,128]{3,2,1,0:T(8,128)(2,1)S(1)}, bf16[2,4,128,128]{3,2,1,0:T(8,128)(2,1)S(1)}, bf16[2,4...) custom-call(s32[8]{0:T(128)S(1)} %get-tuple-element.49.info, ...), custom_call_target="tpu_custom_call" | custom-call | flops 600000000 | bytes 6000000 | tf_op jit(solution)/shard_map/pallas_call | solution.py:391
  42.7 0.0 collective-permute-done.8.refs_6_
  42.7 0.6 shard_map.106
  43.3 3.9 %collective-permute-start.9 = (bf16[4,4,128,128]{3,2,1,0:T(8,128)(2,1)S(1)}, bf16[4,4,128,128]{3,2,1,0:T(8,128)(2,1)S(1)}, u32[]{:S(2)}, u32[]{:S(2)}) collective-permute-start(bf16[4,4,128,128]{3,2,1,0:T(8,128)(2,1)S(1)} %get-tuple-element.78), channel_id=1, source_target_pairs={{0,1},{1,0},{2,3},{3,2},{4,5},{5,4},{6,7},{7,6},{8,9},{9,8},{10,11... | collective-permute-start | bytes 1572872 | tf_op jit(solution)/shard_map/ppermute | solution.py:508
  47.1 0.1 collective-permute-start.10
  47.2 1.4 %collective-permute-done.10.refs_5_ = f32[1,128]{1,0:T(1,128)S(1)} collective-permute-done((f32[1,128]{1,0:T(1,128)S(1)}, f32[1,128]{1,0:T(1,128)S(1)}, u32[]{:S(2)}, u32[]{:S(2)}) %collective-permute-start.10) | collective-permute-done | bytes 544 | tf_op jit(solution)/shard_map/ppermute | solution.py:508
  48.7 0.0 collective-permute-done.9.refs_3_.refs_4_
  48.7 1.2 %shard_map.107 = (bf16[2,4,128,128]{3,2,1,0:T(8,128)(2,1)S(1)}, bf16[2,4,128,128]{3,2,1,0:T(8,128)(2,1)S(1)}, bf16[2,4,128,128]{3,2,1,0:T(8,128)(2,1)S(1)}, f32[64,32]{1,0:T(8,128)}) custom-call(s32[8]{0:T(128)S(1)} %get-tuple-element.49.info, ...), custom_call_target="tpu_custom_call", output_to_operand_aliasing={{0}: (1, {}), {1}: (2, {}), {2}: (3, {})} | custom-call | tf_op jit(solution)/shard_map/pallas_call | solution.py:407
  49.9 0.2 collective-permute-start.11
  50.0 6.9 %collective-permute-start.12 = (bf16[2,4,128,128]{3,2,1,0:T(8,128)(2,1)S(1)}, bf16[2,4,128,128]{3,2,1,0:T(8,128)(2,1)S(1)}, u32[]{:S(2)}, u32[]{:S(2)}) collective-permute-start(bf16[2,4,128,128]{3,2,1,0:T(8,128)(2,1)S(1)} %get-tuple-element.81), channel_id=1, source_target_pairs={{2,0},{7,1},{4,2},{1,3},{6,4},{3,5},{0,6},{5,7},{10,8},{15,9},{12,... | collective-permute-start | bytes 786440 | tf_op jit(solution)/shard_map/ppermute | solution.py:508
  56.9 0.7 collective-permute-start.13
  57.6 11.0 %all-to-all-start = ((f32[64,1,32]{2,1,0:T(1,128)}), f32[64,1,32]{2,1,0:T(1,128)S(1)}, u32[]{:S(2)}, u32[]{:S(2)}) async-start(f32[64,1,32]{2,1,0:T(1,128)} %bitcast.1), calls=%async_computation | async-start | bytes 65536 | tf_op jit(solution)/shard_map/all_to_all | solution.py:525
  68.6 0.0 collective-permute-done.11.refs_1_
  68.6 8.8 %collective-permute-done.12.refs_2_ = bf16[2,4,128,128]{3,2,1,0:T(8,128)(2,1)S(1)} collective-permute-done((bf16[2,4,128,128]{3,2,1,0:T(8,128)(2,1)S(1)}, bf16[2,4,128,128]{3,2,1,0:T(8,128)(2,1)S(1)}, u32[]{:S(2)}, u32[]{:S(2)}) %collective-permute-start.12) | collective-permute-done | bytes 262176 | tf_op jit(solution)/shard_map/ppermute | solution.py:508
  77.4 0.0 collective-permute-done.13.refs_3_
  77.4 1.8 %shard_map.108 = (bf16[128,1024]{1,0:T(8,128)(2,1)}, bf16[128,1024]{1,0:T(8,128)(2,1)}, bf16[128,1024]{1,0:T(8,128)(2,1)}, bf16[128,1024]{1,0:T(8,128)(2,1)}) custom-call(s32[8]{0:T(128)S(1)} %get-tuple-element.49.info, bf16[4,128,128]{2,1,0:T(8,128)(2,1)S(1)} %get-tuple-element.74.refs_0_, bf16[2,4,128,128]{3,2,1,0:T(8,128)(2,1)S(1)} %collective-permute-done.11.refs_1_, ...), custom_call_target="tpu_custom_call" | custom-call | bytes 200000000 | tf_op jit(solution)/shard_map/pallas_call | solution.py:497
  79.2 4.9 %all-to-all-done = f32[64,1,32]{2,1,0:T(1,128)S(1)} async-done(((f32[64,1,32]{2,1,0:T(1,128)}), f32[64,1,32]{2,1,0:T(1,128)S(1)}, u32[]{:S(2)}, u32[]{:S(2)}) %all-to-all-start) | async-done | bytes 8224 | tf_op jit(solution)/shard_map/all_to_all | solution.py:525
  84.2 0.7 shard_map.109
Async XLA Ops:
  0.6 0.7 copy-start.1
  1.3 35.6 %copy-start = (f32[4,8]{1,0:T(4,128)S(1)}, f32[4,8]{1,0:T(4,128)}, u32[]{:S(2)}) copy-start(f32[4,8]{1,0:T(4,128)} %bias.1) | copy-start | bytes 388
  3.8 11.4 %collective-permute-start = (bf16[4,128,128]{2,1,0:T(8,128)(2,1)S(1)}, bf16[4,128,128]{2,1,0:T(8,128)(2,1)S(1)}, u32[]{:S(2)}, u32[]{:S(2)}) collective-permute-start(bf16[4,128,128]{2,1,0:T(8,128)(2,1)S(1)} %get-tuple-element.51), channel_id=1, source_target_pairs={{0,1},{1,0},{2,3},{3,2},{4,5},{5,4},{6,7},{7,6},{8,9},{9,8},{10,11... | collective-permute-start | bytes 393224 | tf_op jit(solution)/shard_map/ppermute | solution.py:508
  7.1 10.4 %collective-permute-start.1 = (bf16[4,128,128]{2,1,0:T(8,128)(2,1)S(1)}, bf16[4,128,128]{2,1,0:T(8,128)(2,1)S(1)}, u32[]{:S(2)}, u32[]{:S(2)}) collective-permute-start(bf16[4,128,128]{2,1,0:T(8,128)(2,1)S(1)} %get-tuple-element.52), channel_id=1, source_target_pairs={{0,2},{1,7},{2,4},{3,1},{4,6},{5,3},{6,0},{7,5},{8,10},{9,15},{10,... | collective-permute-start | bytes 393224 | tf_op jit(solution)/shard_map/ppermute | solution.py:508
  11.4 13.2 %collective-permute-start.2 = (bf16[4,128,128]{2,1,0:T(8,128)(2,1)S(1)}, bf16[4,128,128]{2,1,0:T(8,128)(2,1)S(1)}, u32[]{:S(2)}, u32[]{:S(2)}) collective-permute-start(bf16[4,128,128]{2,1,0:T(8,128)(2,1)S(1)} %get-tuple-element.53), channel_id=1, source_target_pairs={{0,6},{1,3},{2,0},{3,5},{4,2},{5,7},{6,4},{7,1},{8,14},{9,11},{10,... | collective-permute-start | bytes 393224 | tf_op jit(solution)/shard_map/ppermute | solution.py:508
  11.4 13.2 %collective-permute-start.3 = (bf16[4,128,128]{2,1,0:T(8,128)(2,1)S(1)}, bf16[4,128,128]{2,1,0:T(8,128)(2,1)S(1)}, u32[]{:S(2)}, u32[]{:S(2)}) collective-permute-start(bf16[4,128,128]{2,1,0:T(8,128)(2,1)S(1)} %get-tuple-element.54), channel_id=1, source_target_pairs={{0,7},{1,2},{2,1},{3,4},{4,3},{5,6},{6,5},{7,0},{8,15},{9,10},{10,... | collective-permute-start | bytes 393224 | tf_op jit(solution)/shard_map/ppermute | solution.py:508
  12.9 11.7 %collective-permute-start.4 = (bf16[4,128,128]{2,1,0:T(8,128)(2,1)}, bf16[4,128,128]{2,1,0:T(8,128)(2,1)S(1)}, u32[]{:S(2)}, u32[]{:S(2)}) collective-permute-start(bf16[4,128,128]{2,1,0:T(8,128)(2,1)} %get-tuple-element.55), channel_id=1, source_target_pairs={{0,3},{1,6},{2,5},{3,0},{4,7},{5,2},{6,1},{7,4},{8,11},{9,14},{10,... | collective-permute-start | bytes 393224 | tf_op jit(solution)/shard_map/ppermute | solution.py:508
  15.2 14.1 %collective-permute-start.5 = (bf16[4,128,128]{2,1,0:T(8,128)(2,1)S(1)}, bf16[4,128,128]{2,1,0:T(8,128)(2,1)S(1)}, u32[]{:S(2)}, u32[]{:S(2)}) collective-permute-start(bf16[4,128,128]{2,1,0:T(8,128)(2,1)S(1)} %get-tuple-element.56), channel_id=1, source_target_pairs={{0,4},{1,5},{2,6},{3,7},{4,0},{5,1},{6,2},{7,3},{8,12},{9,13},{10,... | collective-permute-start | bytes 393224 | tf_op jit(solution)/shard_map/ppermute | solution.py:508
  17.6 15.3 %collective-permute-start.6 = (bf16[4,128,128]{2,1,0:T(8,128)(2,1)S(1)}, bf16[4,128,128]{2,1,0:T(8,128)(2,1)S(1)}, u32[]{:S(2)}, u32[]{:S(2)}) collective-permute-start(bf16[4,128,128]{2,1,0:T(8,128)(2,1)S(1)} %get-tuple-element.57), channel_id=1, source_target_pairs={{0,5},{1,4},{2,7},{3,6},{4,1},{5,0},{6,3},{7,2},{8,13},{9,12},{10,... | collective-permute-start | bytes 393224 | tf_op jit(solution)/shard_map/ppermute | solution.py:508
  33.4 3.4 %collective-permute-start.7 = (bf16[2,128,128]{2,1,0:T(8,128)(2,1)S(1)}, bf16[2,128,128]{2,1,0:T(8,128)(2,1)S(1)}, u32[]{:S(2)}, u32[]{:S(2)}) collective-permute-start(bf16[2,128,128]{2,1,0:T(8,128)(2,1)S(1)} %shard_map.103), channel_id=1, source_target_pairs={{0,8},{1,9},{2,10},{3,11},{4,12},{5,13},{6,14},{7,15},{8,0},{9,1},... | collective-permute-start | bytes 196616 | tf_op jit(solution)/shard_map/ppermute | solution.py:508
  39.2 3.5 %collective-permute-start.8 = (bf16[272,128]{1,0:T(8,128)(2,1)S(1)}, bf16[272,128]{1,0:T(8,128)(2,1)S(1)}, u32[]{:S(2)}, u32[]{:S(2)}) collective-permute-start(bf16[272,128]{1,0:T(8,128)(2,1)S(1)} %get-tuple-element.72), channel_id=1, source_target_pairs={{0,8},{1,9},{2,10},{3,11},{4,12},{5,13},{6,14},{7,15},{8,0},{9,1},... | collective-permute-start | bytes 208904 | tf_op jit(solution)/shard_map/ppermute | solution.py:508
  43.3 5.4 %collective-permute-start.9 = (bf16[4,4,128,128]{3,2,1,0:T(8,128)(2,1)S(1)}, bf16[4,4,128,128]{3,2,1,0:T(8,128)(2,1)S(1)}, u32[]{:S(2)}, u32[]{:S(2)}) collective-permute-start(bf16[4,4,128,128]{3,2,1,0:T(8,128)(2,1)S(1)} %get-tuple-element.78), channel_id=1, source_target_pairs={{0,1},{1,0},{2,3},{3,2},{4,5},{5,4},{6,7},{7,6},{8,9},{9,8},{10,11... | collective-permute-start | bytes 1572872 | tf_op jit(solution)/shard_map/ppermute | solution.py:508
  47.1 1.5 %collective-permute-start.10 = (f32[1,128]{1,0:T(1,128)S(1)}, f32[1,128]{1,0:T(1,128)S(1)}, u32[]{:S(2)}, u32[]{:S(2)}) collective-permute-start(f32[1,128]{1,0:T(1,128)S(1)} %get-tuple-element.79.refs_4_), channel_id=1, source_target_pairs={{0,1},{1,0},{2,3},{3,2},{4,5},{5,4},{6,7},{7,6},{8,9},{9,8},{10,11... | collective-permute-start | bytes 1544 | tf_op jit(solution)/shard_map/ppermute | solution.py:508
  49.9 18.7 %collective-permute-start.11 = (bf16[2,4,128,128]{3,2,1,0:T(8,128)(2,1)S(1)}, bf16[2,4,128,128]{3,2,1,0:T(8,128)(2,1)S(1)}, u32[]{:S(2)}, u32[]{:S(2)}) collective-permute-start(bf16[2,4,128,128]{3,2,1,0:T(8,128)(2,1)S(1)} %get-tuple-element.80), channel_id=1, source_target_pairs={{4,0},{5,1},{6,2},{7,3},{0,4},{1,5},{2,6},{3,7},{12,8},{13,9},{14,... | collective-permute-start | bytes 786440 | tf_op jit(solution)/shard_map/ppermute | solution.py:508
  50.0 27.4 %collective-permute-start.12 = (bf16[2,4,128,128]{3,2,1,0:T(8,128)(2,1)S(1)}, bf16[2,4,128,128]{3,2,1,0:T(8,128)(2,1)S(1)}, u32[]{:S(2)}, u32[]{:S(2)}) collective-permute-start(bf16[2,4,128,128]{3,2,1,0:T(8,128)(2,1)S(1)} %get-tuple-element.81), channel_id=1, source_target_pairs={{2,0},{7,1},{4,2},{1,3},{6,4},{3,5},{0,6},{5,7},{10,8},{15,9},{12,... | collective-permute-start | bytes 786440 | tf_op jit(solution)/shard_map/ppermute | solution.py:508
  56.9 20.5 %collective-permute-start.13 = (bf16[2,4,128,128]{3,2,1,0:T(8,128)(2,1)S(1)}, bf16[2,4,128,128]{3,2,1,0:T(8,128)(2,1)S(1)}, u32[]{:S(2)}, u32[]{:S(2)}) collective-permute-start(bf16[2,4,128,128]{3,2,1,0:T(8,128)(2,1)S(1)} %get-tuple-element.82), channel_id=1, source_target_pairs={{6,0},{3,1},{0,2},{5,3},{2,4},{7,5},{4,6},{1,7},{14,8},{11,9},{8,1... | collective-permute-start | bytes 786440 | tf_op jit(solution)/shard_map/ppermute | solution.py:508
  57.6 26.5 %all-to-all-start = ((f32[64,1,32]{2,1,0:T(1,128)}), f32[64,1,32]{2,1,0:T(1,128)S(1)}, u32[]{:S(2)}, u32[]{:S(2)}) async-start(f32[64,1,32]{2,1,0:T(1,128)} %bitcast.1), calls=%async_computation | async-start | bytes 65536 | tf_op jit(solution)/shard_map/all_to_all | solution.py:525

commit v5 on v4

--- a/solution.py
+++ b/solution.py
@@ -452,17 +452,17 @@
 
 def relay_kernel(info, *refs):
     core, bias, theirs = refs[3:6]
-    zs, spread = refs[6:9], refs[9]
+    zs, total = refs[6:9], refs[9]
     for dz in range(1, 4):
         zs[dz - 1][0] = core[4 - dz]
-    spread[...] = jnp.broadcast_to((bias[...] + theirs[...])[:, : LEVELS * H], spread.shape)
-
-
-def relay(info, msgs, core, biases, devices):
+    total[...] = bias[...] + theirs[...]
+
+
+def relay(info, msgs, core, biases):
     half = pl.BlockSpec((1, 4, ROWS, HD), lambda i, info: (1, 0, 0, 0))
     return patch(
         relay_kernel,
-        MSGS[1:] + [shape(F32, devices, LEVELS * H)],
+        MSGS[1:] + [shape(F32, 1, 128)],
         [half] * 3,
         [*msgs, core, *biases],
         [full(*CORES.shape), full(1, 128), full(1, 128)],
@@ -520,8 +520,9 @@
     own, *zs, core, bias = merge(info, msgs, own3, xin, bias)
     core = move(core, xor_perm(1))
     biases = [bias, move(bias, xor_perm(1))]
-    *zs, spread = relay(info, zs, core, biases, 64)
+    *zs, bias = relay(info, zs, core, biases)
     zs = [move(x, back_perm(dz, 0)) for dz, x in zip((1, 2, 3), zs)]
+    spread = jnp.broadcast_to(bias[:, : LEVELS * H], (64, LEVELS * H))
     bias = lax.all_to_all(
         spread, ("grp", "seq"), 0, 0, axis_index_groups=GROUPS, tiled=True
     )

time: 85 us -> 84.6 us (level)
  transfers between devices with their start and end apart: 15 -> 15, of which waited for: 6 -> 6; matrix products, arithmetic and copies ran while one was open for 0% -> 1% of each run, Pallas kernels for 8% -> 8%
where the time goes in v5:
time: 84.6 us; the launch traced here: 84.5 us
  starting transfers between devices  45.8 us (54%)
  waiting for transfers between devices  23 us (27%)
  Pallas kernels  13.6 us (16%)
  local copies, waits for them, and re-layouts  1.32 us (2%)
    ppermute x14, starting transfers between devices, move(): return lax.ppermute(x, 'seq', pairs)  34.8 us
    ppermute x14, waiting for transfers between devices, move(): return lax.ppermute(x, 'seq', pairs)  18.1 us
    all_to_all x1, starting transfers between devices, local(): lax.all_to_all(spread, ('grp', 'seq'), 0, 0, axis_index_groups=GROUPS, ti...  11 us
    all_to_all x1, waiting for transfers between devices, local(): lax.all_to_all(spread, ('grp', 'seq'), 0, 0, axis_index_groups=GROUPS, ti...  4.87 us
    pallas_call x1, Pallas kernels, pack(): pl.pallas_call(pack_kernel, out_shape=[shape(BF16, 4, ROWS, HD)] * 8 + [s...  2.48 us
    pallas_call x1, Pallas kernels, backward(): call(bwd_kernel, MSGS + [CORES, shape(F32, 2, ROWS, HD)], [SM] + [VM] * 6...  2.43 us
    pallas_call x1, Pallas kernels, mixing(): call(mix_kernel, [shape(BF16, 8, ROWS, HD), shape(BF16, BASE[3], HD), sha...  2.32 us
    pallas_call x1, Pallas kernels, forward(): call(fwd_kernel, [shape(BF16, 4, COMPACT, HD), shape(F32, BASE[3], 256),...  2.15 us
  transfers between devices with their start and end apart: 15, of which 6 were waited for; matrix products, arithmetic and copies ran while one was open for 1% of the time, Pallas kernels for 8%

profile of v5, /device:TPU:1, one launch (start us, length us, event | category | flops | bytes accessed | tf_op | source)
XLA Modules:
  0.0 84.5 jit_solution(5200439751999951177)
XLA Ops:
  0.6 0.0 copy-start.1
  0.6 0.7 copy-done.1
  1.3 0.0 copy-start
  1.3 2.5 %shard_map.101 = (bf16[4,128,128]{2,1,0:T(8,128)(2,1)S(1)}, bf16[4,128,128]{2,1,0:T(8,128)(2,1)S(1)}, bf16[4,128,128]{2,1,0:T(8,128)(2,1)S(1)}, bf16[4,128,128]{...) custom-call(s32[4,8]{1,0:T(4,128)S(1)} %copy-done.1, ...), custom_call_target="tpu_custom_call" | custom-call | tf_op jit(solution)/shard_map/pallas_call | solution.py:123
  3.8 3.3 %collective-permute-start = (bf16[4,128,128]{2,1,0:T(8,128)(2,1)S(1)}, bf16[4,128,128]{2,1,0:T(8,128)(2,1)S(1)}, u32[]{:S(2)}, u32[]{:S(2)}) collective-permute-start(bf16[4,128,128]{2,1,0:T(8,128)(2,1)S(1)} %get-tuple-element.51), channel_id=1, source_target_pairs={{0,1},{1,0},{2,3},{3,2},{4,5},{5,4},{6,7},{7,6},{8,9},{9,8},{10,11... | collective-permute-start | bytes 393224 | tf_op jit(solution)/shard_map/ppermute | solution.py:508
  7.1 4.3 %collective-permute-start.1 = (bf16[4,128,128]{2,1,0:T(8,128)(2,1)S(1)}, bf16[4,128,128]{2,1,0:T(8,128)(2,1)S(1)}, u32[]{:S(2)}, u32[]{:S(2)}) collective-permute-start(bf16[4,128,128]{2,1,0:T(8,128)(2,1)S(1)} %get-tuple-element.52), channel_id=1, source_target_pairs={{0,2},{1,7},{2,4},{3,1},{4,6},{5,3},{6,0},{7,5},{8,10},{9,15},{10,... | collective-permute-start | bytes 393224 | tf_op jit(solution)/shard_map/ppermute | solution.py:508
  11.4 0.0 collective-permute-start.2
  11.4 1.4 %collective-permute-start.3 = (bf16[4,128,128]{2,1,0:T(8,128)(2,1)S(1)}, bf16[4,128,128]{2,1,0:T(8,128)(2,1)S(1)}, u32[]{:S(2)}, u32[]{:S(2)}) collective-permute-start(bf16[4,128,128]{2,1,0:T(8,128)(2,1)S(1)} %get-tuple-element.54), channel_id=1, source_target_pairs={{0,7},{1,2},{2,1},{3,4},{4,3},{5,6},{6,5},{7,0},{8,15},{9,10},{10,... | collective-permute-start | bytes 393224 | tf_op jit(solution)/shard_map/ppermute | solution.py:508
  12.9 2.4 %collective-permute-start.4 = (bf16[4,128,128]{2,1,0:T(8,128)(2,1)}, bf16[4,128,128]{2,1,0:T(8,128)(2,1)S(1)}, u32[]{:S(2)}, u32[]{:S(2)}) collective-permute-start(bf16[4,128,128]{2,1,0:T(8,128)(2,1)} %get-tuple-element.55), channel_id=1, source_target_pairs={{0,3},{1,6},{2,5},{3,0},{4,7},{5,2},{6,1},{7,4},{8,11},{9,14},{10,... | collective-permute-start | bytes 393224 | tf_op jit(solution)/shard_map/ppermute | solution.py:508
  15.2 0.0 collective-permute-done.refs_1_
  15.2 2.1 %collective-permute-start.5 = (bf16[4,128,128]{2,1,0:T(8,128)(2,1)S(1)}, bf16[4,128,128]{2,1,0:T(8,128)(2,1)S(1)}, u32[]{:S(2)}, u32[]{:S(2)}) collective-permute-start(bf16[4,128,128]{2,1,0:T(8,128)(2,1)S(1)} %get-tuple-element.56), channel_id=1, source_target_pairs={{0,4},{1,5},{2,6},{3,7},{4,0},{5,1},{6,2},{7,3},{8,12},{9,13},{10,... | collective-permute-start | bytes 393224 | tf_op jit(solution)/shard_map/ppermute | solution.py:508
  17.4 0.2 collective-permute-done.1.refs_2_
  17.6 7.0 %collective-permute-start.6 = (bf16[4,128,128]{2,1,0:T(8,128)(2,1)S(1)}, bf16[4,128,128]{2,1,0:T(8,128)(2,1)S(1)}, u32[]{:S(2)}, u32[]{:S(2)}) collective-permute-start(bf16[4,128,128]{2,1,0:T(8,128)(2,1)S(1)} %get-tuple-element.57), channel_id=1, source_target_pairs={{0,5},{1,4},{2,7},{3,6},{4,1},{5,0},{6,3},{7,2},{8,13},{9,12},{10,... | collective-permute-start | bytes 393224 | tf_op jit(solution)/shard_map/ppermute | solution.py:508
  24.6 0.0 collective-permute-done.2.refs_3_
  24.6 0.0 collective-permute-done.3.refs_4_
  24.6 0.0 collective-permute-done.4.refs_5_
  24.6 4.7 %collective-permute-done.5.refs_6_ = bf16[4,128,128]{2,1,0:T(8,128)(2,1)S(1)} collective-permute-done((bf16[4,128,128]{2,1,0:T(8,128)(2,1)S(1)}, bf16[4,128,128]{2,1,0:T(8,128)(2,1)S(1)}, u32[]{:S(2)}, u32[]{:S(2)}) %collective-permute-start.5) | collective-permute-done | bytes 131104 | tf_op jit(solution)/shard_map/ppermute | solution.py:508
  29.3 3.6 %collective-permute-done.6.refs_7_ = bf16[4,128,128]{2,1,0:T(8,128)(2,1)S(1)} collective-permute-done((bf16[4,128,128]{2,1,0:T(8,128)(2,1)S(1)}, bf16[4,128,128]{2,1,0:T(8,128)(2,1)S(1)}, u32[]{:S(2)}, u32[]{:S(2)}) %collective-permute-start.6) | collective-permute-done | bytes 131104 | tf_op jit(solution)/shard_map/ppermute | solution.py:508
  32.9 0.6 shard_map.103
  33.4 1.3 %collective-permute-start.7 = (bf16[2,128,128]{2,1,0:T(8,128)(2,1)S(1)}, bf16[2,128,128]{2,1,0:T(8,128)(2,1)S(1)}, u32[]{:S(2)}, u32[]{:S(2)}) collective-permute-start(bf16[2,128,128]{2,1,0:T(8,128)(2,1)S(1)} %shard_map.103), channel_id=1, source_target_pairs={{0,8},{1,9},{2,10},{3,11},{4,12},{5,13},{6,14},{7,15},{8,0},{9,1},... | collective-permute-start | bytes 196616 | tf_op jit(solution)/shard_map/ppermute | solution.py:508
  34.7 2.2 %shard_map.102 = (bf16[4,1920,128]{2,1,0:T(8,128)(2,1)S(1)}, f32[1792,256]{1,0:T(8,128)S(1)}, f32[1792,128]{1,0:T(8,128)S(1)}, f32[1792,128]{1,0:T(8,128)S(1)}) custom-call(s32[8]{0:T(128)S(1)} %get-tuple-element.49.info, bf16[4,128,128]{2,1,0:T(8,128)(2,1)S(1)} %get-tuple-element.50.refs_0_, bf16[4,128,128]{2,1,0:T(8,128)(2,1)S(1)} %collective-permute-done.refs_1_, ...), custom_call_target="tpu_custom_call" | custom-call | flops 250000000 | bytes 6000000 | tf_op jit(solution)/shard_map/pallas_call | solution.py:226
  36.9 0.0 collective-permute-done.7.xkv
  36.9 0.0 copy-done
  36.9 2.3 %shard_map.104 = (bf16[8,128,128]{2,1,0:T(8,128)(2,1)S(1)}, bf16[1792,128]{1,0:T(8,128)(2,1)S(1)}, f32[1792,128]{1,0:T(8,128)S(1)}, f32[3,128,128]{2,1,0:T(8,128...) custom-call(s32[8]{0:T(128)S(1)} %get-tuple-element.49.info, f32[4,8]{1,0:T(4,128)S(1)} %copy-done, ...), custom_call_target="tpu_custom_call" | custom-call | flops 50000000 | bytes 6000000 | tf_op jit(solution)/shard_map/pallas_call | solution.py:324
  39.2 1.0 %collective-permute-start.8 = (bf16[272,128]{1,0:T(8,128)(2,1)S(1)}, bf16[272,128]{1,0:T(8,128)(2,1)S(1)}, u32[]{:S(2)}, u32[]{:S(2)}) collective-permute-start(bf16[272,128]{1,0:T(8,128)(2,1)S(1)} %get-tuple-element.72), channel_id=1, source_target_pairs={{0,8},{1,9},{2,10},{3,11},{4,12},{5,13},{6,14},{7,15},{8,0},{9,1},... | collective-permute-start | bytes 208904 | tf_op jit(solution)/shard_map/ppermute | solution.py:508
  40.2 2.4 %shard_map.105 = (bf16[4,128,128]{2,1,0:T(8,128)(2,1)S(1)}, bf16[2,4,128,128]{3,2,1,0:T(8,128)(2,1)S(1)}, bf16[2,4,128,128]{3,2,1,0:T(8,128)(2,1)S(1)}, bf16[2,4...) custom-call(s32[8]{0:T(128)S(1)} %get-tuple-element.49.info, ...), custom_call_target="tpu_custom_call" | custom-call | flops 600000000 | bytes 6000000 | tf_op jit(solution)/shard_map/pallas_call | solution.py:391
  42.7 0.0 collective-permute-done.8.refs_6_
  42.7 0.6 shard_map.106
  43.3 3.9 %collective-permute-start.9 = (bf16[4,4,128,128]{3,2,1,0:T(8,128)(2,1)S(1)}, bf16[4,4,128,128]{3,2,1,0:T(8,128)(2,1)S(1)}, u32[]{:S(2)}, u32[]{:S(2)}) collective-permute-start(bf16[4,4,128,128]{3,2,1,0:T(8,128)(2,1)S(1)} %get-tuple-element.78), channel_id=1, source_target_pairs={{0,1},{1,0},{2,3},{3,2},{4,5},{5,4},{6,7},{7,6},{8,9},{9,8},{10,11... | collective-permute-start | bytes 1572872 | tf_op jit(solution)/shard_map/ppermute | solution.py:508
  47.1 0.1 collective-permute-start.10
  47.3 1.4 %collective-permute-done.10.refs_5_ = f32[1,128]{1,0:T(1,128)S(1)} collective-permute-done((f32[1,128]{1,0:T(1,128)S(1)}, f32[1,128]{1,0:T(1,128)S(1)}, u32[]{:S(2)}, u32[]{:S(2)}) %collective-permute-start.10) | collective-permute-done | bytes 544 | tf_op jit(solution)/shard_map/ppermute | solution.py:508
  48.7 0.0 collective-permute-done.9.refs_3_.refs_4_
  48.7 0.6 shard_map.107
  49.3 0.4 collective-permute-start.11
  49.7 6.9 %collective-permute-start.12 = (bf16[2,4,128,128]{3,2,1,0:T(8,128)(2,1)S(1)}, bf16[2,4,128,128]{3,2,1,0:T(8,128)(2,1)S(1)}, u32[]{:S(2)}, u32[]{:S(2)}) collective-permute-start(bf16[2,4,128,128]{3,2,1,0:T(8,128)(2,1)S(1)} %get-tuple-element.81), channel_id=1, source_target_pairs={{2,0},{7,1},{4,2},{1,3},{6,4},{3,5},{0,6},{5,7},{10,8},{15,9},{12,... | collective-permute-start | bytes 786440 | tf_op jit(solution)/shard_map/ppermute | solution.py:508
  56.6 0.7 collective-permute-start.13
  57.3 0.6 broadcast_in_dim.2
  57.9 11.0 %all-to-all-start = ((f32[64,1,32]{2,1,0:T(1,128)}), f32[64,1,32]{2,1,0:T(1,128)S(1)}, u32[]{:S(2)}, u32[]{:S(2)}) async-start(f32[64,1,32]{2,1,0:T(1,128)} %broadcast_in_dim.2), calls=%async_computation | async-start | bytes 65536 | tf_op jit(solution)/shard_map/all_to_all | solution.py:526
  68.9 0.0 collective-permute-done.11.refs_1_
  68.9 8.2 %collective-permute-done.12.refs_2_ = bf16[2,4,128,128]{3,2,1,0:T(8,128)(2,1)S(1)} collective-permute-done((bf16[2,4,128,128]{3,2,1,0:T(8,128)(2,1)S(1)}, bf16[2,4,128,128]{3,2,1,0:T(8,128)(2,1)S(1)}, u32[]{:S(2)}, u32[]{:S(2)}) %collective-permute-start.12) | collective-permute-done | bytes 262176 | tf_op jit(solution)/shard_map/ppermute | solution.py:508
  77.1 0.0 collective-permute-done.13.refs_3_
  77.1 1.8 %shard_map.108 = (bf16[128,1024]{1,0:T(8,128)(2,1)}, bf16[128,1024]{1,0:T(8,128)(2,1)}, bf16[128,1024]{1,0:T(8,128)(2,1)}, bf16[128,1024]{1,0:T(8,128)(2,1)}) custom-call(s32[8]{0:T(128)S(1)} %get-tuple-element.49.info, bf16[4,128,128]{2,1,0:T(8,128)(2,1)S(1)} %get-tuple-element.74.refs_0_, bf16[2,4,128,128]{3,2,1,0:T(8,128)(2,1)S(1)} %collective-permute-done.11.refs_1_, ...), custom_call_target="tpu_custom_call" | custom-call | bytes 200000000 | tf_op jit(solution)/shard_map/pallas_call | solution.py:497
  78.9 4.9 %all-to-all-done = f32[64,1,32]{2,1,0:T(1,128)S(1)} async-done(((f32[64,1,32]{2,1,0:T(1,128)}), f32[64,1,32]{2,1,0:T(1,128)S(1)}, u32[]{:S(2)}, u32[]{:S(2)}) %all-to-all-start) | async-done | bytes 8224 | tf_op jit(solution)/shard_map/all_to_all | solution.py:526
  83.8 0.7 shard_map.109
  (1 shorter events, 0.0 us)
Async XLA Ops:
  0.6 0.7 copy-start.1
  1.3 35.6 %copy-start = (f32[4,8]{1,0:T(4,128)S(1)}, f32[4,8]{1,0:T(4,128)}, u32[]{:S(2)}) copy-start(f32[4,8]{1,0:T(4,128)} %bias.1) | copy-start | bytes 388
  3.8 11.4 %collective-permute-start = (bf16[4,128,128]{2,1,0:T(8,128)(2,1)S(1)}, bf16[4,128,128]{2,1,0:T(8,128)(2,1)S(1)}, u32[]{:S(2)}, u32[]{:S(2)}) collective-permute-start(bf16[4,128,128]{2,1,0:T(8,128)(2,1)S(1)} %get-tuple-element.51), channel_id=1, source_target_pairs={{0,1},{1,0},{2,3},{3,2},{4,5},{5,4},{6,7},{7,6},{8,9},{9,8},{10,11... | collective-permute-start | bytes 393224 | tf_op jit(solution)/shard_map/ppermute | solution.py:508
  7.1 10.4 %collective-permute-start.1 = (bf16[4,128,128]{2,1,0:T(8,128)(2,1)S(1)}, bf16[4,128,128]{2,1,0:T(8,128)(2,1)S(1)}, u32[]{:S(2)}, u32[]{:S(2)}) collective-permute-start(bf16[4,128,128]{2,1,0:T(8,128)(2,1)S(1)} %get-tuple-element.52), channel_id=1, source_target_pairs={{0,2},{1,7},{2,4},{3,1},{4,6},{5,3},{6,0},{7,5},{8,10},{9,15},{10,... | collective-permute-start | bytes 393224 | tf_op jit(solution)/shard_map/ppermute | solution.py:508
  11.4 13.2 %collective-permute-start.2 = (bf16[4,128,128]{2,1,0:T(8,128)(2,1)S(1)}, bf16[4,128,128]{2,1,0:T(8,128)(2,1)S(1)}, u32[]{:S(2)}, u32[]{:S(2)}) collective-permute-start(bf16[4,128,128]{2,1,0:T(8,128)(2,1)S(1)} %get-tuple-element.53), channel_id=1, source_target_pairs={{0,6},{1,3},{2,0},{3,5},{4,2},{5,7},{6,4},{7,1},{8,14},{9,11},{10,... | collective-permute-start | bytes 393224 | tf_op jit(solution)/shard_map/ppermute | solution.py:508
  11.4 13.2 %collective-permute-start.3 = (bf16[4,128,128]{2,1,0:T(8,128)(2,1)S(1)}, bf16[4,128,128]{2,1,0:T(8,128)(2,1)S(1)}, u32[]{:S(2)}, u32[]{:S(2)}) collective-permute-start(bf16[4,128,128]{2,1,0:T(8,128)(2,1)S(1)} %get-tuple-element.54), channel_id=1, source_target_pairs={{0,7},{1,2},{2,1},{3,4},{4,3},{5,6},{6,5},{7,0},{8,15},{9,10},{10,... | collective-permute-start | bytes 393224 | tf_op jit(solution)/shard_map/ppermute | solution.py:508
  12.9 11.7 %collective-permute-start.4 = (bf16[4,128,128]{2,1,0:T(8,128)(2,1)}, bf16[4,128,128]{2,1,0:T(8,128)(2,1)S(1)}, u32[]{:S(2)}, u32[]{:S(2)}) collective-permute-start(bf16[4,128,128]{2,1,0:T(8,128)(2,1)} %get-tuple-element.55), channel_id=1, source_target_pairs={{0,3},{1,6},{2,5},{3,0},{4,7},{5,2},{6,1},{7,4},{8,11},{9,14},{10,... | collective-permute-start | bytes 393224 | tf_op jit(solution)/shard_map/ppermute | solution.py:508
  15.2 14.1 %collective-permute-start.5 = (bf16[4,128,128]{2,1,0:T(8,128)(2,1)S(1)}, bf16[4,128,128]{2,1,0:T(8,128)(2,1)S(1)}, u32[]{:S(2)}, u32[]{:S(2)}) collective-permute-start(bf16[4,128,128]{2,1,0:T(8,128)(2,1)S(1)} %get-tuple-element.56), channel_id=1, source_target_pairs={{0,4},{1,5},{2,6},{3,7},{4,0},{5,1},{6,2},{7,3},{8,12},{9,13},{10,... | collective-permute-start | bytes 393224 | tf_op jit(solution)/shard_map/ppermute | solution.py:508
  17.6 15.3 %collective-permute-start.6 = (bf16[4,128,128]{2,1,0:T(8,128)(2,1)S(1)}, bf16[4,128,128]{2,1,0:T(8,128)(2,1)S(1)}, u32[]{:S(2)}, u32[]{:S(2)}) collective-permute-start(bf16[4,128,128]{2,1,0:T(8,128)(2,1)S(1)} %get-tuple-element.57), channel_id=1, source_target_pairs={{0,5},{1,4},{2,7},{3,6},{4,1},{5,0},{6,3},{7,2},{8,13},{9,12},{10,... | collective-permute-start | bytes 393224 | tf_op jit(solution)/shard_map/ppermute | solution.py:508
  33.4 3.4 %collective-permute-start.7 = (bf16[2,128,128]{2,1,0:T(8,128)(2,1)S(1)}, bf16[2,128,128]{2,1,0:T(8,128)(2,1)S(1)}, u32[]{:S(2)}, u32[]{:S(2)}) collective-permute-start(bf16[2,128,128]{2,1,0:T(8,128)(2,1)S(1)} %shard_map.103), channel_id=1, source_target_pairs={{0,8},{1,9},{2,10},{3,11},{4,12},{5,13},{6,14},{7,15},{8,0},{9,1},... | collective-permute-start | bytes 196616 | tf_op jit(solution)/shard_map/ppermute | solution.py:508
  39.2 3.5 %collective-permute-start.8 = (bf16[272,128]{1,0:T(8,128)(2,1)S(1)}, bf16[272,128]{1,0:T(8,128)(2,1)S(1)}, u32[]{:S(2)}, u32[]{:S(2)}) collective-permute-start(bf16[272,128]{1,0:T(8,128)(2,1)S(1)} %get-tuple-element.72), channel_id=1, source_target_pairs={{0,8},{1,9},{2,10},{3,11},{4,12},{5,13},{6,14},{7,15},{8,0},{9,1},... | collective-permute-start | bytes 208904 | tf_op jit(solution)/shard_map/ppermute | solution.py:508
  43.3 5.4 %collective-permute-start.9 = (bf16[4,4,128,128]{3,2,1,0:T(8,128)(2,1)S(1)}, bf16[4,4,128,128]{3,2,1,0:T(8,128)(2,1)S(1)}, u32[]{:S(2)}, u32[]{:S(2)}) collective-permute-start(bf16[4,4,128,128]{3,2,1,0:T(8,128)(2,1)S(1)} %get-tuple-element.78), channel_id=1, source_target_pairs={{0,1},{1,0},{2,3},{3,2},{4,5},{5,4},{6,7},{7,6},{8,9},{9,8},{10,11... | collective-permute-start | bytes 1572872 | tf_op jit(solution)/shard_map/ppermute | solution.py:508
  47.1 1.5 %collective-permute-start.10 = (f32[1,128]{1,0:T(1,128)S(1)}, f32[1,128]{1,0:T(1,128)S(1)}, u32[]{:S(2)}, u32[]{:S(2)}) collective-permute-start(f32[1,128]{1,0:T(1,128)S(1)} %get-tuple-element.79.refs_4_), channel_id=1, source_target_pairs={{0,1},{1,0},{2,3},{3,2},{4,5},{5,4},{6,7},{7,6},{8,9},{9,8},{10,11... | collective-permute-start | bytes 1544 | tf_op jit(solution)/shard_map/ppermute | solution.py:508
  49.3 19.7 %collective-permute-start.11 = (bf16[2,4,128,128]{3,2,1,0:T(8,128)(2,1)S(1)}, bf16[2,4,128,128]{3,2,1,0:T(8,128)(2,1)S(1)}, u32[]{:S(2)}, u32[]{:S(2)}) collective-permute-start(bf16[2,4,128,128]{3,2,1,0:T(8,128)(2,1)S(1)} %get-tuple-element.80), channel_id=1, source_target_pairs={{4,0},{5,1},{6,2},{7,3},{0,4},{1,5},{2,6},{3,7},{12,8},{13,9},{14,... | collective-permute-start | bytes 786440 | tf_op jit(solution)/shard_map/ppermute | solution.py:508
  49.7 27.4 %collective-permute-start.12 = (bf16[2,4,128,128]{3,2,1,0:T(8,128)(2,1)S(1)}, bf16[2,4,128,128]{3,2,1,0:T(8,128)(2,1)S(1)}, u32[]{:S(2)}, u32[]{:S(2)}) collective-permute-start(bf16[2,4,128,128]{3,2,1,0:T(8,128)(2,1)S(1)} %get-tuple-element.81), channel_id=1, source_target_pairs={{2,0},{7,1},{4,2},{1,3},{6,4},{3,5},{0,6},{5,7},{10,8},{15,9},{12,... | collective-permute-start | bytes 786440 | tf_op jit(solution)/shard_map/ppermute | solution.py:508
  56.6 20.5 %collective-permute-start.13 = (bf16[2,4,128,128]{3,2,1,0:T(8,128)(2,1)S(1)}, bf16[2,4,128,128]{3,2,1,0:T(8,128)(2,1)S(1)}, u32[]{:S(2)}, u32[]{:S(2)}) collective-permute-start(bf16[2,4,128,128]{3,2,1,0:T(8,128)(2,1)S(1)} %get-tuple-element.82), channel_id=1, source_target_pairs={{6,0},{3,1},{0,2},{5,3},{2,4},{7,5},{4,6},{1,7},{14,8},{11,9},{8,1... | collective-permute-start | bytes 786440 | tf_op jit(solution)/shard_map/ppermute | solution.py:508
  57.9 25.9 %all-to-all-start = ((f32[64,1,32]{2,1,0:T(1,128)}), f32[64,1,32]{2,1,0:T(1,128)S(1)}, u32[]{:S(2)}, u32[]{:S(2)}) async-start(f32[64,1,32]{2,1,0:T(1,128)} %broadcast_in_dim.2), calls=%async_computation | async-start | bytes 65536 | tf_op jit(solution)/shard_map/all_to_all | solution.py:526

commit v6 on v5

--- a/solution.py
+++ b/solution.py
@@ -11,7 +11,7 @@
 ROWS = 128
 TILE = 16
 SHADOW = pl.CostEstimate(flops=0, bytes_accessed=200000000, transcendentals=0)
-BIG = 53 * 1024 * 1024
+BIG = 54144 * 1024
 RES = 8
 SCALE = HD ** (-0.5)
 F32 = jnp.float32

time: 84.6 us -> 83.9 us (level)
    all_to_all x1, waiting for transfers between devices: 4.87 us -> 3.32 us  [local(): lax.all_to_all(spread, ('grp', 'seq'), 0, 0, axis_index_groups=GROUPS, ti...]
    ppermute x14, waiting for transfers between devices: 18.1 us -> 19.6 us  [move(): return lax.ppermute(x, 'seq', pairs)]
where the time goes in v6:
time: 83.9 us; the launch traced here: 83.8 us
  starting transfers between devices  45.8 us (55%)
  waiting for transfers between devices  22.9 us (27%)
  Pallas kernels  12.9 us (15%)
  local copies, waits for them, and re-layouts  1.32 us (2%)
    ppermute x14, starting transfers between devices, move(): return lax.ppermute(x, 'seq', pairs)  34.9 us
    ppermute x14, waiting for transfers between devices, move(): return lax.ppermute(x, 'seq', pairs)  19.6 us
    all_to_all x1, starting transfers between devices, local(): lax.all_to_all(spread, ('grp', 'seq'), 0, 0, axis_index_groups=GROUPS, ti...  11 us
    all_to_all x1, waiting for transfers between devices, local(): lax.all_to_all(spread, ('grp', 'seq'), 0, 0, axis_index_groups=GROUPS, ti...  3.32 us
    pallas_call x1, Pallas kernels, backward(): call(bwd_kernel, MSGS + [CORES, shape(F32, 2, ROWS, HD)], [SM] + [VM] * 6...  2.44 us
    pallas_call x1, Pallas kernels, mixing(): call(mix_kernel, [shape(BF16, 8, ROWS, HD), shape(BF16, BASE[3], HD), sha...  2.31 us
    pallas_call x1, Pallas kernels, forward(): call(fwd_kernel, [shape(BF16, 4, COMPACT, HD), shape(F32, BASE[3], 256),...  2.15 us
    pallas_call x1, Pallas kernels, pack(): pl.pallas_call(pack_kernel, out_shape=[shape(BF16, 4, ROWS, HD)] * 8 + [s...  1.87 us
  transfers between devices with their start and end apart: 15, of which 6 were waited for; matrix products, arithmetic and copies ran while one was open for 1% of the time, Pallas kernels for 8%

profile of v6, /device:TPU:1, one launch (start us, length us, event | category | flops | bytes accessed | tf_op | source)
XLA Modules:
  0.0 83.8 jit_solution(15074370882307997203)
XLA Ops:
  0.6 0.0 copy-start.1
  0.6 0.7 copy-done.1
  1.3 0.0 copy-start
  1.3 1.9 %shard_map.101 = (bf16[4,128,128]{2,1,0:T(8,128)(2,1)S(1)}, bf16[4,128,128]{2,1,0:T(8,128)(2,1)S(1)}, bf16[4,128,128]{2,1,0:T(8,128)(2,1)S(1)}, bf16[4,128,128]{...) custom-call(s32[4,8]{1,0:T(4,128)S(1)} %copy-done.1, ...), custom_call_target="tpu_custom_call" | custom-call | tf_op jit(solution)/shard_map/pallas_call | solution.py:123
  3.2 3.3 %collective-permute-start = (bf16[4,128,128]{2,1,0:T(8,128)(2,1)S(1)}, bf16[4,128,128]{2,1,0:T(8,128)(2,1)S(1)}, u32[]{:S(2)}, u32[]{:S(2)}) collective-permute-start(bf16[4,128,128]{2,1,0:T(8,128)(2,1)S(1)} %get-tuple-element.51), channel_id=1, source_target_pairs={{0,1},{1,0},{2,3},{3,2},{4,5},{5,4},{6,7},{7,6},{8,9},{9,8},{10,11... | collective-permute-start | bytes 393224 | tf_op jit(solution)/shard_map/ppermute | solution.py:508
  6.5 4.3 %collective-permute-start.1 = (bf16[4,128,128]{2,1,0:T(8,128)(2,1)S(1)}, bf16[4,128,128]{2,1,0:T(8,128)(2,1)S(1)}, u32[]{:S(2)}, u32[]{:S(2)}) collective-permute-start(bf16[4,128,128]{2,1,0:T(8,128)(2,1)S(1)} %get-tuple-element.52), channel_id=1, source_target_pairs={{0,2},{1,7},{2,4},{3,1},{4,6},{5,3},{6,0},{7,5},{8,10},{9,15},{10,... | collective-permute-start | bytes 393224 | tf_op jit(solution)/shard_map/ppermute | solution.py:508
  10.8 0.0 collective-permute-start.2
  10.8 1.4 %collective-permute-start.3 = (bf16[4,128,128]{2,1,0:T(8,128)(2,1)S(1)}, bf16[4,128,128]{2,1,0:T(8,128)(2,1)S(1)}, u32[]{:S(2)}, u32[]{:S(2)}) collective-permute-start(bf16[4,128,128]{2,1,0:T(8,128)(2,1)S(1)} %get-tuple-element.54), channel_id=1, source_target_pairs={{0,7},{1,2},{2,1},{3,4},{4,3},{5,6},{6,5},{7,0},{8,15},{9,10},{10,... | collective-permute-start | bytes 393224 | tf_op jit(solution)/shard_map/ppermute | solution.py:508
  12.2 2.4 %collective-permute-start.4 = (bf16[4,128,128]{2,1,0:T(8,128)(2,1)S(1)}, bf16[4,128,128]{2,1,0:T(8,128)(2,1)S(1)}, u32[]{:S(2)}, u32[]{:S(2)}) collective-permute-start(bf16[4,128,128]{2,1,0:T(8,128)(2,1)S(1)} %get-tuple-element.55), channel_id=1, source_target_pairs={{0,3},{1,6},{2,5},{3,0},{4,7},{5,2},{6,1},{7,4},{8,11},{9,14},{10,... | collective-permute-start | bytes 393224 | tf_op jit(solution)/shard_map/ppermute | solution.py:508
  14.6 0.0 collective-permute-done.refs_1_
  14.6 2.1 %collective-permute-start.5 = (bf16[4,128,128]{2,1,0:T(8,128)(2,1)S(1)}, bf16[4,128,128]{2,1,0:T(8,128)(2,1)S(1)}, u32[]{:S(2)}, u32[]{:S(2)}) collective-permute-start(bf16[4,128,128]{2,1,0:T(8,128)(2,1)S(1)} %get-tuple-element.56), channel_id=1, source_target_pairs={{0,4},{1,5},{2,6},{3,7},{4,0},{5,1},{6,2},{7,3},{8,12},{9,13},{10,... | collective-permute-start | bytes 393224 | tf_op jit(solution)/shard_map/ppermute | solution.py:508
  16.8 0.2 collective-permute-done.1.refs_2_
  17.0 6.7 %collective-permute-start.6 = (bf16[4,128,128]{2,1,0:T(8,128)(2,1)S(1)}, bf16[4,128,128]{2,1,0:T(8,128)(2,1)S(1)}, u32[]{:S(2)}, u32[]{:S(2)}) collective-permute-start(bf16[4,128,128]{2,1,0:T(8,128)(2,1)S(1)} %get-tuple-element.57), channel_id=1, source_target_pairs={{0,5},{1,4},{2,7},{3,6},{4,1},{5,0},{6,3},{7,2},{8,13},{9,12},{10,... | collective-permute-start | bytes 393224 | tf_op jit(solution)/shard_map/ppermute | solution.py:508
  23.7 0.0 collective-permute-done.2.refs_3_
  23.7 0.0 collective-permute-done.3.refs_4_
  23.7 0.0 collective-permute-done.4.refs_5_
  23.7 4.9 %collective-permute-done.5.refs_6_ = bf16[4,128,128]{2,1,0:T(8,128)(2,1)S(1)} collective-permute-done((bf16[4,128,128]{2,1,0:T(8,128)(2,1)S(1)}, bf16[4,128,128]{2,1,0:T(8,128)(2,1)S(1)}, u32[]{:S(2)}, u32[]{:S(2)}) %collective-permute-start.5) | collective-permute-done | bytes 131104 | tf_op jit(solution)/shard_map/ppermute | solution.py:508
  28.6 3.4 %collective-permute-done.6.refs_7_ = bf16[4,128,128]{2,1,0:T(8,128)(2,1)S(1)} collective-permute-done((bf16[4,128,128]{2,1,0:T(8,128)(2,1)S(1)}, bf16[4,128,128]{2,1,0:T(8,128)(2,1)S(1)}, u32[]{:S(2)}, u32[]{:S(2)}) %collective-permute-start.6) | collective-permute-done | bytes 131104 | tf_op jit(solution)/shard_map/ppermute | solution.py:508
  32.0 0.6 shard_map.103
  32.5 2.5 %collective-permute-start.7 = (bf16[2,128,128]{2,1,0:T(8,128)(2,1)S(1)}, bf16[2,128,128]{2,1,0:T(8,128)(2,1)S(1)}, u32[]{:S(2)}, u32[]{:S(2)}) collective-permute-start(bf16[2,128,128]{2,1,0:T(8,128)(2,1)S(1)} %shard_map.103), channel_id=1, source_target_pairs={{0,8},{1,9},{2,10},{3,11},{4,12},{5,13},{6,14},{7,15},{8,0},{9,1},... | collective-permute-start | bytes 196616 | tf_op jit(solution)/shard_map/ppermute | solution.py:508
  35.0 2.1 %shard_map.102 = (bf16[4,1920,128]{2,1,0:T(8,128)(2,1)S(1)}, f32[1792,256]{1,0:T(8,128)S(1)}, f32[1792,128]{1,0:T(8,128)S(1)}, f32[1792,128]{1,0:T(8,128)S(1)}) custom-call(s32[8]{0:T(128)S(1)} %get-tuple-element.49.info, bf16[4,128,128]{2,1,0:T(8,128)(2,1)S(1)} %get-tuple-element.50.refs_0_, bf16[4,128,128]{2,1,0:T(8,128)(2,1)S(1)} %collective-permute-done.refs_1_, ...), custom_call_target="tpu_custom_call" | custom-call | flops 250000000 | bytes 6000000 | tf_op jit(solution)/shard_map/pallas_call | solution.py:226
  37.2 0.0 collective-permute-done.7.xkv
  37.2 0.0 copy-done
  37.2 2.3 %shard_map.104 = (bf16[8,128,128]{2,1,0:T(8,128)(2,1)S(1)}, bf16[1792,128]{1,0:T(8,128)(2,1)S(1)}, f32[1792,128]{1,0:T(8,128)S(1)}, f32[3,128,128]{2,1,0:T(8,128...) custom-call(s32[8]{0:T(128)S(1)} %get-tuple-element.49.info, f32[4,8]{1,0:T(4,128)S(1)} %copy-done, ...), custom_call_target="tpu_custom_call" | custom-call | flops 50000000 | bytes 6000000 | tf_op jit(solution)/shard_map/pallas_call | solution.py:324
  39.5 1.0 %collective-permute-start.8 = (bf16[272,128]{1,0:T(8,128)(2,1)S(1)}, bf16[272,128]{1,0:T(8,128)(2,1)S(1)}, u32[]{:S(2)}, u32[]{:S(2)}) collective-permute-start(bf16[272,128]{1,0:T(8,128)(2,1)S(1)} %get-tuple-element.72), channel_id=1, source_target_pairs={{0,8},{1,9},{2,10},{3,11},{4,12},{5,13},{6,14},{7,15},{8,0},{9,1},... | collective-permute-start | bytes 208904 | tf_op jit(solution)/shard_map/ppermute | solution.py:508
  40.5 2.4 %shard_map.105 = (bf16[4,128,128]{2,1,0:T(8,128)(2,1)S(1)}, bf16[2,4,128,128]{3,2,1,0:T(8,128)(2,1)S(1)}, bf16[2,4,128,128]{3,2,1,0:T(8,128)(2,1)S(1)}, bf16[2,4...) custom-call(s32[8]{0:T(128)S(1)} %get-tuple-element.49.info, ...), custom_call_target="tpu_custom_call" | custom-call | flops 600000000 | bytes 6000000 | tf_op jit(solution)/shard_map/pallas_call | solution.py:391
  43.0 0.0 collective-permute-done.8.refs_6_
  43.0 0.6 shard_map.106
  43.6 3.0 %collective-permute-start.9 = (bf16[4,4,128,128]{3,2,1,0:T(8,128)(2,1)S(1)}, bf16[4,4,128,128]{3,2,1,0:T(8,128)(2,1)S(1)}, u32[]{:S(2)}, u32[]{:S(2)}) collective-permute-start(bf16[4,4,128,128]{3,2,1,0:T(8,128)(2,1)S(1)} %get-tuple-element.78), channel_id=1, source_target_pairs={{0,1},{1,0},{2,3},{3,2},{4,5},{5,4},{6,7},{7,6},{8,9},{9,8},{10,11... | collective-permute-start | bytes 1572872 | tf_op jit(solution)/shard_map/ppermute | solution.py:508
  46.5 0.1 collective-permute-start.10
  46.6 1.4 %collective-permute-done.10.refs_5_ = f32[1,128]{1,0:T(1,128)S(1)} collective-permute-done((f32[1,128]{1,0:T(1,128)S(1)}, f32[1,128]{1,0:T(1,128)S(1)}, u32[]{:S(2)}, u32[]{:S(2)}) %collective-permute-start.10) | collective-permute-done | bytes 544 | tf_op jit(solution)/shard_map/ppermute | solution.py:508
  48.1 0.0 collective-permute-done.9.refs_3_.refs_4_
  48.1 0.6 shard_map.107
  48.7 0.3 collective-permute-start.11
  48.9 7.1 %collective-permute-start.12 = (bf16[2,4,128,128]{3,2,1,0:T(8,128)(2,1)S(1)}, bf16[2,4,128,128]{3,2,1,0:T(8,128)(2,1)S(1)}, u32[]{:S(2)}, u32[]{:S(2)}) collective-permute-start(bf16[2,4,128,128]{3,2,1,0:T(8,128)(2,1)S(1)} %get-tuple-element.81), channel_id=1, source_target_pairs={{2,0},{7,1},{4,2},{1,3},{6,4},{3,5},{0,6},{5,7},{10,8},{15,9},{12,... | collective-permute-start | bytes 786440 | tf_op jit(solution)/shard_map/ppermute | solution.py:508
  56.0 0.7 collective-permute-start.13
  56.7 0.6 broadcast_in_dim.2
  57.3 11.0 %all-to-all-start = ((f32[64,1,32]{2,1,0:T(1,128)}), f32[64,1,32]{2,1,0:T(1,128)S(1)}, u32[]{:S(2)}, u32[]{:S(2)}) async-start(f32[64,1,32]{2,1,0:T(1,128)} %broadcast_in_dim.2), calls=%async_computation | async-start | bytes 65536 | tf_op jit(solution)/shard_map/all_to_all | solution.py:526
  68.3 0.0 collective-permute-done.11.refs_1_
  68.3 9.7 %collective-permute-done.12.refs_2_ = bf16[2,4,128,128]{3,2,1,0:T(8,128)(2,1)S(1)} collective-permute-done((bf16[2,4,128,128]{3,2,1,0:T(8,128)(2,1)S(1)}, bf16[2,4,128,128]{3,2,1,0:T(8,128)(2,1)S(1)}, u32[]{:S(2)}, u32[]{:S(2)}) %collective-permute-start.12) | collective-permute-done | bytes 262176 | tf_op jit(solution)/shard_map/ppermute | solution.py:508
  78.0 0.0 collective-permute-done.13.refs_3_
  78.0 1.8 %shard_map.108 = (bf16[128,1024]{1,0:T(8,128)(2,1)}, bf16[128,1024]{1,0:T(8,128)(2,1)}, bf16[128,1024]{1,0:T(8,128)(2,1)}, bf16[128,1024]{1,0:T(8,128)(2,1)}) custom-call(s32[8]{0:T(128)S(1)} %get-tuple-element.49.info, bf16[4,128,128]{2,1,0:T(8,128)(2,1)S(1)} %get-tuple-element.74.refs_0_, bf16[2,4,128,128]{3,2,1,0:T(8,128)(2,1)S(1)} %collective-permute-done.11.refs_1_, ...), custom_call_target="tpu_custom_call" | custom-call | bytes 200000000 | tf_op jit(solution)/shard_map/pallas_call | solution.py:497
  79.8 3.3 %all-to-all-done = f32[64,1,32]{2,1,0:T(1,128)S(1)} async-done(((f32[64,1,32]{2,1,0:T(1,128)}), f32[64,1,32]{2,1,0:T(1,128)S(1)}, u32[]{:S(2)}, u32[]{:S(2)}) %all-to-all-start) | async-done | bytes 8224 | tf_op jit(solution)/shard_map/all_to_all | solution.py:526
  83.1 0.7 shard_map.109
  (1 shorter events, 0.0 us)
Async XLA Ops:
  0.6 0.7 copy-start.1
  1.3 35.9 %copy-start = (f32[4,8]{1,0:T(4,128)S(1)}, f32[4,8]{1,0:T(4,128)}, u32[]{:S(2)}) copy-start(f32[4,8]{1,0:T(4,128)} %bias.1) | copy-start | bytes 388
  3.2 11.4 %collective-permute-start = (bf16[4,128,128]{2,1,0:T(8,128)(2,1)S(1)}, bf16[4,128,128]{2,1,0:T(8,128)(2,1)S(1)}, u32[]{:S(2)}, u32[]{:S(2)}) collective-permute-start(bf16[4,128,128]{2,1,0:T(8,128)(2,1)S(1)} %get-tuple-element.51), channel_id=1, source_target_pairs={{0,1},{1,0},{2,3},{3,2},{4,5},{5,4},{6,7},{7,6},{8,9},{9,8},{10,11... | collective-permute-start | bytes 393224 | tf_op jit(solution)/shard_map/ppermute | solution.py:508
  6.5 10.4 %collective-permute-start.1 = (bf16[4,128,128]{2,1,0:T(8,128)(2,1)S(1)}, bf16[4,128,128]{2,1,0:T(8,128)(2,1)S(1)}, u32[]{:S(2)}, u32[]{:S(2)}) collective-permute-start(bf16[4,128,128]{2,1,0:T(8,128)(2,1)S(1)} %get-tuple-element.52), channel_id=1, source_target_pairs={{0,2},{1,7},{2,4},{3,1},{4,6},{5,3},{6,0},{7,5},{8,10},{9,15},{10,... | collective-permute-start | bytes 393224 | tf_op jit(solution)/shard_map/ppermute | solution.py:508
  10.8 12.9 %collective-permute-start.2 = (bf16[4,128,128]{2,1,0:T(8,128)(2,1)S(1)}, bf16[4,128,128]{2,1,0:T(8,128)(2,1)S(1)}, u32[]{:S(2)}, u32[]{:S(2)}) collective-permute-start(bf16[4,128,128]{2,1,0:T(8,128)(2,1)S(1)} %get-tuple-element.53), channel_id=1, source_target_pairs={{0,6},{1,3},{2,0},{3,5},{4,2},{5,7},{6,4},{7,1},{8,14},{9,11},{10,... | collective-permute-start | bytes 393224 | tf_op jit(solution)/shard_map/ppermute | solution.py:508
  10.8 12.9 %collective-permute-start.3 = (bf16[4,128,128]{2,1,0:T(8,128)(2,1)S(1)}, bf16[4,128,128]{2,1,0:T(8,128)(2,1)S(1)}, u32[]{:S(2)}, u32[]{:S(2)}) collective-permute-start(bf16[4,128,128]{2,1,0:T(8,128)(2,1)S(1)} %get-tuple-element.54), channel_id=1, source_target_pairs={{0,7},{1,2},{2,1},{3,4},{4,3},{5,6},{6,5},{7,0},{8,15},{9,10},{10,... | collective-permute-start | bytes 393224 | tf_op jit(solution)/shard_map/ppermute | solution.py:508
  12.2 11.5 %collective-permute-start.4 = (bf16[4,128,128]{2,1,0:T(8,128)(2,1)S(1)}, bf16[4,128,128]{2,1,0:T(8,128)(2,1)S(1)}, u32[]{:S(2)}, u32[]{:S(2)}) collective-permute-start(bf16[4,128,128]{2,1,0:T(8,128)(2,1)S(1)} %get-tuple-element.55), channel_id=1, source_target_pairs={{0,3},{1,6},{2,5},{3,0},{4,7},{5,2},{6,1},{7,4},{8,11},{9,14},{10,... | collective-permute-start | bytes 393224 | tf_op jit(solution)/shard_map/ppermute | solution.py:508
  14.6 14.0 %collective-permute-start.5 = (bf16[4,128,128]{2,1,0:T(8,128)(2,1)S(1)}, bf16[4,128,128]{2,1,0:T(8,128)(2,1)S(1)}, u32[]{:S(2)}, u32[]{:S(2)}) collective-permute-start(bf16[4,128,128]{2,1,0:T(8,128)(2,1)S(1)} %get-tuple-element.56), channel_id=1, source_target_pairs={{0,4},{1,5},{2,6},{3,7},{4,0},{5,1},{6,2},{7,3},{8,12},{9,13},{10,... | collective-permute-start | bytes 393224 | tf_op jit(solution)/shard_map/ppermute | solution.py:508
  17.0 15.0 %collective-permute-start.6 = (bf16[4,128,128]{2,1,0:T(8,128)(2,1)S(1)}, bf16[4,128,128]{2,1,0:T(8,128)(2,1)S(1)}, u32[]{:S(2)}, u32[]{:S(2)}) collective-permute-start(bf16[4,128,128]{2,1,0:T(8,128)(2,1)S(1)} %get-tuple-element.57), channel_id=1, source_target_pairs={{0,5},{1,4},{2,7},{3,6},{4,1},{5,0},{6,3},{7,2},{8,13},{9,12},{10,... | collective-permute-start | bytes 393224 | tf_op jit(solution)/shard_map/ppermute | solution.py:508
  32.5 4.6 %collective-permute-start.7 = (bf16[2,128,128]{2,1,0:T(8,128)(2,1)S(1)}, bf16[2,128,128]{2,1,0:T(8,128)(2,1)S(1)}, u32[]{:S(2)}, u32[]{:S(2)}) collective-permute-start(bf16[2,128,128]{2,1,0:T(8,128)(2,1)S(1)} %shard_map.103), channel_id=1, source_target_pairs={{0,8},{1,9},{2,10},{3,11},{4,12},{5,13},{6,14},{7,15},{8,0},{9,1},... | collective-permute-start | bytes 196616 | tf_op jit(solution)/shard_map/ppermute | solution.py:508
  39.5 3.5 %collective-permute-start.8 = (bf16[272,128]{1,0:T(8,128)(2,1)S(1)}, bf16[272,128]{1,0:T(8,128)(2,1)S(1)}, u32[]{:S(2)}, u32[]{:S(2)}) collective-permute-start(bf16[272,128]{1,0:T(8,128)(2,1)S(1)} %get-tuple-element.72), channel_id=1, source_target_pairs={{0,8},{1,9},{2,10},{3,11},{4,12},{5,13},{6,14},{7,15},{8,0},{9,1},... | collective-permute-start | bytes 208904 | tf_op jit(solution)/shard_map/ppermute | solution.py:508
  43.6 4.5 %collective-permute-start.9 = (bf16[4,4,128,128]{3,2,1,0:T(8,128)(2,1)S(1)}, bf16[4,4,128,128]{3,2,1,0:T(8,128)(2,1)S(1)}, u32[]{:S(2)}, u32[]{:S(2)}) collective-permute-start(bf16[4,4,128,128]{3,2,1,0:T(8,128)(2,1)S(1)} %get-tuple-element.78), channel_id=1, source_target_pairs={{0,1},{1,0},{2,3},{3,2},{4,5},{5,4},{6,7},{7,6},{8,9},{9,8},{10,11... | collective-permute-start | bytes 1572872 | tf_op jit(solution)/shard_map/ppermute | solution.py:508
  46.5 1.5 %collective-permute-start.10 = (f32[1,128]{1,0:T(1,128)S(1)}, f32[1,128]{1,0:T(1,128)S(1)}, u32[]{:S(2)}, u32[]{:S(2)}) collective-permute-start(f32[1,128]{1,0:T(1,128)S(1)} %get-tuple-element.79.refs_4_), channel_id=1, source_target_pairs={{0,1},{1,0},{2,3},{3,2},{4,5},{5,4},{6,7},{7,6},{8,9},{9,8},{10,11... | collective-permute-start | bytes 1544 | tf_op jit(solution)/shard_map/ppermute | solution.py:508
  48.7 19.6 %collective-permute-start.11 = (bf16[2,4,128,128]{3,2,1,0:T(8,128)(2,1)S(1)}, bf16[2,4,128,128]{3,2,1,0:T(8,128)(2,1)S(1)}, u32[]{:S(2)}, u32[]{:S(2)}) collective-permute-start(bf16[2,4,128,128]{3,2,1,0:T(8,128)(2,1)S(1)} %get-tuple-element.80), channel_id=1, source_target_pairs={{4,0},{5,1},{6,2},{7,3},{0,4},{1,5},{2,6},{3,7},{12,8},{13,9},{14,... | collective-permute-start | bytes 786440 | tf_op jit(solution)/shard_map/ppermute | solution.py:508
  48.9 29.0 %collective-permute-start.12 = (bf16[2,4,128,128]{3,2,1,0:T(8,128)(2,1)S(1)}, bf16[2,4,128,128]{3,2,1,0:T(8,128)(2,1)S(1)}, u32[]{:S(2)}, u32[]{:S(2)}) collective-permute-start(bf16[2,4,128,128]{3,2,1,0:T(8,128)(2,1)S(1)} %get-tuple-element.81), channel_id=1, source_target_pairs={{2,0},{7,1},{4,2},{1,3},{6,4},{3,5},{0,6},{5,7},{10,8},{15,9},{12,... | collective-permute-start | bytes 786440 | tf_op jit(solution)/shard_map/ppermute | solution.py:508
  56.0 22.0 %collective-permute-start.13 = (bf16[2,4,128,128]{3,2,1,0:T(8,128)(2,1)S(1)}, bf16[2,4,128,128]{3,2,1,0:T(8,128)(2,1)S(1)}, u32[]{:S(2)}, u32[]{:S(2)}) collective-permute-start(bf16[2,4,128,128]{3,2,1,0:T(8,128)(2,1)S(1)} %get-tuple-element.82), channel_id=1, source_target_pairs={{6,0},{3,1},{0,2},{5,3},{2,4},{7,5},{4,6},{1,7},{14,8},{11,9},{8,1... | collective-permute-start | bytes 786440 | tf_op jit(solution)/shard_map/ppermute | solution.py:508
  57.3 25.8 %all-to-all-start = ((f32[64,1,32]{2,1,0:T(1,128)}), f32[64,1,32]{2,1,0:T(1,128)S(1)}, u32[]{:S(2)}, u32[]{:S(2)}) async-start(f32[64,1,32]{2,1,0:T(1,128)} %broadcast_in_dim.2), calls=%async_computation | async-start | bytes 65536 | tf_op jit(solution)/shard_map/all_to_all | solution.py:526
